TPU v7x, 32 devices: a whole 2x2x4 slice. The times are simulated.
32 devices in a mesh: ctx: 8 (over z, y), shard: 4 (over x, core).
Axes of the slice: x: 2, y: 2, z: 4, core: 2. Of those that a mesh axis runs over, the one named last changes fastest.
Arguments:
- tokens: bfloat16 [8, 2048, 1536], P('shard', 'ctx'), may hold values from -6 to 6
- segments: int32 [8, 2048], P('shard'), may hold values from 0 to 127, as said below
- assign: int32 [16], replicated, may hold values from 0 to 15, each once
- w_qkv: bfloat16 [1536, 1792], P('shard'), may hold values from -0.15625 to 0.15625
- w_out: bfloat16 [1536, 1536], P('shard'), may hold values from -1.25 to 1.25
- w_gate_up: bfloat16 [1536, 9216], P('shard'), may hold values from -0.15625 to 0.15625
- w_down: bfloat16 [4608, 1536], P('shard'), may hold values from -0.09375 to 0.09375
- gain_attn: bfloat16 [1536], P('shard'), may hold values from 0.099609375 to 1.8984375
- gain_ffn: bfloat16 [1536], P('shard'), may hold values from 0.099609375 to 1.8984375
- cotangent: bfloat16 [8, 2048, 1536], P('shard', 'ctx'), may hold values from -6 to 6
Outputs:
- output: float32 [8, 2048, 1536], P('shard', 'ctx')
- input_grad: float32 [8, 2048, 1536], P('shard', 'ctx')
- grad_qkv: float32 [1536, 1792], P('shard')
- grad_out: float32 [1536, 1536], P('shard')
- grad_gate_up: float32 [1536, 9216], P('shard')
- grad_down: float32 [4608, 1536], P('shard')
- grad_gain_attn: float32 [1536], P('shard')
- grad_gain_ffn: float32 [1536], P('shard')
Inputs may be any that keep to these rules, and one draw needn't show every extreme that they name: `segments`: within each sequence the numbers start at 0 and never fall; of the 2 sequences at one index of shard, at least one is a single document; some sequence reaches the largest number.
All inputs are finite; a program needn't handle non-finite values.
Results may differ from a plain program's by a relative error of at most 0.018.
Values may be sent and summed in bfloat16 or wider, within the bound.
No kernel may reach another device: no remote copies, remote signals or barrier semaphores. Data moves between devices by JAX's collectives and lax.ppermute only.
A program may use at most 256 MiB of HBM per device.

v0:
```python
import jax
import jax.numpy as jnp
from jax import lax
from jax.sharding import PartitionSpec as P

H = 12
HD = 128
FF = 4608
W = 1024
BLK = 128


epsilon = 1e-06
masked_score = -1e30


def norm_hat(tok_rows):
    return tok_rows * lax.rsqrt(jnp.mean(tok_rows * tok_rows, axis=-1, keepdims=True) + epsilon)


def norm_back(grad_hat, row_hat, tok_rows):
    scale_inv = lax.rsqrt(jnp.mean(tok_rows * tok_rows, axis=-1, keepdims=True) + epsilon)
    return scale_inv * (grad_hat - row_hat * jnp.mean(grad_hat * row_hat, axis=-1, keepdims=True))


def transpose_dot(left_rows, right_rows):
    return lax.dot_general(
        left_rows, right_rows, (((1,), (1,)), ((), ())), preferred_element_type=jnp.float32
    )


def normed_project(row_hat, weight, gain):
    gain_piece = lax.all_gather(gain, "shard", axis=0, tiled=True).astype(jnp.float32)
    columns = (row_hat * gain_piece).astype(jnp.bfloat16)
    running = jnp.dot(
        columns,
        lax.all_gather(weight, "shard", axis=0, tiled=True),
        preferred_element_type=jnp.float32,
    )
    return (running, gain_piece, None)


def plain_project(low_rows, weight):
    return (
        jnp.dot(
            low_rows,
            lax.all_gather(weight, "shard", axis=0, tiled=True),
            preferred_element_type=jnp.float32,
        ),
        None,
    )


def back_project(grad_low, weight):
    return transpose_dot(grad_low, lax.all_gather(weight, "shard", axis=0, tiled=True))


def weight_grad(left_low, right_low):
    return lax.psum_scatter(
        lax.dot_general(
            left_low, right_low, (((0,), (0,)), ((), ())), preferred_element_type=jnp.float32
        ).astype(jnp.bfloat16),
        "shard",
        scatter_dimension=0,
        tiled=True,
    ).astype(jnp.float32)


def block_mask(segments, seg_pad, first_pos):
    query_pos = first_pos + jnp.arange(BLK, dtype=jnp.int32)
    key_pos = first_pos - W + jnp.arange(W + BLK, dtype=jnp.int32)
    query_seg = lax.dynamic_slice_in_dim(segments, first_pos, BLK, 1)
    key_seg = lax.dynamic_slice_in_dim(seg_pad, first_pos, W + BLK, 1)
    causal = (key_pos[None, :] <= query_pos[:, None]) & (query_pos[:, None] - key_pos[None, :] < W)
    return (query_seg[:, :, None] == key_seg[:, None, :]) & causal[None]


def block_scores(queries, key_block, allowed):
    scores = jnp.einsum(
        "sqhd,skd->shqk", queries, key_block, preferred_element_type=jnp.float32
    ) * HD ** (-0.5)
    return jnp.where(allowed[:, None], scores, masked_score)


def body(tokens, segments, assign, w_qkv, w_out, w_gate_up, w_down, gain_attn, gain_ffn, cotangent):
    seq_count = tokens.shape[0]
    rows_dev = tokens.shape[1]
    model_width = tokens.shape[2]
    row_count = seq_count * rows_dev
    block_count = assign.shape[0]
    length = block_count * BLK
    my_blocks = lax.dynamic_slice_in_dim(assign, 2 * lax.axis_index("ctx"), 2, 0)
    slot_ids = jnp.arange(block_count, dtype=jnp.int32)
    inverse = jnp.sum(jnp.where(assign[None, :] == slot_ids[:, None], slot_ids[None, :], 0), axis=1)
    seg_pad = jnp.concatenate([jnp.full((seq_count, W), -1, jnp.int32), segments], axis=1)
    tok_rows = tokens.reshape(row_count, model_width).astype(jnp.float32)
    hat_one = norm_hat(tok_rows)
    qkv_rows, gain_one, full_qkv = normed_project(hat_one, w_qkv, gain_attn)
    qkv_low = qkv_rows.astype(jnp.bfloat16)
    query_all = qkv_low[:, : H * HD].reshape(seq_count, rows_dev, H, HD)
    key_value = qkv_low[:, H * HD :].reshape(seq_count, rows_dev, 2 * HD)
    gathered = lax.all_gather(key_value, "ctx", axis=1, tiled=True)
    natural = gathered.reshape(seq_count, block_count, BLK, 2 * HD)[:, inverse].reshape(
        seq_count, length, 2 * HD
    )
    padded = jnp.concatenate([jnp.zeros((seq_count, W, 2 * HD), jnp.bfloat16), natural], axis=1)
    outputs = []
    log_totals = []
    for block_slot in range(2):
        first_pos = my_blocks[block_slot] * BLK
        allowed = block_mask(segments, seg_pad, first_pos)
        key_vals = lax.dynamic_slice_in_dim(padded, first_pos, W + BLK, 1)
        queries = query_all[:, block_slot * BLK : (block_slot + 1) * BLK]
        scores = block_scores(queries, key_vals[..., :HD], allowed)
        row_max = jnp.max(scores, axis=-1, keepdims=True)
        expo_vals = jnp.exp(scores - row_max)
        row_total = jnp.sum(expo_vals, axis=-1, keepdims=True)
        attn_probs = (expo_vals / row_total).astype(jnp.bfloat16)
        outputs.append(
            jnp.einsum(
                "shqk,skd->sqhd", attn_probs, key_vals[..., HD:], preferred_element_type=jnp.float32
            )
        )
        log_totals.append(row_max + jnp.log(row_total))
    mixed_low = jnp.concatenate(outputs, axis=1).reshape(row_count, H * HD).astype(jnp.bfloat16)
    branch, full_out = plain_project(mixed_low, w_out)
    hidden = tok_rows + branch
    hat_two = norm_hat(hidden)
    gate_up, gain_two, full_gate_up = normed_project(hat_two, w_gate_up, gain_ffn)
    gate_part = gate_up[:, :FF]
    up_part = gate_up[:, FF:]

    def gelu_product(gate_in, up_in):
        return jax.nn.gelu(gate_in, approximate=True) * up_in

    active, gelu_pull = jax.vjp(gelu_product, gate_part, up_part)
    active_low = active.astype(jnp.bfloat16)
    final_branch, full_down = plain_project(active_low, w_down)
    output = (hidden + final_branch).reshape(seq_count, rows_dev, model_width)
    grad_low = cotangent.reshape(row_count, model_width)
    grad_rows = grad_low.astype(jnp.float32)
    grad_down_part = weight_grad(active_low, grad_low)
    d_active = back_project(grad_low, w_down)
    d_gate, d_up = gelu_pull(d_active)
    d_gu_low = jnp.concatenate([d_gate, d_up], axis=1).astype(jnp.bfloat16)
    normed_two = (hat_two * gain_two).astype(jnp.bfloat16)
    grad_gate_up_part = weight_grad(normed_two, d_gu_low)
    d_normed_two = back_project(d_gu_low, w_gate_up)
    gain_two_local = jnp.sum(d_normed_two * hat_two, axis=0)
    d_hidden = grad_rows + norm_back(d_normed_two * gain_two, hat_two, hidden)
    d_branch_low = d_hidden.astype(jnp.bfloat16)
    grad_out_part = weight_grad(mixed_low, d_branch_low)
    d_mixed_low = back_project(d_branch_low, w_out).astype(jnp.bfloat16)
    d_mixed_all = d_mixed_low.reshape(seq_count, rows_dev, H, HD)
    key_buffer = jnp.zeros((seq_count, W + length, 2 * HD), jnp.float32)
    query_grads = []
    for block_slot in range(2):
        first_pos = my_blocks[block_slot] * BLK
        allowed = block_mask(segments, seg_pad, first_pos)
        key_vals = lax.dynamic_slice_in_dim(padded, first_pos, W + BLK, 1)
        queries = query_all[:, block_slot * BLK : (block_slot + 1) * BLK]
        d_out_block = d_mixed_all[:, block_slot * BLK : (block_slot + 1) * BLK]
        scores = block_scores(queries, key_vals[..., :HD], allowed)
        attn_probs = jnp.exp(scores - log_totals[block_slot])
        d_probs = jnp.einsum(
            "sqhd,skd->shqk", d_out_block, key_vals[..., HD:], preferred_element_type=jnp.float32
        )
        row_delta = jnp.sum(attn_probs * d_probs, axis=-1, keepdims=True)
        d_raw = (attn_probs * (d_probs - row_delta) * HD ** (-0.5)).astype(jnp.bfloat16)
        query_grads.append(
            jnp.einsum(
                "shqk,skd->sqhd", d_raw, key_vals[..., :HD], preferred_element_type=jnp.float32
            )
        )
        d_keys = jnp.einsum("shqk,sqhd->skd", d_raw, queries, preferred_element_type=jnp.float32)
        d_values = jnp.einsum(
            "shqk,sqhd->skd",
            attn_probs.astype(jnp.bfloat16),
            d_out_block,
            preferred_element_type=jnp.float32,
        )
        current = lax.dynamic_slice_in_dim(key_buffer, first_pos, W + BLK, 1)
        key_buffer = lax.dynamic_update_slice_in_dim(
            key_buffer, current + jnp.concatenate([d_keys, d_values], axis=-1), first_pos, 1
        )
    natural_grad = key_buffer[:, W:]
    stored_grad = natural_grad.reshape(seq_count, block_count, BLK, 2 * HD)[:, assign].reshape(
        seq_count, length, 2 * HD
    )
    key_value_grad = lax.psum_scatter(
        stored_grad.astype(jnp.bfloat16), "ctx", scatter_dimension=1, tiled=True
    ).astype(jnp.float32)
    d_qkv_low = jnp.concatenate(
        [
            jnp.concatenate(query_grads, axis=1).reshape(row_count, H * HD),
            key_value_grad.reshape(row_count, 2 * HD),
        ],
        axis=1,
    ).astype(jnp.bfloat16)
    normed_one = (hat_one * gain_one).astype(jnp.bfloat16)
    grad_qkv_part = weight_grad(normed_one, d_qkv_low)
    d_normed_one = back_project(d_qkv_low, w_qkv)
    gain_one_local = jnp.sum(d_normed_one * hat_one, axis=0)
    input_grad = (d_hidden + norm_back(d_normed_one * gain_one, hat_one, tok_rows)).reshape(
        seq_count, rows_dev, model_width
    )
    grad_qkv, grad_out, grad_gate_up, grad_down = (
        lax.psum(grad_qkv_part.astype(jnp.bfloat16), "ctx").astype(jnp.float32),
        lax.psum(grad_out_part.astype(jnp.bfloat16), "ctx").astype(jnp.float32),
        lax.psum(grad_gate_up_part.astype(jnp.bfloat16), "ctx").astype(jnp.float32),
        lax.psum(grad_down_part.astype(jnp.bfloat16), "ctx").astype(jnp.float32),
    )
    gain_one_sum, gain_two_sum = lax.psum((gain_one_local, gain_two_local), ("ctx", "shard"))
    gain_rows = gain_attn.shape[0]
    gain_offset = lax.axis_index("shard") * gain_rows
    grad_gain_attn = lax.dynamic_slice_in_dim(gain_one_sum, gain_offset, gain_rows, 0)
    grad_gain_ffn = lax.dynamic_slice_in_dim(gain_two_sum, gain_offset, gain_rows, 0)
    return (
        output,
        input_grad,
        grad_qkv,
        grad_out,
        grad_gate_up,
        grad_down,
        grad_gain_attn,
        grad_gain_ffn,
    )


def solution(mesh):
    return jax.shard_map(
        body,
        mesh=mesh,
        in_specs=(
            P("shard", "ctx", None),
            P("shard", None),
            P(),
            P("shard", None),
            P("shard", None),
            P("shard", None),
            P("shard", None),
            P("shard"),
            P("shard"),
            P("shard", "ctx", None),
        ),
        out_specs=(
            P("shard", "ctx", None),
            P("shard", "ctx", None),
            P("shard", None),
            P("shard", None),
            P("shard", None),
            P("shard", None),
            P("shard"),
            P("shard"),
        ),
        check_vma=False,
    )
```

profile of v0, /device:TPU:0, one launch (start us, length us, event | category | flops | bytes accessed | tf_op | source)
XLA Modules:
  0.0 1505.2 jit_solution(14265442829174924277)
XLA Ops:
  18.4 35.8 %all-gather.8.cloned.1.call-done = bf16[1536,1792]{1,0:T(8,128)(2,1)} async-done(((bf16[384,1792]{1,0:T(8,128)(2,1)}), bf16[1536,1792]{1,0:T(8,128)(2,1)}) %all-gather.8.cloned.1.call-update) | async-done | bytes 5505040 | tf_op jit(solution)/shard_map/all_gather | solution.py:37
  79.4 30.8 %all-gather.10.cloned.1.call-done = bf16[2,2048,256]{2,1,0:T(8,128)(2,1)} async-done(((bf16[2,256,256]{2,1,0:T(8,128)(2,1)}), bf16[2,2048,256]{2,1,0:T(8,128)(2,1)}) %all-gather.10.cloned.1.call-update) | async-done | bytes 2097168 | tf_op jit(solution)/shard_map/all_gather | solution.py:102
  139.7 8.5 fusion.50
  153.0 8.3 multiply_reduce_fusion.4
  161.9 159.5 %all-gather.14.cloned.1.call-done = bf16[1536,9216]{1,0:T(8,128)(2,1)} async-done(((bf16[384,9216]{1,0:T(8,128)(2,1)}), bf16[1536,9216]{1,0:T(8,128)(2,1)}) %all-gather.14.cloned.1.call-update) | async-done | bytes 28311568 | tf_op jit(solution)/shard_map/all_gather | solution.py:37
  321.4 26.7 %fusion.107 = f32[512,9216]{1,0:T(8,128)} fusion(bf16[1536,9216]{1,0:T(8,128)(2,1)} %all-gather.14.cloned.1.call-done, f32[512,1536]{1,0:T(8,128)} %get-tuple-element.36, f32[1536]{0:T(1024)S(1)} %reshape.303, f32[512]{0:T(512)S(1)} %add_rsqrt_fusion), kind=kOutput, calls=%fused_computation.168 | convolution fusion | flops 14497873920 | bytes 50339840 | tf_op jit(solution)/shard_map/dot_general | solution.py:35
  348.1 65.8 %all-gather.16.cloned.1.call-done = bf16[4608,1536]{1,0:T(8,128)(2,1)} async-done(((bf16[1152,1536]{1,0:T(8,128)(2,1)}), bf16[4608,1536]{1,0:T(8,128)(2,1)}) %all-gather.16.cloned.1.call-update) | async-done | bytes 14155792 | tf_op jit(solution)/shard_map/all_gather | solution.py:47
  413.9 23.8 %fusion.18 = (bf16[512,4608]{1,0:T(8,128)(2,1)}, bf16[512,4608]{1,0:T(8,128)(2,1)}, bf16[512,4608]{1,0:T(8,128)(2,1)}) fusion(f32[512,9216]{1,0:T(8,128)} %fusion.107, bf16[512,1536]{1,0:T(8,128)(2,1)} %bitcast.197, bf16[4608,1536]{1,0:T(8,128)(2,1)} %all-gather.16.cloned.1.call-done), kind=kOutput, calls=%fused_computation.36 | convolution fusion | flops 7309099008 | bytes 48758784 | tf_op jit(solution)/shard_map/dot_general | solution.py:27
  437.6 22.9 %multiply_reduce_fusion = (f32[1536]{0:T(1024)}, f32[512]{0:T(512)S(1)}, f32[512,1536]{1,0:T(8,128)}) fusion(f32[512,1536]{1,0:T(8,128)S(1)} %copy-done.12, f32[512]{0:T(512)S(1)} %add_rsqrt_fusion, f32[1536]{0:T(1024)S(1)} %reshape.303, bf16[1536,9216]{1,0:T(8,128)(2,1)} %all-gather.14.cloned.1.call-done, bf16[512,4608]{1,0:T(8,128)(2,1)} %get-tuple-element.19, ...), kind=kOutput, calls=%fused_computation.63 | convolution fusion | flops 14519105536 | bytes 44056576 | tf_op jit(solution)/shard_map/dot_general | solution.py:27
  500.7 23.1 %fusion.34 = f32[2,1152,128]{1,2,0:T(8,128)} fusion(f32[2,1152,128,12]{2,1,3,0:T(8,128)} %fusion.61, f32[2,12,128,1152]{2,3,1,0:T(8,128)} %get-tuple-element.32, f32[2,12,128]{2,1,0:T(8,128)S(1)} %log_add_fusion, bf16[2,128,12,128]{3,2,1,0:T(8,128)(2,1)} %get-tuple-element.24), kind=kOutput, calls=%fused_computation.75 | convolution fusion | flops 930746496 | bytes 30289920 | tf_op jit(solution)/shard_map/shqk,sqhd->skd/dot_general | solution.py:175
  523.8 8.2 fusion.36
  532.0 22.6 %fusion.35 = f32[2,1152,128]{1,2,0:T(8,128)S(1)} fusion(f32[2,1152,128,12]{2,1,3,0:T(8,128)} %fusion.64, f32[2,12,128,1152]{2,3,1,0:T(8,128)} %copy-done, f32[2,12,128]{2,1,0:T(8,128)S(1)} %copy-done.24, bf16[2,128,12,128]{3,2,1,0:T(8,128)(2,1)} %get-tuple-element.23), kind=kOutput, calls=%fused_computation.76 | convolution fusion | flops 930746496 | bytes 30289920 | tf_op jit(solution)/shard_map/shqk,sqhd->skd/dot_general | solution.py:175
  576.8 20.5 %fusion.47 = bf16[2,128,12,128]{3,1,2,0:T(8,128)(2,1)S(1)} fusion(f32[2,1152,128,12]{2,1,3,0:T(8,128)} %fusion.64, f32[2,12,128,1152]{2,3,1,0:T(8,128)} %copy-done, f32[2,12,128]{2,1,0:T(8,128)S(1)} %copy-done.24, s32[]{:T(128)S(6)} %select_n.59, bf16[2,2048,256]{2,1,0:T(8,128)(2,1)S(1)} %bitcast.182), kind=kOutput, calls=%fused_computation.90 | convolution fusion | flops 931139712 | bytes 59539460 | tf_op jit(solution)/shard_map/shqk,skd->sqhd/dot_general | solution.py:171
  597.4 21.1 %fusion.48 = bf16[2,128,12,128]{3,1,2,0:T(8,128)(2,1)} fusion(f32[2,1152,128,12]{2,1,3,0:T(8,128)} %fusion.61, f32[2,12,128,1152]{2,3,1,0:T(8,128)} %get-tuple-element.32, f32[2,12,128]{2,1,0:T(8,128)S(1)} %log_add_fusion, s32[]{:T(128)S(6)} %select_n.62, bf16[2,2048,256]{2,1,0:T(8,128)(2,1)S(1)} %bitcast.183), kind=kOutput, calls=%fused_computation.91 | convolution fusion | flops 931139712 | bytes 59539460 | tf_op jit(solution)/shard_map/shqk,skd->sqhd/dot_general | solution.py:171
  621.4 16.0 %reduce-scatter.6.cloned.1.call-done = bf16[2,256,256]{2,1,0:T(8,128)(2,1)} async-done(((bf16[2,2048,256]{2,1,0:T(8,128)(2,1)}), bf16[2,256,256]{2,1,0:T(8,128)(2,1)}) %reduce-scatter.6.cloned.1.call-update) | async-done | bytes 262160 | tf_op jit(solution)/shard_map/reduce_scatter | solution.py:190
  647.2 13.2 convolution_convert_fusion.1
  662.3 23.4 %convolution_convert_fusion = bf16[1536,9216]{1,0:T(8,128)(2,1)} fusion(bf16[512,4608]{1,0:T(8,128)(2,1)} %get-tuple-element.19, bf16[512,4608]{1,0:T(8,128)(2,1)} %get-tuple-element.18, f32[512,1536]{1,0:T(8,128)S(1)} %copy-done.13, f32[1536]{0:T(1024)S(1)} %reshape.303, f32[512]{0:T(512)S(1)} %add_rsqrt_fusion), kind=kOutput, calls=%fused_computation.4 | convolution fusion | flops 14530904064 | bytes 40902656 | tf_op jit(solution)/shard_map/dot_general | solution.py:60
  686.9 56.4 %reduce-scatter.8.cloned.1.call-done = bf16[384,1792]{1,0:T(8,128)(2,1)} async-done(((bf16[1536,1792]{1,0:T(8,128)(2,1)}), bf16[384,1792]{1,0:T(8,128)(2,1)}) %reduce-scatter.8.cloned.1.call-update) | async-done | bytes 1376272 | tf_op jit(solution)/shard_map/reduce_scatter | solution.py:59
  743.3 112.7 %reduce-scatter.14.cloned.1.call-done = bf16[1152,1536]{1,0:T(8,128)(2,1)} async-done(((bf16[4608,1536]{1,0:T(8,128)(2,1)}), bf16[1152,1536]{1,0:T(8,128)(2,1)}) %reduce-scatter.14.cloned.1.call-update) | async-done | bytes 3538960 | tf_op jit(solution)/shard_map/reduce_scatter | solution.py:59
  856.0 203.5 %reduce-scatter.12.cloned.1.call-done = bf16[384,9216]{1,0:T(8,128)(2,1)} async-done(((bf16[1536,9216]{1,0:T(8,128)(2,1)}), bf16[384,9216]{1,0:T(8,128)(2,1)}) %reduce-scatter.12.cloned.1.call-update) | async-done | bytes 7077904 | tf_op jit(solution)/shard_map/reduce_scatter | solution.py:59
  1059.6 13.8 convolution_add_fusion
  1081.3 43.8 %all-reduce.2 = (f32[1536]{0:T(1024)S(1)}, f32[1536]{0:T(1024)S(1)}) all-reduce(f32[1536]{0:T(1024)S(1)} %get-tuple-element.10, f32[1536]{0:T(1024)S(1)} %copy-done.28), channel_id=1, replica_groups=mesh['ctx'=8,'shard'=4] {'ctx','shard'}, use_global_device_ids=true, to_apply=%region_21.22 | all-reduce | flops 3072 | bytes 24576 | tf_op jit(solution)/shard_map/psum | solution.py:213
  1131.7 348.9 %all-reduce.6.cloned.1.call-done = (bf16[384,1792]{1,0:T(8,128)(2,1)}, bf16[384,1536]{1,0:T(8,128)(2,1)}, bf16[384,9216]{1,0:T(8,128)(2,1)}, bf16[1152,1536]{1,0:T(8,128)(2,1)}) async-done(((bf16[384,1792]{1,0:T(8,128)(2,1)}, bf16[384,1536]{1,0:T(8,128)(2,1)}, bf16[384,9216]{1,0:T(8,128)(2,1)}, bf16[1152,1536]{1,0:T(8,128)(2,1)}), (bf16[384,1792]{1,0:T(8,128)(2,1)}, bf16[384,1536]{1,0:T(8,128)(2,1)}, ...) | async-done | bytes 13172752 | tf_op jit(solution)/shard_map/psum | solution.py:208
  1480.6 10.2 convert_element_type.127
  (161 shorter events, 169.4 us)
Async XLA Ops:
  7.2 47.0 %all-gather.8.cloned.1.call-start = ((), (), s32[]{:S(2)}) async-start(), calls=%async_computation.5 | async-start | bytes 6881280 | tf_op jit(solution)/shard_map/all_gather | solution.py:37
  7.9 102.3 %all-gather.10.cloned.1.call-start = ((), (), s32[]{:S(2)}) async-start(), calls=%async_computation.6 | async-start | bytes 2359296 | tf_op jit(solution)/shard_map/all_gather | solution.py:102
  18.4 41.3 %copy-start.17 = (bf16[512,1536]{1,0:T(8,128)(2,1)}, bf16[512,1536]{1,0:T(8,128)(2,1)S(1)}, u32[]{:S(2)}) copy-start(bf16[512,1536]{1,0:T(8,128)(2,1)S(1)} %multiply_convert_fusion.3) | copy-start | bytes 4718596
  60.5 92.5 %all-gather.12.cloned.1.call-start = ((), (), s32[]{:S(2)}) async-start(), calls=%async_computation.7 | async-start | bytes 5898240 | tf_op jit(solution)/shard_map/all_gather | solution.py:47
  61.3 8.5 copy-start.25
  61.3 260.1 %all-gather.14.cloned.1.call-start = ((), (), s32[]{:S(2)}) async-start(), calls=%async_computation.8 | async-start | bytes 35389440 | tf_op jit(solution)/shard_map/all_gather | solution.py:37
  61.9 352.0 %all-gather.16.cloned.1.call-start = ((), (), s32[]{:S(2)}) async-start(), calls=%async_computation.9 | async-start | bytes 17694720 | tf_op jit(solution)/shard_map/all_gather | solution.py:47
  62.5 575.0 %reduce-scatter.6.cloned.1.call-start = ((), (), s32[]{:S(2)}) async-start(), calls=%async_computation.10 | async-start | bytes 2359296 | tf_op jit(solution)/shard_map/reduce_scatter | solution.py:190
  117.4 17.1 %copy-start = (f32[2,12,128,1152]{2,3,1,0:T(8,128)}, f32[2,12,128,1152]{2,3,1,0:T(8,128)S(1)}, u32[]{:S(2)}) copy-start(f32[2,12,128,1152]{2,3,1,0:T(8,128)S(1)} %get-tuple-element.34) | copy-start | bytes 42467332
  153.0 8.3 copy-start.16
  413.9 23.8 %copy-start.12 = (f32[512,1536]{1,0:T(8,128)S(1)}, f32[512,1536]{1,0:T(8,128)}, u32[]{:S(2)}) copy-start(f32[512,1536]{1,0:T(8,128)} %get-tuple-element.36) | copy-start | bytes 9437188
  500.7 23.1 %copy-start.24 = (f32[2,12,128]{2,1,0:T(8,128)S(1)}, f32[2,12,128]{2,1,0:T(8,128)}, u32[]{:S(2)}) copy-start(f32[2,12,128]{2,1,0:T(8,128)} %log_add_fusion.1) | copy-start | bytes 36868
  569.6 117.3 %reduce-scatter.10.cloned.1.call-start = ((), (), s32[]{:S(2)}) async-start(), calls=%async_computation.12 | async-start | bytes 5898240 | tf_op jit(solution)/shard_map/reduce_scatter | solution.py:59
  576.8 166.5 %reduce-scatter.8.cloned.1.call-start = ((), (), s32[]{:S(2)}) async-start(), calls=%async_computation.11 | async-start | bytes 6881280 | tf_op jit(solution)/shard_map/reduce_scatter | solution.py:59
  621.4 24.2 %copy-start.14 = (bf16[192,8,2,256]{3,1,2,0:T(8,128)(2,1)}, bf16[192,8,2,256]{3,1,2,0:T(8,128)(2,1)S(1)}, u32[]{:S(2)}) copy-start(bf16[192,8,2,256]{3,1,2,0:T(8,128)(2,1)S(1)} %copy.160) | copy-start | bytes 4718596
  645.7 210.3 %reduce-scatter.14.cloned.1.call-start = ((), (), s32[]{:S(2)}) async-start(), calls=%async_computation.14 | async-start | bytes 17694720 | tf_op jit(solution)/shard_map/reduce_scatter | solution.py:59
  660.4 399.1 %reduce-scatter.12.cloned.1.call-start = ((), (), s32[]{:S(2)}) async-start(), calls=%async_computation.13 | async-start | bytes 35389440 | tf_op jit(solution)/shard_map/reduce_scatter | solution.py:59
  685.7 794.9 %all-reduce.6.cloned.1.call-start = ((), (), s32[]{:S(2)}) async-start(), calls=%async_computation.15 | async-start | bytes 26345472 | tf_op jit(solution)/shard_map/psum | solution.py:208
  1059.5 13.8 copy-start.5
  1059.5 13.8 copy-start.15
  1059.5 13.8 copy-start.23
  1059.5 13.8 copy-start.27
  1073.3 7.9 copy-start.28
  1480.6 10.2 copy-start.11
  (18 other events, 51.7 us)
Sparse Core Ops, SparseCore 0:
  9.6 44.6 all-gather.7
  60.7 49.4 all-gather.9
  111.7 35.9 all-gather.11
  149.1 172.2 all-gather.13
  322.8 91.0 all-gather.15
  569.7 67.7 reduce-scatter.5
  640.0 46.8 reduce-scatter.9
  690.1 53.1 reduce-scatter.7
  746.5 109.4 reduce-scatter.13
  858.4 201.0 reduce-scatter.11
  1065.1 415.4 all-reduce.5
where the time goes:
time: 1510 us
  waiting for transfers between devices  1030 us (68%)
  matrix products  308 us (20%)
  blocking collectives  55 us (4%)
  other arithmetic  46.2 us (3%)
  local copies, waits for them, and re-layouts  45.7 us (3%)
  between operations  16.3 us (1%)
    reduce_scatter x4, waiting for transfers between devices, weight_grad(): lax.psum_scatter(lax.dot_general(left_low, right_low, (((0,), (0,)), ((),...  374 us
    psum x1, waiting for transfers between devices, body(): lax.psum(grad_qkv_part.astype(jnp.bfloat16), 'ctx').astype(jnp.float32)  349 us
    all_gather x2, waiting for transfers between devices, normed_project(): lax.all_gather(weight, 'shard', axis=0, tiled=True)  195 us
    all_gather x2, waiting for transfers between devices, plain_project(): lax.all_gather(weight, 'shard', axis=0, tiled=True)  65.8 us
    dot_general x4, matrix products, transpose_dot(): lax.dot_general(left_rows, right_rows, (((1,), (1,)), ((), ())), preferre...  60.6 us
    dot_general x4, matrix products, weight_grad(): lax.dot_general(left_low, right_low, (((0,), (0,)), ((), ())), preferred_...  50.8 us
    dot_general x2, matrix products, body(): jnp.einsum('shqk,sqhd->skd', d_raw, queries, preferred_element_type=jnp.f...  45.8 us
    psum x1, blocking collectives, body(): lax.psum((gain_one_local, gain_two_local), ('ctx', 'shard'))  43.8 us
  transfers between devices with their start and end apart: 11, of which 10 were waited for; matrix products, arithmetic and copies ran while one was open for 14% of the time, Pallas kernels for 0%

commit v1 on v0

v1 whole, which is shorter than its diff:
```python
import functools

import jax
import jax.numpy as jnp
from jax import lax
from jax.experimental import pallas as pl
from jax.experimental.pallas import tpu as pltpu
from jax.sharding import PartitionSpec as P

H = 12
HD = 128
FF = 4608
W = 1024
BLK = 128
BACK = W // BLK
QW = H * HD

epsilon = 1e-06
masked_score = -1e30
scale = HD ** (-0.5)
log2e = 1.4426950408889634


def dot_f32(left, right, dims=((1,), (0,))):
    return lax.dot_general(left, right, (dims, ((), ())), preferred_element_type=jnp.float32)


def inv_rms(rows):
    return lax.rsqrt(jnp.mean(rows * rows, axis=-1, keepdims=True) + epsilon)


def add_low(a, b):
    return (a.astype(jnp.float32) + b.astype(jnp.float32)).astype(jnp.bfloat16)


def stack_heads(dst, src):
    for h in range(H):
        dst[h * BLK : (h + 1) * BLK, :] = src[0, :, h * HD : (h + 1) * HD]


def block_bias(seg_ref, seq, q_block, k_block, step):
    q_seg = jnp.broadcast_to(seg_ref[seq, q_block], (BLK, BLK))
    k_seg = jnp.broadcast_to(seg_ref[seq, k_block], (BLK, BLK)).T
    allowed = q_seg == k_seg
    if step in (0, BACK):
        key_at = lax.broadcasted_iota(jnp.int32, (BLK, BLK), 0)
        query_at = lax.broadcasted_iota(jnp.int32, (BLK, BLK), 1)
        allowed &= key_at <= query_at if step == BACK else key_at > query_at
    bias = jnp.where(allowed, 0.0, masked_score)
    return jnp.concatenate([bias] * H, axis=1)


def fold8(v, how):
    return how(v.reshape(BLK // 8, 8, QW), axis=0)


def attend_kernel(
    blk_ref, low_ref, slot_ref, half_ref, q_ref, kv_ref, seg_ref, o_ref, lse_ref, qs, sc, mx, tot, acc
):
    seq, mine = pl.program_id(0), pl.program_id(1)
    q_block = blk_ref[mine]
    lowest = low_ref[seq * 2 + mine]
    stack_heads(qs, q_ref)
    mx[...] = jnp.full(mx.shape, masked_score, jnp.float32)
    tot[...] = jnp.zeros_like(tot)
    acc[...] = jnp.zeros_like(acc)
    for step in range(BACK + 1):
        k_block = q_block - BACK + step

        @pl.when(k_block >= lowest)
        def _(step=step, k_block=k_block):
            keys = kv_ref[slot_ref[k_block], seq, half_ref[k_block], :, :HD]
            s = dot_f32(keys, qs[...], ((1,), (1,))) * (scale * log2e)
            s += block_bias(seg_ref, seq, q_block, k_block, step)
            sc[step * BLK : (step + 1) * BLK, :] = s
            mx[...] = jnp.maximum(mx[...], fold8(s, jnp.max))

    top = jnp.max(mx[...], axis=0, keepdims=True)
    for step in range(BACK + 1):
        k_block = q_block - BACK + step

        @pl.when(k_block >= lowest)
        def _(step=step, k_block=k_block):
            vals = kv_ref[slot_ref[k_block], seq, half_ref[k_block], :, HD:]
            p = jnp.exp2(sc[step * BLK : (step + 1) * BLK, :] - top)
            tot[...] += fold8(p, jnp.sum)
            acc[...] += dot_f32(vals, p.astype(jnp.bfloat16), ((0,), (0,)))

    total = jnp.sum(tot[...], axis=0, keepdims=True)
    out = acc[...] / total
    for h in range(H):
        o_ref[0, :, h * HD : (h + 1) * HD] = out[:, h * BLK : (h + 1) * BLK].T.astype(jnp.bfloat16)
    lse_ref[0, 0] = top + jnp.log2(total)


def attend_back_kernel(
    blk_ref, low_ref, slot_ref, half_ref, q_ref, do_ref, o_ref, kv_ref, seg_ref, lse_ref,
    dq_ref, dkv_ref, qs, dos, dqt, dacc,
):
    seq, mine = pl.program_id(0), pl.program_id(1)
    q_block = blk_ref[mine]
    lowest = low_ref[seq * 2 + mine]

    @pl.when((seq == 0) & (mine == 0))
    def _():
        dacc[...] = jnp.zeros_like(dacc)

    stack_heads(qs, q_ref)
    stack_heads(dos, do_ref)
    dqt[...] = jnp.zeros_like(dqt)
    deltas = []
    for h in range(H):
        cols = slice(h * HD, (h + 1) * HD)
        both = do_ref[0, :, cols].astype(jnp.float32) * o_ref[0, :, cols].astype(jnp.float32)
        deltas.append(jnp.sum(both.T, axis=0, keepdims=True))
    delta = jnp.concatenate(deltas, axis=1)
    lse = lse_ref[0, 0]
    for step in range(BACK + 1):
        k_block = q_block - BACK + step

        @pl.when(k_block >= lowest)
        def _(step=step, k_block=k_block):
            slot, half = slot_ref[k_block], half_ref[k_block]
            keys = kv_ref[slot, seq, half, :, :HD]
            vals = kv_ref[slot, seq, half, :, HD:]
            s = dot_f32(keys, qs[...], ((1,), (1,))) * (scale * log2e)
            p = jnp.exp2(s + block_bias(seg_ref, seq, q_block, k_block, step) - lse)
            dp = dot_f32(vals, dos[...], ((1,), (1,)))
            d_raw = (p * (dp - delta)).astype(jnp.bfloat16)
            dqt[...] += dot_f32(keys, d_raw, ((0,), (0,)))
            dacc[slot, seq, half, :, :HD] += dot_f32(d_raw, qs[...]) * scale
            dacc[slot, seq, half, :, HD:] += dot_f32(p.astype(jnp.bfloat16), dos[...])

    out = dqt[...] * scale
    for h in range(H):
        dq_ref[0, :, h * HD : (h + 1) * HD] = out[:, h * BLK : (h + 1) * BLK].T.astype(jnp.bfloat16)

    @pl.when((seq == pl.num_programs(0) - 1) & (mine == 1))
    def _():
        dkv_ref[...] = dacc[...].astype(jnp.bfloat16)


def whole_spec(shape):
    return pl.BlockSpec(shape, lambda s, m, *_: (0,) * len(shape))


def row_spec():
    return pl.BlockSpec((1, BLK, QW), lambda s, m, *_: (s, m, 0))


lse_spec = pl.BlockSpec((1, 1, 1, QW), lambda s, m, *_: (s, m, 0, 0))
kernel_params = pltpu.CompilerParams(vmem_limit_bytes=48 * 2**20)


def attend(scalars, qkv, key_value, seg):
    seqs, rows = qkv.shape[:2]
    return pl.pallas_call(
        attend_kernel,
        grid_spec=pltpu.PrefetchScalarGridSpec(
            num_scalar_prefetch=4,
            grid=(seqs, 2),
            in_specs=[row_spec(), whole_spec(key_value.shape), whole_spec(seg.shape)],
            out_specs=[row_spec(), lse_spec],
            scratch_shapes=[
                pltpu.VMEM((QW, HD), jnp.bfloat16),
                pltpu.VMEM((W + BLK, QW), jnp.float32),
                pltpu.VMEM((8, QW), jnp.float32),
                pltpu.VMEM((8, QW), jnp.float32),
                pltpu.VMEM((HD, QW), jnp.float32),
            ],
        ),
        out_shape=[
            jax.ShapeDtypeStruct((seqs, rows, QW), jnp.bfloat16),
            jax.ShapeDtypeStruct((seqs, 2, 1, QW), jnp.float32),
        ],
        compiler_params=kernel_params,
        cost_estimate=pl.CostEstimate(flops=7 * 10**9, bytes_accessed=8 * 2**20, transcendentals=7 * 10**6),
        name="attend",
    )(*scalars, qkv, key_value, seg)


def attend_back(scalars, qkv, d_mixed, mixed, key_value, seg, lse):
    seqs, rows = qkv.shape[:2]
    return pl.pallas_call(
        attend_back_kernel,
        grid_spec=pltpu.PrefetchScalarGridSpec(
            num_scalar_prefetch=4,
            grid=(seqs, 2),
            in_specs=[row_spec(), row_spec(), row_spec(), whole_spec(key_value.shape), whole_spec(seg.shape), lse_spec],
            out_specs=[row_spec(), whole_spec(key_value.shape)],
            scratch_shapes=[
                pltpu.VMEM((QW, HD), jnp.bfloat16),
                pltpu.VMEM((QW, HD), jnp.bfloat16),
                pltpu.VMEM((HD, QW), jnp.float32),
                pltpu.VMEM(key_value.shape, jnp.float32),
            ],
        ),
        out_shape=[
            jax.ShapeDtypeStruct((seqs, rows, QW), jnp.bfloat16),
            jax.ShapeDtypeStruct(key_value.shape, jnp.bfloat16),
        ],
        compiler_params=kernel_params,
        cost_estimate=pl.CostEstimate(flops=18 * 10**9, bytes_accessed=12 * 2**20, transcendentals=7 * 10**6),
        name="attend_back",
    )(*scalars, qkv, d_mixed, mixed, key_value, seg, lse)


class Plan:
    def __init__(self, mesh):
        self.shards = mesh.shape["shard"]
        self.ctxs = mesh.shape["ctx"]
        half = self.ctxs // 2
        self.ring = [2 * z for z in range(half)] + [2 * z + 1 for z in reversed(range(half))]
        self.place = [self.ring.index(c) for c in range(self.ctxs)]
        self.right = [(self.ring[i], self.ring[(i + 1) % self.ctxs]) for i in range(self.ctxs)]
        self.left = [(b, a) for a, b in self.right]
        self.bits = [1 << b for b in range(self.shards.bit_length() - 1)]

    def my_place(self):
        table = jnp.array(self.place, jnp.int32)
        at = jnp.arange(self.ctxs, dtype=jnp.int32) == lax.axis_index("ctx")
        return jnp.sum(jnp.where(at, table, 0))

    def swap(self, v, bit):
        return lax.ppermute(v, "shard", [(i, i ^ bit) for i in range(self.shards)])

    def my_bit(self, bit):
        return (lax.axis_index("shard") // bit) % 2

    def gather_xor(self, v):
        pieces = {0: v}
        for bit in reversed(self.bits):
            pieces |= {j | bit: self.swap(p, bit) for j, p in pieces.items()}
        return [pieces[j] for j in range(self.shards)]

    def scatter_xor(self, pieces):
        pieces = dict(enumerate(pieces))
        for bit in self.bits:
            got = {j ^ bit: self.swap(pieces[j], bit) for j in sorted(pieces, reverse=True) if j & bit}
            pieces = {j: add_low(pieces[j], got[j]) for j in got}
        return pieces[0]

    def gather_rows(self, v):
        out = v[None]
        for bit in reversed(self.bits):
            other = self.swap(out, bit)
            first = self.my_bit(bit) == 0
            out = jnp.stack([jnp.where(first, out, other), jnp.where(first, other, out)], axis=1)
            out = out.reshape(-1, *v.shape)
        return out.reshape(-1, *v.shape[1:])

    def scatter_rows(self, v, add=add_low):
        cur = v.reshape(self.shards, v.shape[0] // self.shards, *v.shape[1:])
        for bit in self.bits:
            pairs = cur.reshape(cur.shape[0] // 2, 2, *cur.shape[1:])
            mine = self.my_bit(bit)
            keep = lax.dynamic_index_in_dim(pairs, mine, 1, False)
            give = lax.dynamic_index_in_dim(pairs, 1 - mine, 1, False)
            cur = add(keep, self.swap(give, bit))
        return cur[0]

    def exchange_columns(self, v, blocks):
        me = lax.axis_index("shard")
        own = blocks(me)
        out = jnp.zeros((self.shards, *own.shape), own.dtype)
        out = lax.dynamic_update_index_in_dim(out, own, me, 0)
        for j in range(1, self.shards):
            other = me ^ j
            out = lax.dynamic_update_index_in_dim(out, self.swap(blocks(other), j), other, 0)
        return out

    def ring_gather(self, v):
        n = self.ctxs
        pieces = {0: v}
        a = b = v
        for step in range(1, n // 2 + 1):
            a = lax.ppermute(a, "ctx", self.right)
            pieces[step] = a
            if n - step > n // 2:
                b = lax.ppermute(b, "ctx", self.left)
                pieces[n - step] = b
        return jnp.stack([pieces[k] for k in range(n)])

    def ring_scatter(self, v):
        n = self.ctxs
        a, b = v[n // 2], v[n // 2 - 1]
        for step in range(n // 2 + 1, n + 1):
            a = lax.ppermute(a, "ctx", self.right)
            a = add_low(a, v[step % n])
        for step in range(n // 2 - 2, -1, -1):
            b = lax.ppermute(b, "ctx", self.left)
            if step:
                b = add_low(b, v[step])
        return a.astype(jnp.float32) + b.astype(jnp.float32)

    def ring_sum(self, v):
        n = self.ctxs
        rows, cols = v.shape
        cut = cols // 2
        place = self.my_place()
        chunks = v.reshape(n, rows // n, cols)

        def part(k, way):
            at = chunks[:, :, :cut] if way > 0 else chunks[:, :, cut:]
            return lax.dynamic_index_in_dim(at, lax.rem(place - way * k + 2 * n, n), 0, False)

        a, b = part(1, 1), part(1, -1)
        for step in range(2, n + 1):
            a = add_low(lax.ppermute(a, "ctx", self.right), part(step, 1))
            b = add_low(lax.ppermute(b, "ctx", self.left), part(step, -1))
        out = jnp.zeros(chunks.shape, jnp.float32)

        def put(out, piece, k, way):
            at = lax.rem(place - way * k + 2 * n, n)
            return lax.dynamic_update_slice(
                out, piece.astype(jnp.float32)[None], (at, 0, 0 if way > 0 else cut)
            )

        out = put(put(out, a, 0, 1), b, 0, -1)
        for step in range(1, n):
            a = lax.ppermute(a, "ctx", self.right)
            b = lax.ppermute(b, "ctx", self.left)
            out = put(put(out, a, step, 1), b, step, -1)
        return out.reshape(rows, cols)

    def small_sum(self, v):
        mine = self.scatter_rows(v, lambda a, b: a + b)
        bit = 1
        while bit < self.ctxs:
            mine = mine + lax.ppermute(mine, "ctx", [(c, c ^ bit) for c in range(self.ctxs)])
            bit *= 2
        return mine


def body(plan, tokens, segments, assign, w_qkv, w_out, w_gate_up, w_down, gain_attn, gain_ffn, cotangent):
    seqs, rows_dev, width = tokens.shape
    rows = seqs * rows_dev
    blocks = assign.shape[0]
    n = plan.shards
    ffn = FF // n
    low = jnp.bfloat16
    ids = jnp.arange(blocks, dtype=jnp.int32)
    my_blocks = lax.dynamic_slice_in_dim(assign, 2 * lax.axis_index("ctx"), 2, 0)
    place_of = jnp.array([plan.place[i // 2] for i in range(blocks)], jnp.int32)
    back = lax.rem(plan.my_place() - place_of + plan.ctxs, plan.ctxs)
    hit = assign[None, :] == ids[:, None]
    slot_of = jnp.sum(jnp.where(hit, back[None, :], 0), axis=1)
    half_of = jnp.sum(jnp.where(hit, (ids % 2)[None, :], 0), axis=1)
    firsts = jnp.stack([lax.dynamic_index_in_dim(segments, my_blocks[m] * BLK, 1, False) for m in range(2)], 1)
    starts = jnp.sum((segments[:, None, :] < firsts[:, :, None]).astype(jnp.int32), axis=2)
    lowest = jnp.maximum(jnp.maximum(starts // BLK, my_blocks[None, :] - BACK), 0).reshape(-1)
    scalars = (my_blocks, lowest, slot_of, half_of)
    seg = segments.astype(jnp.float32).reshape(seqs, blocks, 1, BLK)

    gains = plan.gather_rows(jnp.stack([gain_attn, gain_ffn], 1)).astype(jnp.float32)
    gain_one, gain_two = gains[:, 0], gains[:, 1]
    w_kv = plan.gather_rows(w_qkv[:, QW:])
    w_q = plan.gather_rows(w_qkv[:, :QW])
    w_o = plan.gather_rows(w_out)

    def gu_block(t):
        g = lax.dynamic_slice_in_dim(w_gate_up, t * ffn, ffn, 1)
        u = lax.dynamic_slice_in_dim(w_gate_up, FF + t * ffn, ffn, 1)
        return jnp.concatenate([g, u], axis=1)

    w_gu = plan.exchange_columns(w_gate_up, gu_block).reshape(width, 2 * ffn)

    tok = tokens.reshape(rows, width).astype(jnp.float32)
    scale_one = inv_rms(tok)
    hat_one = tok * scale_one
    normed_one = (hat_one * gain_one).astype(low)
    key_value = dot_f32(normed_one, w_kv).astype(low).reshape(seqs, 2, BLK, 2 * HD)
    kv_all = plan.ring_gather(key_value)
    queries = dot_f32(normed_one, w_q).astype(low).reshape(seqs, rows_dev, QW)
    mixed, lse = attend(scalars, queries, kv_all, seg)
    mixed_low = mixed.reshape(rows, QW)
    hidden = tok + dot_f32(mixed_low, w_o)
    scale_two = inv_rms(hidden)
    hat_two = hidden * scale_two
    normed_two = (hat_two * gain_two).astype(low)

    grad_low = cotangent.reshape(rows, width)
    n2 = jnp.concatenate(plan.gather_xor(normed_two))
    gy = jnp.concatenate(plan.gather_xor(grad_low))
    gate_up = dot_f32(n2, w_gu)
    d_act = dot_f32(gy, w_down, ((1,), (1,)))

    def gelu_product(gate_in, up_in):
        return jax.nn.gelu(gate_in, approximate=True) * up_in

    act, pull = jax.vjp(gelu_product, gate_up[:, :ffn], gate_up[:, ffn:])
    act = act.astype(low)
    d_gu = jnp.concatenate(pull(d_act), axis=1).astype(low)
    grad_down = plan.ring_sum(dot_f32(act, gy, ((0,), (0,))).astype(low))
    d_n2 = dot_f32(d_gu, w_gu, ((1,), (1,))).astype(low)
    d_normed_two = plan.scatter_xor([d_n2[j * rows : (j + 1) * rows] for j in range(n)]).astype(jnp.float32)
    part_gu = dot_f32(n2, d_gu, ((0,), (0,))).astype(low)
    me = lax.axis_index("shard")
    own_gu = plan.exchange_columns(
        part_gu, lambda t: lax.dynamic_slice_in_dim(part_gu, t * (width // n), width // n, 0)
    )
    summed = plan.ring_sum(own_gu.reshape(n * (width // n), 2 * ffn))
    summed = summed.reshape(n, width // n, 2, ffn)
    grad_gate_up = jnp.moveaxis(summed, 0, 2).reshape(width // n, 2 * FF)
    down = dot_f32(act, w_down).astype(low)
    branch = plan.scatter_xor([down[j * rows : (j + 1) * rows] for j in range(n)]).astype(jnp.float32)
    output = (hidden + branch).reshape(seqs, rows_dev, width)

    grad_gain_ffn = plan.small_sum(jnp.sum(d_normed_two * hat_two, axis=0))
    e = d_normed_two * gain_two
    d_hidden = grad_low.astype(jnp.float32) + scale_two * (
        e - hat_two * jnp.mean(e * hat_two, axis=-1, keepdims=True)
    )
    d_branch = d_hidden.astype(low)
    d_mixed = dot_f32(d_branch, w_o, ((1,), (1,))).astype(low).reshape(seqs, rows_dev, QW)
    dq, dkv = attend_back(scalars, queries, d_mixed, mixed, kv_all, seg, lse)
    dkv_own = plan.ring_scatter(dkv)
    d_qkv = jnp.concatenate([dq.reshape(rows, QW), dkv_own.astype(low).reshape(rows, 2 * HD)], axis=1)
    part_out = plan.scatter_rows(dot_f32(mixed_low, d_branch, ((0,), (0,))).astype(low))
    grad_out = plan.ring_sum(part_out)
    part_qkv = plan.scatter_rows(dot_f32(normed_one, d_qkv, ((0,), (0,))).astype(low))
    grad_qkv = plan.ring_sum(part_qkv)
    d_normed_one = dot_f32(dq.reshape(rows, QW), w_q, ((1,), (1,))) + dot_f32(
        d_qkv[:, QW:], w_kv, ((1,), (1,))
    )
    grad_gain_attn = plan.small_sum(jnp.sum(d_normed_one * hat_one, axis=0))
    f = d_normed_one * gain_one
    input_grad = d_hidden + scale_one * (f - hat_one * jnp.mean(f * hat_one, axis=-1, keepdims=True))
    return (
        output,
        input_grad.reshape(seqs, rows_dev, width),
        grad_qkv,
        grad_out,
        grad_gate_up,
        grad_down,
        grad_gain_attn,
        grad_gain_ffn,
    )


def solution(mesh):
    return jax.shard_map(
        functools.partial(body, Plan(mesh)),
        mesh=mesh,
        in_specs=(
            P("shard", "ctx", None),
            P("shard", None),
            P(),
            P("shard", None),
            P("shard", None),
            P("shard", None),
            P("shard", None),
            P("shard"),
            P("shard"),
            P("shard", "ctx", None),
        ),
        out_specs=(
            P("shard", "ctx", None),
            P("shard", "ctx", None),
            P("shard", None),
            P("shard", None),
            P("shard", None),
            P("shard", None),
            P("shard"),
            P("shard"),
        ),
        check_vma=False,
    )
```

time: 1510 us -> 1010 us (0.67)
  waiting for transfers between devices: 1030 us -> 422 us
  starting transfers between devices: 0.44 us -> 175 us
  matrix products: 308 us -> 135 us
  local copies, waits for them, and re-layouts: 45.7 us -> 125 us
  other arithmetic: 46.2 us -> 112 us
  blocking collectives: 55 us -> 0 us
  Pallas kernels: 0 us -> 27.2 us
    ppermute x0 -> x166, waiting for transfers between devices: none -> 422 us  [the longest x34 156 us: swap(): return lax.ppermute(v, 'shard', [(i, i ^ bit) for i in range(self.shards)])]
    reduce_scatter x5 -> x0, waiting for transfers between devices: 390 us -> none  [the longest x4 374 us: weight_grad(): lax.psum_scatter(lax.dot_general(left_low, right_low, (((0,), (0,)), ((),...]
    psum x1 -> x0, waiting for transfers between devices: 349 us -> none  [body(): lax.psum(grad_qkv_part.astype(jnp.bfloat16), 'ctx').astype(jnp.float32)]
    all_gather x5 -> x0, waiting for transfers between devices: 292 us -> none  [the longest x2 195 us: normed_project(): lax.all_gather(weight, 'shard', axis=0, tiled=True)]
    ppermute x0 -> x166, starting transfers between devices: none -> 175 us  [the longest x28 37.6 us: ring_sum(): a = lax.ppermute(a, 'ctx', self.right)]
    dot_general x24 -> x14, matrix products: 308 us -> 135 us  [dot_f32(): lax.dot_general(left, right, (dims, ((), ())), preferred_element_type=jnp...]
    psum x1 -> x0, blocking collectives: 43.8 us -> none  [body(): lax.psum((gain_one_local, gain_two_local), ('ctx', 'shard'))]
    dynamic_update_slice x2 -> x65, other arithmetic: 0.79 us -> 43.5 us  [the longest x64 42.2 us: put(): lax.dynamic_update_slice(out, piece.astype(jnp.float32)[None], (at, 0, 0...]
  transfers between devices with their start and end apart: 11 -> 166, of which waited for: 10 -> 97; matrix products, arithmetic and copies ran while one was open for 14% -> 31% of each run, Pallas kernels for 0% -> 3%
where the time goes in v1:
time: 1010 us
  waiting for transfers between devices  422 us (42%)
  starting transfers between devices  175 us (17%)
  matrix products  135 us (13%)
  local copies, waits for them, and re-layouts  125 us (12%)
  other arithmetic  112 us (11%)
  Pallas kernels  27.2 us (3%)
  between operations  15 us (1%)
    ppermute x34, waiting for transfers between devices, swap(): return lax.ppermute(v, 'shard', [(i, i ^ bit) for i in range(self.shards)])  156 us
    dot_general x14, matrix products, dot_f32(): lax.dot_general(left, right, (dims, ((), ())), preferred_element_type=jnp...  135 us
    ppermute x28, waiting for transfers between devices, ring_sum(): a = add_low(lax.ppermute(a, 'ctx', self.right), part(step, 1))  83.5 us
    ppermute x28, waiting for transfers between devices, ring_sum(): a = lax.ppermute(a, 'ctx', self.right)  58.3 us
    ppermute x28, waiting for transfers between devices, ring_sum(): b = add_low(lax.ppermute(b, 'ctx', self.left), part(step, -1))  45.6 us
    dynamic_update_slice x64, other arithmetic, put(): lax.dynamic_update_slice(out, piece.astype(jnp.float32)[None], (at, 0, 0...  42.2 us
    ppermute x28, starting transfers between devices, ring_sum(): a = lax.ppermute(a, 'ctx', self.right)  37.6 us
    ppermute x28, waiting for transfers between devices, ring_sum(): b = lax.ppermute(b, 'ctx', self.left)  36.5 us
  transfers between devices with their start and end apart: 166, of which 97 were waited for; matrix products, arithmetic and copies ran while one was open for 31% of the time, Pallas kernels for 3%

profile of v1, /device:TPU:0, one launch (start us, length us, event | category | flops | bytes accessed | tf_op | source)
XLA Modules:
  0.0 1010.0 jit_solution(4078506567476604968)
XLA Ops:
  85.7 10.0 attend.1
  121.5 29.0 %collective-permute-done.25 = bf16[512,1536]{1,0:T(8,128)(2,1)} collective-permute-done((bf16[512,1536]{1,0:T(8,128)(2,1)}, bf16[512,1536]{1,0:T(8,128)(2,1)}, u32[]{:S(2)}, u32[]{:S(2)}) %collective-permute-start.25) | collective-permute-done | bytes 1572896 | tf_op jit(solution)/shard_map/ppermute | solution.py:225
  153.9 30.4 %collective-permute-done.16 = bf16[512,1536]{1,0:T(8,128)(2,1)} collective-permute-done((bf16[512,1536]{1,0:T(8,128)(2,1)}, bf16[512,1536]{1,0:T(8,128)(2,1)}, u32[]{:S(2)}, u32[]{:S(2)}) %collective-permute-start.16) | collective-permute-done | bytes 1572896 | tf_op jit(solution)/shard_map/ppermute | solution.py:225
  187.0 29.0 %collective-permute-done.20 = bf16[384,2304]{1,0:T(8,128)(2,1)} collective-permute-done((bf16[384,2304]{1,0:T(8,128)(2,1)}, bf16[384,2304]{1,0:T(8,128)(2,1)}, u32[]{:S(2)}, u32[]{:S(2)}) %collective-permute-start.20) | collective-permute-done | bytes 1769504 | tf_op jit(solution)/shard_map/ppermute | solution.py:225
  218.8 25.6 %fusion.20 = f32[2048,2304]{1,0:T(8,128)} fusion(bf16[1536,2304]{1,0:T(8,128)(2,1)} %bitcast.49, bf16[512,1536]{1,0:T(8,128)(2,1)} %collective-permute-done.17, bf16[512,1536]{1,0:T(8,128)(2,1)} %collective-permute-done.16, bf16[512,1536]{1,0:T(8,128)(2,1)S(1)} %collective-permute-done.15, bf16[512,1536]{1,0:T(8,128)(2,1)} %multiply_convert_fusion.3), kind=kOutput, calls=%fused_computation.86 | convolution fusion | flops 14520680448 | bytes 32243712 | tf_op jit(solution)/shard_map/dot_general | solution.py:25
  245.5 23.9 %fusion.6 = (bf16[2048,1152]{1,0:T(8,128)(2,1)}, bf16[2048,1152]{1,0:T(8,128)(2,1)}, bf16[2048,1152]{1,0:T(8,128)(2,1)}) fusion(f32[2048,2304]{1,0:T(8,128)} %fusion.20, bf16[1152,1536]{1,0:T(8,128)(2,1)S(1)} %copy-done, bf16[512,1536]{1,0:T(8,128)(2,1)} %collective-permute-done.26, bf16[512,1536]{1,0:T(8,128)(2,1)} %collective-permute-done.25, ...), kind=kOutput, calls=%fused_computation.9 | convolution fusion | flops 7334264832 | bytes 42860544 | tf_op jit(solution)/shard_map/dot_general | solution.py:25
  269.4 19.4 %convolution_convert_fusion.4 = bf16[2048,1536]{1,0:T(8,128)(2,1)S(1)} fusion(bf16[1536,2304]{1,0:T(8,128)(2,1)} %bitcast.49, bf16[2048,1152]{1,0:T(8,128)(2,1)} %get-tuple-element.60, bf16[2048,1152]{1,0:T(8,128)(2,1)} %get-tuple-element.59), kind=kOutput, calls=%fused_computation.17 | convolution fusion | flops 14517534720 | bytes 22806528 | tf_op jit(solution)/shard_map/dot_general | solution.py:25
  295.1 8.7 convolution_convert_fusion.5
  308.4 9.5 convolution_convert_fusion.1
  321.5 21.8 %convolution_convert_fusion = bf16[1536,2304]{1,0:T(8,128)(2,1)} fusion(bf16[2048,1152]{1,0:T(8,128)(2,1)} %get-tuple-element.60, bf16[2048,1152]{1,0:T(8,128)(2,1)} %get-tuple-element.59, bf16[512,1536]{1,0:T(8,128)(2,1)} %collective-permute-done.17, bf16[512,1536]{1,0:T(8,128)(2,1)} %collective-permute-done.16, bf16[512,1536]{1,0:T(8,128)(2,1)} %copy-done.58, ...), kind=kOutput, calls=%fused_computation.2 | convolution fusion | flops 14543093760 | bytes 22806528 | tf_op jit(solution)/shard_map/dot_general | solution.py:25
  358.1 6.2 collective-permute-done.136
  407.6 6.6 collective-permute-done.140
  438.5 29.5 %collective-permute-done.98 = bf16[384,2304]{1,0:T(8,128)(2,1)S(1)} collective-permute-done((bf16[384,2304]{1,0:T(8,128)(2,1)S(1)}, bf16[384,2304]{1,0:T(8,128)(2,1)S(1)}, u32[]{:S(2)}, u32[]{:S(2)}) %collective-permute-start.98) | collective-permute-done | bytes 1769504 | tf_op jit(solution)/shard_map/ppermute | solution.py:225
  468.9 36.2 %collective-permute-done.99 = bf16[384,2304]{1,0:T(8,128)(2,1)S(1)} collective-permute-done((bf16[384,2304]{1,0:T(8,128)(2,1)S(1)}, bf16[384,2304]{1,0:T(8,128)(2,1)S(1)}, u32[]{:S(2)}, u32[]{:S(2)}) %collective-permute-start.99) | collective-permute-done | bytes 1769504 | tf_op jit(solution)/shard_map/ppermute | solution.py:225
  528.2 8.3 collective-permute-done.100
  588.4 8.6 collective-permute-done.102
  622.8 6.1 convolution_convert_fusion.6
  629.8 17.1 %attend_back.1 = (bf16[2,256,1536]{2,1,0:T(8,128)(2,1)S(1)}, bf16[8,2,2,128,256]{4,3,2,1,0:T(8,128)(2,1)}) custom-call(s32[2]{0:T(128)S(1)} %copy-done.5, s32[4]{0:T(128)S(1)} %copy-done.15, s32[16]{0:T(128)S(1)} %copy-done.9, s32[16]{0:T(128)S(1)} %copy-done.7, bf16[2,256,1536]{2,1,0:T(8,128)(2,1)S(1)} %bitcast.603, bf16[2,256,1536]{2,1,0:T(8,128)(2,1)S(1)} %bitcast.606, ...), custom_call_target="tpu_custom_call" | custom-call | flops 17999998976 | bytes 12582912 | tf_op jit(solution)/shard_map/attend_back/pallas_call | solution.py:184
  666.1 10.0 collective-permute-start.67
  735.5 7.3 collective-permute-done.106
  742.8 6.6 broadcast_in_dim.548
  885.6 17.3 %reshape_reshape.34 = f32[4,384,2,1152]{3,2,1,0:T(2,128)} reshape(f32[8,192,2304]{2,1,0:T(8,128)} %convert_dynamic-update-slice_fusion) | data formatting | bytes 28311552 | tf_op jit(solution)/shard_map/reshape;reshape | solution.py:403
  902.9 22.0 %copy.46 = f32[384,2,4,1152]{0,3,2,1:T(8,128)} copy(f32[384,2,4,1152]{3,1,0,2:T(2,128)} %bitcast.607) | data formatting | bytes 28311552 | tf_op jit(solution)/shard_map/transpose | solution.py:404
  924.9 15.1 %copy.47 = f32[384,9216]{1,0:T(8,128)} copy(f32[384,9216]{0,1:T(8,128)} %bitcast.608) | data formatting | bytes 28311552
  (705 shorter events, 590.8 us)
Async XLA Ops:
  0.6 54.8 %collective-permute-start.13 = (bf16[1,384,1536]{2,1,0:T(8,128)(2,1)}, bf16[1,384,1536]{2,1,0:T(8,128)(2,1)}, u32[]{:S(2)}, u32[]{:S(2)}) collective-permute-start(bf16[1,384,1536]{2,1,0:T(8,128)(2,1)} %bitcast.636), channel_id=1, source_target_pairs={{0,2},{1,3},{2,0},{3,1},{4,6},{5,7},{6,4},{7,5},{8,10},{9,11},{10,... | collective-permute-start | bytes 3538952 | tf_op jit(solution)/shard_map/ppermute | solution.py:225
  11.6 51.5 %collective-permute-start.2 = (bf16[1,384,1536]{2,1,0:T(8,128)(2,1)}, bf16[1,384,1536]{2,1,0:T(8,128)(2,1)}, u32[]{:S(2)}, u32[]{:S(2)}) collective-permute-start(bf16[1,384,1536]{2,1,0:T(8,128)(2,1)} %slice_bitcast_fusion), channel_id=1, source_target_pairs={{0,2},{1,3},{2,0},{3,1},{4,6},{5,7},{6,4},{7,5},{8,10},{9,11},{10,... | collective-permute-start | bytes 3538952 | tf_op jit(solution)/shard_map/ppermute | solution.py:225
  18.7 131.8 %collective-permute-start.18 = (bf16[384,2304]{1,0:T(8,128)(2,1)}, bf16[384,2304]{1,0:T(8,128)(2,1)}, u32[]{:S(2)}, u32[]{:S(2)}) collective-permute-start(bf16[384,2304]{1,0:T(8,128)(2,1)} %pad_maximum_fusion.7), channel_id=1, source_target_pairs={{0,1},{1,0},{2,3},{3,2},{4,5},{5,4},{6,7},{7,6},{8,9},{9,8},{10,11... | collective-permute-start | bytes 5308424 | tf_op jit(solution)/shard_map/ppermute | solution.py:225
  75.0 78.9 %collective-permute-start.19 = (bf16[384,2304]{1,0:T(8,128)(2,1)}, bf16[384,2304]{1,0:T(8,128)(2,1)}, u32[]{:S(2)}, u32[]{:S(2)}) collective-permute-start(bf16[384,2304]{1,0:T(8,128)(2,1)} %pad_maximum_fusion.8), channel_id=1, source_target_pairs={{0,2},{1,3},{2,0},{3,1},{4,6},{5,7},{6,4},{7,5},{8,10},{9,11},{10,... | collective-permute-start | bytes 5308424 | tf_op jit(solution)/shard_map/ppermute | solution.py:225
  76.4 74.1 %collective-permute-start.25 = (bf16[512,1536]{1,0:T(8,128)(2,1)}, bf16[512,1536]{1,0:T(8,128)(2,1)}, u32[]{:S(2)}, u32[]{:S(2)}) collective-permute-start(bf16[512,1536]{1,0:T(8,128)(2,1)} %bitcast.51), channel_id=1, source_target_pairs={{0,2},{1,3},{2,0},{3,1},{4,6},{5,7},{6,4},{7,5},{8,10},{9,11},{10,... | collective-permute-start | bytes 4718600 | tf_op jit(solution)/shard_map/ppermute | solution.py:225
  100.1 84.1 %collective-permute-start.16 = (bf16[512,1536]{1,0:T(8,128)(2,1)}, bf16[512,1536]{1,0:T(8,128)(2,1)}, u32[]{:S(2)}, u32[]{:S(2)}) collective-permute-start(bf16[512,1536]{1,0:T(8,128)(2,1)} %multiply_convert_fusion.3), channel_id=1, source_target_pairs={{0,2},{1,3},{2,0},{3,1},{4,6},{5,7},{6,4},{7,5},{8,10},{9,11},{10,... | collective-permute-start | bytes 4718600 | tf_op jit(solution)/shard_map/ppermute | solution.py:225
  103.1 112.9 %collective-permute-start.20 = (bf16[384,2304]{1,0:T(8,128)(2,1)}, bf16[384,2304]{1,0:T(8,128)(2,1)}, u32[]{:S(2)}, u32[]{:S(2)}) collective-permute-start(bf16[384,2304]{1,0:T(8,128)(2,1)} %pad_maximum_fusion.9), channel_id=1, source_target_pairs={{0,3},{1,2},{2,1},{3,0},{4,7},{5,6},{6,5},{7,4},{8,11},{9,10},{10,... | collective-permute-start | bytes 5308424 | tf_op jit(solution)/shard_map/ppermute | solution.py:225
  150.5 93.9 %collective-permute-start.24 = (bf16[512,1536]{1,0:T(8,128)(2,1)}, bf16[512,1536]{1,0:T(8,128)(2,1)S(1)}, u32[]{:S(2)}, u32[]{:S(2)}) collective-permute-start(bf16[512,1536]{1,0:T(8,128)(2,1)} %bitcast.51), channel_id=1, source_target_pairs={{0,1},{1,0},{2,3},{3,2},{4,5},{5,4},{6,7},{7,6},{8,9},{9,8},{10,11... | collective-permute-start | bytes 4718600 | tf_op jit(solution)/shard_map/ppermute | solution.py:225
  150.5 95.0 %collective-permute-start.26 = (bf16[512,1536]{1,0:T(8,128)(2,1)}, bf16[512,1536]{1,0:T(8,128)(2,1)}, u32[]{:S(2)}, u32[]{:S(2)}) collective-permute-start(bf16[512,1536]{1,0:T(8,128)(2,1)} %collective-permute-done.25), channel_id=1, source_target_pairs={{0,1},{1,0},{2,3},{3,2},{4,5},{5,4},{6,7},{7,6},{8,9},{9,8},{10,11... | collective-permute-start | bytes 4718600 | tf_op jit(solution)/shard_map/ppermute | solution.py:225
  153.9 65.0 %collective-permute-start.15 = (bf16[512,1536]{1,0:T(8,128)(2,1)}, bf16[512,1536]{1,0:T(8,128)(2,1)S(1)}, u32[]{:S(2)}, u32[]{:S(2)}) collective-permute-start(bf16[512,1536]{1,0:T(8,128)(2,1)} %multiply_convert_fusion.3), channel_id=1, source_target_pairs={{0,1},{1,0},{2,3},{3,2},{4,5},{5,4},{6,7},{7,6},{8,9},{9,8},{10,11... | collective-permute-start | bytes 4718600 | tf_op jit(solution)/shard_map/ppermute | solution.py:225
  293.5 133.0 %collective-permute-start.28 = (bf16[512,1536]{1,0:T(8,128)(2,1)}, bf16[512,1536]{1,0:T(8,128)(2,1)}, u32[]{:S(2)}, u32[]{:S(2)}) collective-permute-start(bf16[512,1536]{1,0:T(8,128)(2,1)} %get-tuple-element.76), channel_id=1, source_target_pairs={{0,1},{1,0},{2,3},{3,2},{4,5},{5,4},{6,7},{7,6},{8,9},{9,8},{10,11... | collective-permute-start | bytes 4718600 | tf_op jit(solution)/shard_map/ppermute | solution.py:225
  295.1 316.1 %collective-permute-start.27 = (bf16[512,1536]{1,0:T(8,128)(2,1)}, bf16[512,1536]{1,0:T(8,128)(2,1)}, u32[]{:S(2)}, u32[]{:S(2)}) collective-permute-start(bf16[512,1536]{1,0:T(8,128)(2,1)} %get-tuple-element.75), channel_id=1, source_target_pairs={{0,1},{1,0},{2,3},{3,2},{4,5},{5,4},{6,7},{7,6},{8,9},{9,8},{10,11... | collective-permute-start | bytes 4718600 | tf_op jit(solution)/shard_map/ppermute | solution.py:225
  307.4 125.0 %collective-permute-start.22 = (bf16[512,1536]{1,0:T(8,128)(2,1)}, bf16[512,1536]{1,0:T(8,128)(2,1)}, u32[]{:S(2)}, u32[]{:S(2)}) collective-permute-start(bf16[512,1536]{1,0:T(8,128)(2,1)} %get-tuple-element.78), channel_id=1, source_target_pairs={{0,1},{1,0},{2,3},{3,2},{4,5},{5,4},{6,7},{7,6},{8,9},{9,8},{10,11... | collective-permute-start | bytes 4718600 | tf_op jit(solution)/shard_map/ppermute | solution.py:225
  348.4 88.3 %collective-permute-start.97 = (bf16[384,2304]{1,0:T(8,128)(2,1)S(1)}, bf16[384,2304]{1,0:T(8,128)(2,1)S(1)}, u32[]{:S(2)}, u32[]{:S(2)}) collective-permute-start(bf16[384,2304]{1,0:T(8,128)(2,1)S(1)} %get-tuple-element.66), channel_id=1, source_target_pairs={{0,1},{1,0},{2,3},{3,2},{4,5},{5,4},{6,7},{7,6},{8,9},{9,8},{10,11... | collective-permute-start | bytes 5308424 | tf_op jit(solution)/shard_map/ppermute | solution.py:225
  426.4 190.8 %collective-permute-start.21 = (bf16[512,1536]{1,0:T(8,128)(2,1)}, bf16[512,1536]{1,0:T(8,128)(2,1)}, u32[]{:S(2)}, u32[]{:S(2)}) collective-permute-start(bf16[512,1536]{1,0:T(8,128)(2,1)} %get-tuple-element.77), channel_id=1, source_target_pairs={{0,1},{1,0},{2,3},{3,2},{4,5},{5,4},{6,7},{7,6},{8,9},{9,8},{10,11... | collective-permute-start | bytes 4718600 | tf_op jit(solution)/shard_map/ppermute | solution.py:225
  432.4 72.7 %collective-permute-start.99 = (bf16[384,2304]{1,0:T(8,128)(2,1)S(1)}, bf16[384,2304]{1,0:T(8,128)(2,1)S(1)}, u32[]{:S(2)}, u32[]{:S(2)}) collective-permute-start(bf16[384,2304]{1,0:T(8,128)(2,1)S(1)} %get-tuple-element.64), channel_id=1, source_target_pairs={{0,3},{1,2},{2,1},{3,0},{4,7},{5,6},{6,5},{7,4},{8,11},{9,10},{10,... | collective-permute-start | bytes 5308424 | tf_op jit(solution)/shard_map/ppermute | solution.py:225
  436.6 70.5 %collective-permute-start.142 = (bf16[144,768]{1,0:T(8,128)(2,1)S(1)}, bf16[144,768]{1,0:T(8,128)(2,1)}, u32[]{:S(2)}, u32[]{:S(2)}) collective-permute-start(bf16[144,768]{1,0:T(8,128)(2,1)S(1)} %get-tuple-element.43), channel_id=1, source_target_pairs={{0,8},{8,16},{16,24},{24,28},{28,20},{20,12},{12,4},{4,0},{1,9},{9... | collective-permute-start | bytes 663560 | tf_op jit(solution)/shard_map/ppermute | solution.py:321
  468.0 42.7 %collective-permute-start.143 = (bf16[144,768]{1,0:T(8,128)(2,1)S(1)}, bf16[144,768]{1,0:T(8,128)(2,1)}, u32[]{:S(2)}, u32[]{:S(2)}) collective-permute-start(bf16[144,768]{1,0:T(8,128)(2,1)S(1)} %get-tuple-element.41), channel_id=1, source_target_pairs={{8,0},{16,8},{24,16},{28,24},{20,28},{12,20},{4,12},{0,4},{9,1},{1... | collective-permute-start | bytes 663560 | tf_op jit(solution)/shard_map/ppermute | solution.py:322
  505.1 107.6 %collective-permute-start.29 = (bf16[512,1536]{1,0:T(8,128)(2,1)}, bf16[512,1536]{1,0:T(8,128)(2,1)S(1)}, u32[]{:S(2)}, u32[]{:S(2)}) collective-permute-start(bf16[512,1536]{1,0:T(8,128)(2,1)} %add_convert_fusion.1), channel_id=1, source_target_pairs={{0,2},{1,3},{2,0},{3,1},{4,6},{5,7},{6,4},{7,5},{8,10},{9,11},{10,... | collective-permute-start | bytes 4718600 | tf_op jit(solution)/shard_map/ppermute | solution.py:225
  609.9 68.0 %collective-permute-start.110 = (bf16[192,1152]{1,0:T(8,128)(2,1)}, bf16[192,1152]{1,0:T(8,128)(2,1)}, u32[]{:S(2)}, u32[]{:S(2)}) collective-permute-start(bf16[192,1152]{1,0:T(8,128)(2,1)} %fusion.25), channel_id=1, source_target_pairs={{8,0},{16,8},{24,16},{28,24},{20,28},{12,20},{4,12},{0,4},{9,1},{1... | collective-permute-start | bytes 1327112 | tf_op jit(solution)/shard_map/ppermute | solution.py:310
  611.2 76.1 %collective-permute-start.103 = (bf16[192,1152]{1,0:T(8,128)(2,1)}, bf16[192,1152]{1,0:T(8,128)(2,1)}, u32[]{:S(2)}, u32[]{:S(2)}) collective-permute-start(bf16[192,1152]{1,0:T(8,128)(2,1)} %fusion.32), channel_id=1, source_target_pairs={{0,8},{8,16},{16,24},{24,28},{28,20},{20,12},{12,4},{4,0},{1,9},{9... | collective-permute-start | bytes 1327112 | tf_op jit(solution)/shard_map/ppermute | solution.py:309
  666.1 101.9 %collective-permute-start.67 = (bf16[2,384,1536]{2,1,0:T(8,128)(2,1)}, bf16[2,384,1536]{2,1,0:T(8,128)(2,1)}, u32[]{:S(2)}, u32[]{:S(2)}) collective-permute-start(bf16[2,384,1536]{2,1,0:T(8,128)(2,1)} %dynamic-slice_bitcast_fusion.1), channel_id=1, source_target_pairs={{0,1},{1,0},{2,3},{3,2},{4,5},{5,4},{6,7},{7,6},{8,9},{9,8},{10,11... | collective-permute-start | bytes 7077896 | tf_op jit(solution)/shard_map/ppermute | solution.py:225
  723.9 96.3 %collective-permute-start.37 = (bf16[2,384,1792]{2,1,0:T(8,128)(2,1)}, bf16[2,384,1792]{2,1,0:T(8,128)(2,1)S(1)}, u32[]{:S(2)}, u32[]{:S(2)}) collective-permute-start(bf16[2,384,1792]{2,1,0:T(8,128)(2,1)} %dynamic-slice_bitcast_fusion), channel_id=1, source_target_pairs={{0,1},{1,0},{2,3},{3,2},{4,5},{5,4},{6,7},{7,6},{8,9},{9,8},{10,11... | collective-permute-start | bytes 8257544 | tf_op jit(solution)/shard_map/ppermute | solution.py:225
  822.0 118.0 %collective-permute-start.38 = (bf16[1,384,1792]{2,1,0:T(8,128)(2,1)}, bf16[1,384,1792]{2,1,0:T(8,128)(2,1)}, u32[]{:S(2)}, u32[]{:S(2)}) collective-permute-start(bf16[1,384,1792]{2,1,0:T(8,128)(2,1)} %constant_dynamic-slice_fusion.12), channel_id=1, source_target_pairs={{0,2},{1,3},{2,0},{3,1},{4,6},{5,7},{6,4},{7,5},{8,10},{9,11},{10,... | collective-permute-start | bytes 4128776 | tf_op jit(solution)/shard_map/ppermute | solution.py:225
  (212 other events, 2642.3 us)

commit v2 on v1

--- a/solution.py
+++ b/solution.py
@@ -19,6 +19,8 @@
 masked_score = -1e30
 scale = HD ** (-0.5)
 log2e = 1.4426950408889634
+gelu_c = 0.7978845608028654
+gelu_a = 0.044715
 
 
 def dot_f32(left, right, dims=((1,), (0,))):
@@ -205,6 +207,201 @@
     )(*scalars, qkv, d_mixed, mixed, key_value, seg, lse)
 
 
+def ffn_kernel(counts, at_ref, n2_a, gy_a, n2_b, gy_b, *refs):
+    total = sum(counts)
+    pieces = refs[:total]
+    *outs, wg_ref, wu_ref, wd_ref, sems = refs[-13:]
+    act_ref, dg_ref, du_ref, n2_out, gy_out, dn2_a, down_a, dn2_b, down_b = outs
+    step = pl.program_id(0)
+    first = step < pl.num_programs(0) // 2
+    weights = []
+    for dst, count in zip((wg_ref, wu_ref, wd_ref), counts, strict=True):
+        copies = []
+        for _ in range(count):
+            i = sum(map(len, weights)) + len(copies)
+            src = pieces[i]
+            rows = src.shape[0]
+            place = dst.at[pl.ds(pl.multiple_of(at_ref[i], 16), rows)]
+            copies.append(pltpu.make_async_copy(src, place, sems.at[i]))
+        weights.append(copies)
+
+    @pl.when(step == 0)
+    def _():
+        for copies in weights:
+            for copy in copies:
+                copy.start()
+
+    def ready(copies):
+        @pl.when(step == 0)
+        def _():
+            for copy in copies:
+                copy.wait()
+
+    n2 = jnp.where(first, n2_a[...], n2_b[...])
+    gy = jnp.where(first, gy_a[...], gy_b[...])
+    n2_out[0] = n2
+    gy_out[0] = gy
+    ready(weights[0])
+    gate = dot_f32(n2, wg_ref[...])
+    ready(weights[1])
+    up = dot_f32(n2, wu_ref[...])
+    ready(weights[2])
+    d_act = dot_f32(gy, wd_ref[...], ((1,), (1,)))
+    square = gate * gate
+    inner = jnp.tanh(gate * (gelu_c + gelu_c * gelu_a * square))
+    half = 0.5 + 0.5 * inner
+    gelu = gate * half
+    slope = half + 0.5 * gate * (1.0 - inner * inner) * (gelu_c + 3.0 * gelu_c * gelu_a * square)
+    act = (gelu * up).astype(jnp.bfloat16)
+    d_gate = (d_act * up * slope).astype(jnp.bfloat16)
+    d_up = (d_act * gelu).astype(jnp.bfloat16)
+    act_ref[0] = act
+    dg_ref[0] = d_gate
+    du_ref[0] = d_up
+    dn2 = dot_f32(d_gate, wg_ref[...], ((1,), (1,))) + dot_f32(d_up, wu_ref[...], ((1,), (1,)))
+    dn2 = dn2.astype(jnp.bfloat16)
+    down = dot_f32(act, wd_ref[...]).astype(jnp.bfloat16)
+
+    @pl.when(first)
+    def _():
+        dn2_a[...] = dn2
+        down_a[...] = down
+
+    @pl.when(jnp.logical_not(first))
+    def _():
+        dn2_b[...] = dn2
+        down_b[...] = down
+
+
+def ffn(pair, pieces, n2, gy, gate, up, w_down, held):
+    rows, width = n2[0].shape
+    units = w_down.shape[0]
+    tile = rows // 2
+    held_shapes = [(pieces, rows, units)] * 3 + [(pieces, rows, width)] * 2
+    held_spec = [
+        pl.BlockSpec((1, tile, s[2]), lambda t, at: (2 * pair + t // 2, t % 2, 0)) for s in held_shapes
+    ]
+    a_spec = pl.BlockSpec((tile, width), lambda t, at: (jnp.minimum(t, 1), 0))
+    b_spec = pl.BlockSpec((tile, width), lambda t, at: (jnp.maximum(t - 2, 0), 0))
+    parts = [*gate, *up, (w_down, 0)]
+    places = jnp.stack([jnp.asarray(at, jnp.int32) for _, at in parts])
+    arrays = [p for p, _ in parts]
+    out = pl.pallas_call(
+        functools.partial(ffn_kernel, (len(gate), len(up), 1)),
+        grid_spec=pltpu.PrefetchScalarGridSpec(
+            num_scalar_prefetch=1,
+            grid=(4,),
+            in_specs=[a_spec, a_spec, b_spec, b_spec]
+            + [pl.BlockSpec(memory_space=pl.ANY)] * (len(arrays) + len(held)),
+            out_specs=held_spec + [a_spec, a_spec, b_spec, b_spec],
+            scratch_shapes=[
+                pltpu.VMEM((width, units), jnp.bfloat16),
+                pltpu.VMEM((width, units), jnp.bfloat16),
+                pltpu.VMEM((units, width), jnp.bfloat16),
+                pltpu.SemaphoreType.DMA((len(arrays),)),
+            ],
+        ),
+        out_shape=[jax.ShapeDtypeStruct(s, jnp.bfloat16) for s in held_shapes]
+        + [jax.ShapeDtypeStruct((rows, width), jnp.bfloat16)] * 4,
+        input_output_aliases={5 + len(arrays) + i: i for i in range(len(held))},
+        compiler_params=pltpu.CompilerParams(vmem_limit_bytes=56 * 2**20),
+        cost_estimate=pl.CostEstimate(
+            flops=28 * rows * units * width, bytes_accessed=40 * 2**20, transcendentals=2 * rows * units
+        ),
+        name="ffn",
+    )(places, n2[0], gy[0], n2[1], gy[1], *arrays, *held)
+    return out[:5], [out[5], out[7]], [out[6], out[8]]
+
+
+def blank(shape, dtype):
+    return pl.pallas_call(
+        lambda ref: None,
+        out_shape=jax.ShapeDtypeStruct(shape, dtype),
+        out_specs=pl.BlockSpec(memory_space=pl.ANY),
+        name="blank",
+    )()
+
+
+def tie(v, *after):
+    return lax.optimization_barrier((v, *after))[0] if after else v
+
+
+def place_kernel(splits, at_ref, low_ref, high_ref, *outs):
+    first = pl.program_id(0) < pl.num_programs(0) // 2
+    piece = jnp.where(first, low_ref[0], high_ref[0]).astype(jnp.float32)
+    col = 0
+    for out, width in zip(outs, splits, strict=True):
+        out[...] = piece[:, col : col + width]
+        col += width
+
+
+def place_rows(at, first, second, splits):
+    count, rows, cols = first.shape
+    if rows % 8:
+        outs = []
+        col = 0
+        for width in splits:
+            out = blank((2 * count * rows, width), jnp.float32)
+            for i in range(2 * count):
+                piece = (first if i < count else second)[i % count, :, col : col + width]
+                out = lax.dynamic_update_slice(out, piece.astype(jnp.float32), (at[i] * rows, 0))
+            outs.append(out)
+            col += width
+        return outs
+    return pl.pallas_call(
+        functools.partial(place_kernel, splits),
+        grid_spec=pltpu.PrefetchScalarGridSpec(
+            num_scalar_prefetch=1,
+            grid=(2 * count,),
+            in_specs=[
+                pl.BlockSpec((1, rows, cols), lambda t, at: (jnp.minimum(t, count - 1), 0, 0)),
+                pl.BlockSpec((1, rows, cols), lambda t, at: (jnp.maximum(t - count, 0), 0, 0)),
+            ],
+            out_specs=[pl.BlockSpec((rows, width), lambda t, at: (at[t], 0)) for width in splits],
+        ),
+        out_shape=[jax.ShapeDtypeStruct((2 * count * rows, width), jnp.float32) for width in splits],
+        cost_estimate=pl.CostEstimate(flops=0, bytes_accessed=12 * count * rows * cols, transcendentals=0),
+        name="place",
+    )(at, first, second)
+
+
+class Order:
+    def __init__(self):
+        self.last = ()
+
+    def after(self, *vals):
+        out = lax.optimization_barrier((*vals, *self.last))[: len(vals)] if self.last else vals
+        return out[0] if len(vals) == 1 else out
+
+    def did(self, *vals):
+        self.last = vals
+
+
+class Chain:
+    def __init__(self, order, steps):
+        self.order, self.steps, self.result = order, steps, None
+        self.running = True
+        self.resume(None)
+
+    def resume(self, taken):
+        try:
+            self.arriving, sent = self.steps.send(taken)
+            self.order.did(*sent)
+        except StopIteration as end:
+            self.running, self.result = False, end.value
+            self.order.did(*jax.tree.leaves(end.value))
+
+    def step(self):
+        if self.running:
+            taken = self.order.after(*self.arriving)
+            self.resume(list(taken) if len(self.arriving) > 1 else [taken])
+
+    def finish(self):
+        while self.running:
+            self.step()
+        return self.result
+
+
 class Plan:
     def __init__(self, mesh):
         self.shards = mesh.shape["shard"]
@@ -224,30 +421,95 @@
     def swap(self, v, bit):
         return lax.ppermute(v, "shard", [(i, i ^ bit) for i in range(self.shards)])
 
+    def swap_ctx(self, v, bit):
+        return lax.ppermute(v, "ctx", [(i, i ^ bit) for i in range(self.ctxs)])
+
+    def go_right(self, v):
+        return lax.ppermute(v, "ctx", self.right)
+
+    def go_left(self, v):
+        return lax.ppermute(v, "ctx", self.left)
+
     def my_bit(self, bit):
         return (lax.axis_index("shard") // bit) % 2
 
-    def gather_xor(self, v):
+    def lay_rows(self, pieces):
+        me = lax.axis_index("shard")
+        rows, cols = pieces[0].shape
+        out = blank((self.shards * rows, cols), pieces[0].dtype)
+        for j, piece in enumerate(pieces):
+            out = lax.dynamic_update_slice(out, piece, ((me ^ j) * rows, 0))
+        return out
+
+    def near(self, v, first=0):
         pieces = {0: v}
-        for bit in reversed(self.bits):
+        for bit in reversed(self.bits[:-1]):
             pieces |= {j | bit: self.swap(p, bit) for j, p in pieces.items()}
-        return [pieces[j] for j in range(self.shards)]
-
-    def scatter_xor(self, pieces):
+        return [pieces[j] for j in range(self.bits[-1])]
+
+    def gather_near(self, v):
+        _, *others = self.near(v)
+        return [v, *(yield others, [v])]
+
+    def gather_far(self, v):
+        [got] = yield [self.swap(v, self.bits[-1])], [v]
+        _, *others = self.near(got)
+        return [got, *(yield others, [got])]
+
+    def gather_far_halved(self, v):
+        half = v.shape[0] // 2
+        y = lax.axis_index("ctx") % 2
+        give = lax.dynamic_slice_in_dim(v, y * half, half, 0)
+        [mine] = yield [self.swap(give, self.bits[-1])], [give]
+        [other] = yield [self.swap_ctx(mine, 1)], [mine]
+        whole = blank(v.shape, v.dtype)
+        whole = lax.dynamic_update_slice(whole, mine, (y * half, 0))
+        whole = lax.dynamic_update_slice(whole, other, ((1 - y) * half, 0))
+        _, *others = self.near(whole)
+        return [whole, *(yield others, [whole])]
+
+    def gate_up_columns(self, w):
+        n = self.shards
+        rows, units = w.shape[0], FF // n
+        me = lax.axis_index("shard")
+
+        def block(shard, row, count):
+            return [lax.dynamic_slice(w, (row, base + shard * units), (count, units)) for base in (0, FF)]
+
+        own = block(me, 0, rows)
+        pieces = [(own, me * rows)]
+        if n == 4 and self.ctxs % 4 == 0:
+            y, z = lax.axis_index("ctx") % 2, (lax.axis_index("ctx") // 2) % 2
+            half = rows // 2
+            pairs = [(c * n + s, c * n + (s ^ 2 ^ (c % 2))) for c in range(self.ctxs) for s in range(n)]
+            give = block(me ^ 2 ^ y, z * half, half)
+            got = [lax.ppermute(b, ("ctx", "shard"), pairs) for b in give]
+            got = yield got, give
+            mine, theirs = (me ^ 2 ^ y) * rows, (me ^ 2 ^ (1 - y)) * rows
+            at, far = z * half, (1 - z) * half
+            second = [self.swap_ctx(got[0], 1), self.swap_ctx(got[1], 2)]
+            near_give = block(me ^ 1, 0, rows)
+            near = [self.swap(b, 1) for b in near_give]
+            g_y, u_z = yield second, [*got, *near_give]
+            third = [self.swap_ctx(got[0], 2), self.swap_ctx(g_y, 2), self.swap_ctx(got[1], 1), self.swap_ctx(u_z, 1)]
+            near = yield near, [g_y, u_z]
+            g_z, g_yz, u_y, u_zy = yield third, near
+            gate = [(own[0], me * rows), (near[0], (me ^ 1) * rows), (got[0], mine + at), (g_y, theirs + at)]
+            gate += [(g_z, mine + far), (g_yz, theirs + far)]
+            up = [(own[1], me * rows), (near[1], (me ^ 1) * rows), (got[1], mine + at), (u_z, mine + far)]
+            up += [(u_y, theirs + at), (u_zy, theirs + far)]
+            return gate, up
+        for j in range(1, n):
+            pieces.append(([self.swap(b, j) for b in block(me ^ j, 0, rows)], (me ^ j) * rows))
+        return [[(pair[i], at) for pair, at in pieces] for i in range(2)]
+
+    def scatter(self, pieces):
         pieces = dict(enumerate(pieces))
         for bit in self.bits:
-            got = {j ^ bit: self.swap(pieces[j], bit) for j in sorted(pieces, reverse=True) if j & bit}
-            pieces = {j: add_low(pieces[j], got[j]) for j in got}
+            give = {j: p for j, p in pieces.items() if j & bit}
+            got = yield [self.swap(p, bit) for p in give.values()], list(give.values())
+            pieces = {j ^ bit: add_low(pieces[j ^ bit], g) for j, g in zip(give, got, strict=True)}
         return pieces[0]
-
-    def gather_rows(self, v):
-        out = v[None]
-        for bit in reversed(self.bits):
-            other = self.swap(out, bit)
-            first = self.my_bit(bit) == 0
-            out = jnp.stack([jnp.where(first, out, other), jnp.where(first, other, out)], axis=1)
-            out = out.reshape(-1, *v.shape)
-        return out.reshape(-1, *v.shape[1:])
 
     def scatter_rows(self, v, add=add_low):
         cur = v.reshape(self.shards, v.shape[0] // self.shards, *v.shape[1:])
@@ -256,80 +518,142 @@
             mine = self.my_bit(bit)
             keep = lax.dynamic_index_in_dim(pairs, mine, 1, False)
             give = lax.dynamic_index_in_dim(pairs, 1 - mine, 1, False)
-            cur = add(keep, self.swap(give, bit))
+            [got] = yield [self.swap(give, bit)], [give]
+            cur = add(keep, got)
         return cur[0]
-
-    def exchange_columns(self, v, blocks):
-        me = lax.axis_index("shard")
-        own = blocks(me)
-        out = jnp.zeros((self.shards, *own.shape), own.dtype)
-        out = lax.dynamic_update_index_in_dim(out, own, me, 0)
-        for j in range(1, self.shards):
-            other = me ^ j
-            out = lax.dynamic_update_index_in_dim(out, self.swap(blocks(other), j), other, 0)
-        return out
 
     def ring_gather(self, v):
         n = self.ctxs
         pieces = {0: v}
-        a = b = v
+        a, b = v, v
         for step in range(1, n // 2 + 1):
-            a = lax.ppermute(a, "ctx", self.right)
-            pieces[step] = a
-            if n - step > n // 2:
-                b = lax.ppermute(b, "ctx", self.left)
-                pieces[n - step] = b
+            both = n - step > n // 2
+            got = yield [self.go_right(a)] + ([self.go_left(b)] if both else []), [a, b] if both else [a]
+            pieces[step] = a = got[0]
+            if both:
+                pieces[n - step] = b = got[1]
         return jnp.stack([pieces[k] for k in range(n)])
 
     def ring_scatter(self, v):
         n = self.ctxs
-        a, b = v[n // 2], v[n // 2 - 1]
-        for step in range(n // 2 + 1, n + 1):
-            a = lax.ppermute(a, "ctx", self.right)
-            a = add_low(a, v[step % n])
-        for step in range(n // 2 - 2, -1, -1):
-            b = lax.ppermute(b, "ctx", self.left)
-            if step:
-                b = add_low(b, v[step])
-        return a.astype(jnp.float32) + b.astype(jnp.float32)
-
-    def ring_sum(self, v):
+        m = n // 2
+        a, b = v[m], v[m - 1]
+        for step in range(1, m):
+            a, b = yield [self.go_right(a), self.go_left(b)], [a, b]
+            a = add_low(a, v[m + step])
+            if step < m - 1:
+                b = add_low(b, v[m - 1 - step])
+        [a] = yield [self.go_right(a)], [a]
+        return v[0].astype(jnp.float32) + a.astype(jnp.float32) + b.astype(jnp.float32)
+
+    def halve(self, v, axis, order):
+        top = self.ctxs.bit_length() - 1
+        left = [1 << b for b in reversed(range(top))]
+        cur = v.reshape(*v.shape[:axis], *([2] * top), *v.shape[axis + 1 :])
+        for bit in order:
+            at = axis + left.index(bit)
+            left.remove(bit)
+            mine = (lax.axis_index("ctx") // bit) % 2
+            give = lax.dynamic_index_in_dim(cur, 1 - mine, at, False)
+            keep = lax.dynamic_index_in_dim(cur, mine, at, False)
+            [got] = yield [self.swap_ctx(give, bit)], [give]
+            cur = add_low(keep, got)
+        return cur
+
+    def double(self, v, order):
+        cur, ids = v[None], [0]
+        for bit in reversed(order):
+            [other] = yield [self.swap_ctx(cur, bit)], [cur]
+            ids += [k ^ bit for k in ids]
+            if len(ids) < self.ctxs:
+                cur = jnp.concatenate([cur, other])
+        return cur, other, lax.axis_index("ctx") ^ jnp.array(ids, jnp.int32)
+
+    def order(self, first):
+        bits = [1 << b for b in range(self.ctxs.bit_length() - 1)]
+        return [first] + [b for b in bits if b != first]
+
+    def ring_reduce(self, own, axis):
+        m = self.ctxs // 2
+        far = own(m)
+        cut = far.shape[axis] // 2
+        head = functools.partial(lax.slice_in_dim, start_index=0, limit_index=cut, axis=axis)
+        tail = functools.partial(lax.slice_in_dim, start_index=cut, limit_index=None, axis=axis)
+        a, b = head(far), tail(far)
+        for k in range(m - 1, -1, -1):
+            a, b = yield [self.go_right(a), self.go_left(b)], [a, b]
+            at_a, at_b = own(k), own(-k)
+            if k == 0:
+                total = at_a.astype(jnp.float32) + a.astype(jnp.float32) + b.astype(jnp.float32)
+            elif k == m - 1:
+                a = jnp.concatenate([add_low(a, head(at_a)), tail(at_a)], axis)
+                b = jnp.concatenate([head(at_b), add_low(b, tail(at_b))], axis)
+            else:
+                a, b = add_low(a, at_a), add_low(b, at_b)
+        return total.astype(jnp.bfloat16)
+
+    def ring_spread(self, out, chunk, col):
+        m = self.ctxs // 2
+        place = self.my_place()
+        cut = chunk.shape[1] // 2
+
+        def put(piece, k, col):
+            at = lax.rem(place + k + 2 * m, 2 * m) * piece.shape[0]
+            out[0] = lax.dynamic_update_slice(out[0], piece.astype(jnp.float32), (at, col))
+
+        put(chunk, 0, col)
+        a = b = chunk
+        for k in range(1, m + 1):
+            if k == m:
+                a, b = a[:, :cut], b[:, cut:]
+            a, b = yield [self.go_right(a), self.go_left(b)], [a, b]
+            put(a, -k, col)
+            put(b, k, col + cut if k == m else col)
+
+    def own_chunk(self, chunks, axis):
+        place = self.my_place()
         n = self.ctxs
+        return lambda k: lax.dynamic_index_in_dim(chunks, lax.rem(place + k + n, n), axis, False)
+
+    def sum_rows(self, v, out):
         rows, cols = v.shape
-        cut = cols // 2
-        place = self.my_place()
-        chunks = v.reshape(n, rows // n, cols)
-
-        def part(k, way):
-            at = chunks[:, :, :cut] if way > 0 else chunks[:, :, cut:]
-            return lax.dynamic_index_in_dim(at, lax.rem(place - way * k + 2 * n, n), 0, False)
-
-        a, b = part(1, 1), part(1, -1)
-        for step in range(2, n + 1):
-            a = add_low(lax.ppermute(a, "ctx", self.right), part(step, 1))
-            b = add_low(lax.ppermute(b, "ctx", self.left), part(step, -1))
-        out = jnp.zeros(chunks.shape, jnp.float32)
-
-        def put(out, piece, k, way):
-            at = lax.rem(place - way * k + 2 * n, n)
-            return lax.dynamic_update_slice(
-                out, piece.astype(jnp.float32)[None], (at, 0, 0 if way > 0 else cut)
-            )
-
-        out = put(put(out, a, 0, 1), b, 0, -1)
-        for step in range(1, n):
-            a = lax.ppermute(a, "ctx", self.right)
-            b = lax.ppermute(b, "ctx", self.left)
-            out = put(put(out, a, step, 1), b, step, -1)
-        return out.reshape(rows, cols)
+        chunks = v.reshape(self.ctxs, rows // self.ctxs, cols)
+        mine = yield from self.ring_reduce(self.own_chunk(chunks, 0), 1)
+        yield from self.ring_spread(out, mine, 0)
+        return out[0]
+
+    def sum_over_all(self, v, out):
+        mine = yield from self.scatter_rows(v)
+        return (yield from self.sum_rows(mine, out))
+
+    def sum_small_over_all(self, v):
+        mine = yield from self.scatter_rows(v)
+        rows, cols = mine.shape
+        order = self.order(1)
+        mine = yield from self.halve(mine.reshape(self.ctxs, rows // self.ctxs, cols), 0, order)
+        low_half, high_half, at = yield from self.double(mine, order)
+        return place_rows(at, low_half, high_half, [cols])[0]
+
+    def sum_columns(self, part, out, col):
+        n, c = self.shards, self.ctxs
+        me = lax.axis_index("shard")
+        rows, units = part.shape[0] // n // c, part.shape[1]
+        mine = yield from self.ring_reduce(self.own_chunk(part.reshape(n, c, rows, units), 1), 0)
+        got = [lax.dynamic_index_in_dim(mine, me ^ j, 0, False) for j in range(n)]
+        others = yield [self.swap(g, j) for j, g in enumerate(got) if j], got[1:]
+        whole = blank((rows, n * units), jnp.bfloat16)
+        for j, g in enumerate([got[0], *others]):
+            whole = lax.dynamic_update_slice(whole, g, (0, (me ^ j) * units))
+        yield from self.ring_spread(out, whole, col)
+        return out[0]
 
     def small_sum(self, v):
-        mine = self.scatter_rows(v, lambda a, b: a + b)
-        bit = 1
-        while bit < self.ctxs:
-            mine = mine + lax.ppermute(mine, "ctx", [(c, c ^ bit) for c in range(self.ctxs)])
-            bit *= 2
-        return mine
+        cur = yield from self.scatter_rows(v, lambda a, b: a + b)
+        cur = cur[0] if cur.ndim == v.ndim else cur
+        for bit in self.order(1):
+            [got] = yield [self.swap_ctx(cur, bit)], [cur]
+            cur = cur + got
+        return cur
 
 
 def body(plan, tokens, segments, assign, w_qkv, w_out, w_gate_up, w_down, gain_attn, gain_ffn, cotangent):
@@ -337,7 +661,6 @@
     rows = seqs * rows_dev
     blocks = assign.shape[0]
     n = plan.shards
-    ffn = FF // n
     low = jnp.bfloat16
     ids = jnp.arange(blocks, dtype=jnp.int32)
     my_blocks = lax.dynamic_slice_in_dim(assign, 2 * lax.axis_index("ctx"), 2, 0)
@@ -352,80 +675,132 @@
     scalars = (my_blocks, lowest, slot_of, half_of)
     seg = segments.astype(jnp.float32).reshape(seqs, blocks, 1, BLK)
 
-    gains = plan.gather_rows(jnp.stack([gain_attn, gain_ffn], 1)).astype(jnp.float32)
-    gain_one, gain_two = gains[:, 0], gains[:, 1]
-    w_kv = plan.gather_rows(w_qkv[:, QW:])
-    w_q = plan.gather_rows(w_qkv[:, :QW])
-    w_o = plan.gather_rows(w_out)
-
-    def gu_block(t):
-        g = lax.dynamic_slice_in_dim(w_gate_up, t * ffn, ffn, 1)
-        u = lax.dynamic_slice_in_dim(w_gate_up, FF + t * ffn, ffn, 1)
-        return jnp.concatenate([g, u], axis=1)
-
-    w_gu = plan.exchange_columns(w_gate_up, gu_block).reshape(width, 2 * ffn)
-
+    order = Order()
+    chains = {}
+
+    def chain(steps, name=None):
+        chains[name] = Chain(order, steps)
+        return chains[name]
+
+    def take(names):
+        for name in names.split():
+            chains[name].step()
+
+    lanes = jnp.zeros((gain_attn.shape[0], HD - 2), low)
+    first = jnp.concatenate([w_qkv[:, QW:], gain_attn[:, None], gain_ffn[:, None], lanes], axis=1)
+    first_far, first_near = chain(plan.gather_far(first)), chain(plan.gather_near(first))
     tok = tokens.reshape(rows, width).astype(jnp.float32)
     scale_one = inv_rms(tok)
     hat_one = tok * scale_one
+    first_far.step()
+    q_rows = order.after(w_qkv[:, :QW])
+    q_far, q_near = chain(plan.gather_far_halved(q_rows)), chain(plan.gather_near(q_rows))
+    packed = plan.lay_rows(first_near.finish() + first_far.finish())
+    w_kv = packed[:, : 2 * HD]
+    gain_one, gain_two = (packed[:, 2 * HD + i].astype(jnp.float32) for i in range(2))
     normed_one = (hat_one * gain_one).astype(low)
     key_value = dot_f32(normed_one, w_kv).astype(low).reshape(seqs, 2, BLK, 2 * HD)
-    kv_all = plan.ring_gather(key_value)
+    kv = chain(plan.ring_gather(key_value))
+    o_rows = order.after(w_out)
+    o_far, o_near = chain(plan.gather_far_halved(o_rows)), chain(plan.gather_near(o_rows))
+    q_far.step()
+    kv.step()
+    gu = chain(plan.gate_up_columns(order.after(w_gate_up)))
+    kv.step()
+    q_far.step()
+    o_far.step()
+    kv.step()
+    kv_all = kv.finish()
+    o_far.step()
+    gu.step()
+    grad_low = cotangent.reshape(rows, width)
+    gy_rows = order.after(grad_low)
+    gy_far, gy_near = chain(plan.gather_far(gy_rows)), chain(plan.gather_near(gy_rows))
+    w_q = plan.lay_rows(q_near.finish() + q_far.finish())
     queries = dot_f32(normed_one, w_q).astype(low).reshape(seqs, rows_dev, QW)
     mixed, lse = attend(scalars, queries, kv_all, seg)
+    order.did(mixed)
+    gu.step()
+    w_o = plan.lay_rows(o_near.finish() + o_far.finish())
     mixed_low = mixed.reshape(rows, QW)
     hidden = tok + dot_f32(mixed_low, w_o)
     scale_two = inv_rms(hidden)
     hat_two = hidden * scale_two
     normed_two = (hat_two * gain_two).astype(low)
-
-    grad_low = cotangent.reshape(rows, width)
-    n2 = jnp.concatenate(plan.gather_xor(normed_two))
-    gy = jnp.concatenate(plan.gather_xor(grad_low))
-    gate_up = dot_f32(n2, w_gu)
-    d_act = dot_f32(gy, w_down, ((1,), (1,)))
-
-    def gelu_product(gate_in, up_in):
-        return jax.nn.gelu(gate_in, approximate=True) * up_in
-
-    act, pull = jax.vjp(gelu_product, gate_up[:, :ffn], gate_up[:, ffn:])
-    act = act.astype(low)
-    d_gu = jnp.concatenate(pull(d_act), axis=1).astype(low)
-    grad_down = plan.ring_sum(dot_f32(act, gy, ((0,), (0,))).astype(low))
-    d_n2 = dot_f32(d_gu, w_gu, ((1,), (1,))).astype(low)
-    d_normed_two = plan.scatter_xor([d_n2[j * rows : (j + 1) * rows] for j in range(n)]).astype(jnp.float32)
-    part_gu = dot_f32(n2, d_gu, ((0,), (0,))).astype(low)
-    me = lax.axis_index("shard")
-    own_gu = plan.exchange_columns(
-        part_gu, lambda t: lax.dynamic_slice_in_dim(part_gu, t * (width // n), width // n, 0)
-    )
-    summed = plan.ring_sum(own_gu.reshape(n * (width // n), 2 * ffn))
-    summed = summed.reshape(n, width // n, 2, ffn)
-    grad_gate_up = jnp.moveaxis(summed, 0, 2).reshape(width // n, 2 * FF)
-    down = dot_f32(act, w_down).astype(low)
-    branch = plan.scatter_xor([down[j * rows : (j + 1) * rows] for j in range(n)]).astype(jnp.float32)
-    output = (hidden + branch).reshape(seqs, rows_dev, width)
-
-    grad_gain_ffn = plan.small_sum(jnp.sum(d_normed_two * hat_two, axis=0))
+    order.did(normed_two)
+    n2_far, n2_near = chain(plan.gather_far(normed_two)), chain(plan.gather_near(normed_two))
+    gy_far.step()
+    w_gate, w_up = gu.finish()
+
+    held, d_n2, down = (), [], []
+
+    def feed_forward(n2, gy):
+        nonlocal held, d_n2, down
+        for p in range(0, len(n2), 2):
+            at = len(d_n2) // 2
+            held, d_n2_pair, down_pair = ffn(at, n, n2[p : p + 2], gy[p : p + 2], w_gate, w_up, w_down, held)
+            d_n2, down = d_n2 + d_n2_pair, down + down_pair
+        order.did(*d_n2)
+
+    feed_forward(n2_near.finish(), gy_near.finish())
+    n2_far.step()
+    feed_forward(n2_far.finish(), gy_far.finish())
+    act, d_gate, d_up, n2_all, gy_all = (v.reshape(n * rows, -1) for v in held)
+
+    def grad(left, right):
+        part = dot_f32(order.after(left), right, ((0,), (0,))).astype(low)
+        order.did(part)
+        return part
+
+    def blank_like(w):
+        return [blank(w.shape, jnp.float32)]
+
+    chain(plan.scatter(d_n2), "T")
+    chain(plan.sum_rows(grad(act, gy_all), blank_like(w_down)), "D")
+    take("T")
+    out_gate_up = blank_like(w_gate_up)
+    chain(plan.sum_columns(grad(n2_all, d_gate), out_gate_up, 0), "G")
+    take("D")
+    chain(plan.sum_columns(grad(n2_all, d_up), out_gate_up, FF), "U")
+    take("G D U")
+    d_normed_two = chains["T"].finish().astype(jnp.float32)
     e = d_normed_two * gain_two
     d_hidden = grad_low.astype(jnp.float32) + scale_two * (
         e - hat_two * jnp.mean(e * hat_two, axis=-1, keepdims=True)
     )
     d_branch = d_hidden.astype(low)
-    d_mixed = dot_f32(d_branch, w_o, ((1,), (1,))).astype(low).reshape(seqs, rows_dev, QW)
-    dq, dkv = attend_back(scalars, queries, d_mixed, mixed, kv_all, seg, lse)
-    dkv_own = plan.ring_scatter(dkv)
-    d_qkv = jnp.concatenate([dq.reshape(rows, QW), dkv_own.astype(low).reshape(rows, 2 * HD)], axis=1)
-    part_out = plan.scatter_rows(dot_f32(mixed_low, d_branch, ((0,), (0,))).astype(low))
-    grad_out = plan.ring_sum(part_out)
-    part_qkv = plan.scatter_rows(dot_f32(normed_one, d_qkv, ((0,), (0,))).astype(low))
-    grad_qkv = plan.ring_sum(part_qkv)
-    d_normed_one = dot_f32(dq.reshape(rows, QW), w_q, ((1,), (1,))) + dot_f32(
-        d_qkv[:, QW:], w_kv, ((1,), (1,))
-    )
-    grad_gain_attn = plan.small_sum(jnp.sum(d_normed_one * hat_one, axis=0))
+    order.did(d_branch)
+    chain(plan.scatter(order.after(*down)), "B")
+    d_mixed = dot_f32(order.after(d_branch), w_o, ((1,), (1,))).astype(low).reshape(seqs, rows_dev, QW)
+    order.did(d_mixed)
+    take("G B D U")
+    dq, dkv = attend_back(scalars, queries, order.after(d_mixed), mixed, kv_all, seg, lse)
+    order.did(dq, dkv)
+    chain(plan.ring_scatter(dkv), "K")
+    dq = dq.reshape(rows, QW)
+    take("D U G")
+    chain(plan.sum_over_all(grad(mixed_low, d_branch), blank_like(w_out)), "O")
+    out_qkv = blank_like(w_qkv)
+    chain(plan.sum_over_all(grad(normed_one, dq), out_qkv), "Q")
+    branch = chains["B"].finish().astype(jnp.float32)
+    output = (hidden + branch).reshape(seqs, rows_dev, width)
+    take("O Q K D U G K D")
+    dkv_low = chains["K"].finish().astype(low).reshape(rows, 2 * HD)
+    chain(plan.sum_small_over_all(grad(normed_one, dkv_low)), "V")
+    take("U V D G")
+    d_normed_one = dot_f32(dq, w_q, ((1,), (1,))) + dot_f32(order.after(dkv_low), w_kv, ((1,), (1,)))
+    gains = jnp.stack([jnp.sum(d_normed_one * hat_one, axis=0), jnp.sum(d_normed_two * hat_two, axis=0)])
+    chain(plan.small_sum(jnp.moveaxis(gains.reshape(2, n, width // n), 0, 1)), "S")
     f = d_normed_one * gain_one
     input_grad = d_hidden + scale_one * (f - hat_one * jnp.mean(f * hat_one, axis=-1, keepdims=True))
+    take("U D Q U V Q O G V S Q U V O S Q V U Q V O Q V O Q V O Q G O Q S O G S O G S O G O")
+    sums = [chains[name] for name in "DGUOQVS"]
+    while any(c.running for c in sums):
+        for c in sums:
+            c.step()
+    grad_down, grad_out, grad_gate_up = chains["D"].result, chains["O"].result, out_gate_up[0]
+    grad_qkv = lax.dynamic_update_slice(out_qkv[0], chains["V"].result, (0, QW))
+    grad_gain_attn, grad_gain_ffn = chains["S"].result
     return (
         output,
         input_grad.reshape(seqs, rows_dev, width),

time: 1010 us -> 663 us (0.66)
  waiting for transfers between devices: 422 us -> 175 us
  local copies, waits for them, and re-layouts: 125 us -> 41.5 us
  matrix products: 135 us -> 55.7 us
  Pallas kernels: 27.2 us -> 104 us
  other arithmetic: 112 us -> 93.3 us
    ppermute x34 -> x37, waiting for transfers between devices: 156 us -> 21.1 us  [swap(): return lax.ppermute(v, 'shard', [(i, i ^ bit) for i in range(self.shards)])]
    ppermute x132 -> x113, waiting for transfers between devices: 265 us -> 154 us  [the longest x48 93.5 us: go_right(): return lax.ppermute(v, 'ctx', self.right)]
    pallas_call x0 -> x14, Pallas kernels: none -> 82 us  [the longest x2 77 us: ffn(): pl.pallas_call(functools.partial(ffn_kernel, (len(gate), len(up), 1)), gr...]
    dot_general x14 -> x12, matrix products: 135 us -> 55.7 us  [dot_f32(): lax.dot_general(left, right, (dims, ((), ())), preferred_element_type=jnp...]
    another operation x6 -> x4, local copies, waits for them, and re-layouts: 25 us -> 1.29 us  [the longest x1 0.67 us: ffn(): places = jnp.stack([jnp.asarray(at, jnp.int32) for _, at in parts])]
    transpose x1 -> x0, local copies, waits for them, and re-layouts: 22 us -> none  [body(): grad_gate_up = jnp.moveaxis(summed, 0, 2).reshape(width // n, 2 * FF)]
    unnamed x151 -> x170, local copies, waits for them, and re-layouts: 28.1 us -> 7.54 us
    broadcast_in_dim x6 -> x3, local copies, waits for them, and re-layouts: 13.4 us -> 1.69 us  [the longest x1 0.89 us: body(): gain_ffn[:, None]]
  transfers between devices with their start and end apart: 166 -> 150, of which waited for: 97 -> 56; matrix products, arithmetic and copies ran while one was open for 31% -> 27% of each run, Pallas kernels for 3% -> 16%
where the time goes in v2:
time: 663 us; the launch traced here: 658 us
  starting transfers between devices  178 us (27%)
  waiting for transfers between devices  175 us (26%)
  Pallas kernels  104 us (16%)
  other arithmetic  93.3 us (14%)
  matrix products  55.7 us (8%)
  local copies, waits for them, and re-layouts  41.5 us (6%)
  between operations  10.5 us (2%)
    ppermute x48, waiting for transfers between devices, go_right(): return lax.ppermute(v, 'ctx', self.right)  93.5 us
    pallas_call x2, Pallas kernels, ffn(): pl.pallas_call(functools.partial(ffn_kernel, (len(gate), len(up), 1)), gr...  77 us
    ppermute x48, starting transfers between devices, go_right(): return lax.ppermute(v, 'ctx', self.right)  75.9 us
    dot_general x12, matrix products, dot_f32(): lax.dot_general(left, right, (dims, ((), ())), preferred_element_type=jnp...  55.7 us
    dynamic_update_slice x45, other arithmetic, put(): lax.dynamic_update_slice(out[0], piece.astype(jnp.float32), (at, col))  44.4 us
    ppermute x46, starting transfers between devices, go_left(): return lax.ppermute(v, 'ctx', self.left)  44.3 us
    ppermute x46, waiting for transfers between devices, go_left(): return lax.ppermute(v, 'ctx', self.left)  40 us
    ppermute x37, starting transfers between devices, swap(): return lax.ppermute(v, 'shard', [(i, i ^ bit) for i in range(self.shards)])  28.8 us
  transfers between devices with their start and end apart: 150, of which 56 were waited for; matrix products, arithmetic and copies ran while one was open for 27% of the time, Pallas kernels for 16%

profile of v2, /device:TPU:0, one launch (start us, length us, event | category | flops | bytes accessed | tf_op | source)
XLA Modules:
  0.0 657.8 jit_solution(1426656110157631976)
XLA Ops:
  38.3 12.8 %collective-permute-done.11 = bf16[2,2,128,256]{3,2,1,0:T(8,128)(2,1)S(1)} collective-permute-done((bf16[2,2,128,256]{3,2,1,0:T(8,128)(2,1)S(1)}, bf16[2,2,128,256]{3,2,1,0:T(8,128)(2,1)S(1)}, u32[]{:S(2)}, u32[]{:S(2)}) %collective-permute-start.11) | collective-permute-done | bytes 262176 | tf_op jit(solution)/shard_map/ppermute | solution.py:428
  61.4 14.5 %collective-permute-done.16 = bf16[2,2,128,256]{3,2,1,0:T(8,128)(2,1)S(1)} collective-permute-done((bf16[2,2,128,256]{3,2,1,0:T(8,128)(2,1)S(1)}, bf16[2,2,128,256]{3,2,1,0:T(8,128)(2,1)S(1)}, u32[]{:S(2)}, u32[]{:S(2)}) %collective-permute-start.16) | collective-permute-done | bytes 262176 | tf_op jit(solution)/shard_map/ppermute | solution.py:428
  81.6 7.7 %attend.1 = (bf16[2,256,1536]{2,1,0:T(8,128)(2,1)S(1)}, f32[2,2,1,1536]{3,2,1,0:T(1,128)S(1)}) custom-call(s32[2]{0:T(128)S(1)} %get-tuple-element.408.blk_ref, s32[4]{0:T(128)S(1)} %maximum_maximum_fusion.1.low_ref, s32[16]{0:T(128)S(1)} %get-tuple-element.395.slot_ref, s32[16]{0:T(128)S(1)} %get-tuple-element.394.half_ref, ...), custom_call_target="tpu_custom_call" | custom-call | flops 7000000000 | bytes 8388608 | tf_op jit(solution)/shard_map/attend/pallas_call | solution.py:159
  107.6 7.1 %collective-permute-start.26 = (bf16[192,1152]{1,0:T(8,128)(2,1)}, bf16[192,1152]{1,0:T(8,128)(2,1)S(1)}, u32[]{:S(2)}, u32[]{:S(2)}) collective-permute-start(bf16[192,1152]{1,0:T(8,128)(2,1)} %collective-permute-done.7.refs_2_), channel_id=1, source_target_pairs={{0,8},{4,12},{8,0},{12,4},{16,24},{20,28},{24,16},{28,20},{1,9},{5... | collective-permute-start | bytes 1327112 | tf_op jit(solution)/shard_map/ppermute | solution.py:425
  114.7 5.3 collective-permute-start.28
  120.0 5.3 collective-permute-done.26.refs_4_
  132.3 5.0 collective-permute-done.27.refs_5_
  138.6 38.4 %ffn.2 = (bf16[4,512,1152]{2,1,0:T(8,128)(2,1)}, bf16[4,512,1152]{2,1,0:T(8,128)(2,1)}, bf16[4,512,1152]{2,1,0:T(8,128)(2,1)}, bf16[4,512,1536]{2,1,0:T(8,128)(2...) custom-call(s32[13]{0:T(128)} %stack.93.at_ref, ...), custom_call_target="tpu_custom_call" | custom-call | flops 25367150592 | bytes 41943040 | tf_op jit(solution)/shard_map/ffn/pallas_call | solution.py:289
  184.6 38.6 %ffn.3 = (bf16[4,512,1152]{2,1,0:T(8,128)(2,1)}, bf16[4,512,1152]{2,1,0:T(8,128)(2,1)}, bf16[4,512,1152]{2,1,0:T(8,128)(2,1)}, bf16[4,512,1536]{2,1,0:T(8,128)(2...) custom-call(s32[13]{0:T(128)} %stack.93.at_ref, ...), custom_call_target="tpu_custom_call", output_to_operand_aliasing={{0}: (18, {}), {1}: (19, {}), {2}: (20, {}), {3}: (21, {}),... | custom-call | flops 25367150592 | bytes 41943040 | tf_op jit(solution)/shard_map/ffn/pallas_call | solution.py:289
  223.7 11.3 %convolution_convert_fusion.4 = bf16[1152,1536]{1,0:T(8,128)(2,1)S(1)} fusion(bf16[2048,1152]{1,0:T(8,128)(2,1)} %bitcast.427, bf16[2048,1536]{1,0:T(8,128)(2,1)} %bitcast.426), kind=kOutput, calls=%fused_computation.4 | convolution fusion | flops 7249526784 | bytes 14548992 | tf_op jit(solution)/shard_map/dot_general | solution.py:27
  235.2 5.3 collective-permute-start.37
  243.5 9.1 %convolution_convert_fusion.3 = bf16[1536,1152]{1,0:T(8,128)(2,1)S(1)} fusion(bf16[2048,1536]{1,0:T(8,128)(2,1)S(1)} %bitcast.424, bf16[2048,1152]{1,0:T(8,128)(2,1)S(1)} %bitcast.430), kind=kOutput, calls=%fused_computation.3 | convolution fusion | flops 7249526784 | bytes 14548992 | tf_op jit(solution)/shard_map/dot_general | solution.py:27
  258.1 11.1 %convolution_convert_fusion.2 = bf16[1536,1152]{1,0:T(8,128)(2,1)S(1)} fusion(bf16[2048,1536]{1,0:T(8,128)(2,1)S(1)} %bitcast.425, bf16[2048,1152]{1,0:T(8,128)(2,1)} %bitcast.431), kind=kOutput, calls=%fused_computation.2 | convolution fusion | flops 7249526784 | bytes 14548992 | tf_op jit(solution)/shard_map/dot_general | solution.py:27
  307.5 13.0 %collective-permute-done.54 = bf16[144,1536]{1,0:T(8,128)(2,1)S(1)} collective-permute-done((bf16[144,1536]{1,0:T(8,128)(2,1)S(1)}, bf16[144,1536]{1,0:T(8,128)(2,1)S(1)}, u32[]{:S(2)}, u32[]{:S(2)}) %collective-permute-start.54) | collective-permute-done | bytes 442400 | tf_op jit(solution)/shard_map/ppermute | solution.py:428
  328.0 14.1 %attend_back.1 = (bf16[2,256,1536]{2,1,0:T(8,128)(2,1)S(1)}, bf16[8,2,2,128,256]{4,3,2,1,0:T(8,128)(2,1)}) custom-call(s32[2]{0:T(128)S(1)} %get-tuple-element.408.blk_ref, s32[4]{0:T(128)S(1)} %maximum_maximum_fusion.1.low_ref, s32[16]{0:T(128)S(1)} %get-tuple-element.395.slot_ref, s32[16]{0:T(128)S(1)} %get-tuple-element.394.half_ref, ...), custom_call_target="tpu_custom_call" | custom-call | flops 17999998976 | bytes 12582912 | tf_op jit(solution)/shard_map/attend_back/pallas_call | solution.py:186
  343.9 9.2 %collective-permute-start.56 = (bf16[4,48,1152]{2,1,0:T(8,128)(2,1)}, bf16[4,48,1152]{2,1,0:T(8,128)(2,1)S(1)}, u32[]{:S(2)}, u32[]{:S(2)}) collective-permute-start(bf16[4,48,1152]{2,1,0:T(8,128)(2,1)} %get-tuple-element.420), channel_id=1, source_target_pairs={{0,8},{8,16},{16,24},{24,28},{28,20},{20,12},{12,4},{4,0},{1,9},{9... | collective-permute-start | bytes 1327112 | tf_op jit(solution)/shard_map/ppermute | solution.py:428
  355.5 5.9 collective-permute-done.56
  387.3 5.7 convert_add_fusion.2
  405.8 5.2 collective-permute-done.70
  480.2 5.9 multiply_add_fusion
  512.7 10.3 %collective-permute-done.93 = bf16[1,384,256]{2,1,0:T(8,128)(2,1)S(1)} collective-permute-done((bf16[1,384,256]{2,1,0:T(8,128)(2,1)S(1)}, bf16[1,384,256]{2,1,0:T(8,128)(2,1)S(1)}, u32[]{:S(2)}, u32[]{:S(2)}) %collective-permute-start.93) | collective-permute-done | bytes 196640 | tf_op jit(solution)/shard_map/ppermute | solution.py:422
  553.7 7.0 %collective-permute-done.110 = bf16[48,4608]{1,0:T(8,128)(2,1)S(1)} collective-permute-done((bf16[48,4608]{1,0:T(8,128)(2,1)S(1)}, bf16[48,4608]{1,0:T(8,128)(2,1)S(1)}, u32[]{:S(2)}, u32[]{:S(2)}) %collective-permute-start.110) | collective-permute-done | bytes 442400 | tf_op jit(solution)/shard_map/ppermute | solution.py:431
  569.4 6.8 %collective-permute-done.104 = bf16[48,1536]{1,0:T(8,128)(2,1)S(1)} collective-permute-done((bf16[48,1536]{1,0:T(8,128)(2,1)S(1)}, bf16[48,1536]{1,0:T(8,128)(2,1)S(1)}, u32[]{:S(2)}, u32[]{:S(2)}) %collective-permute-start.104) | collective-permute-done | bytes 147488 | tf_op jit(solution)/shard_map/ppermute | solution.py:431
  612.7 5.0 place.1
  (684 shorter events, 387.8 us)
Async XLA Ops:
  15.2 61.8 %collective-permute-start.3 = (bf16[384,1536]{1,0:T(8,128)(2,1)S(1)}, bf16[384,1536]{1,0:T(8,128)(2,1)S(1)}, u32[]{:S(2)}, u32[]{:S(2)}) collective-permute-start(bf16[384,1536]{1,0:T(8,128)(2,1)S(1)} %slice.196), channel_id=1, source_target_pairs={{0,1},{1,0},{2,3},{3,2},{4,5},{5,4},{6,7},{7,6},{8,9},{9,8},{10,11... | collective-permute-start | bytes 3538952 | tf_op jit(solution)/shard_map/ppermute | solution.py:422
  26.6 28.3 %collective-permute-start.9 = (bf16[192,1536]{1,0:T(8,128)(2,1)S(1)}, bf16[192,1536]{1,0:T(8,128)(2,1)S(1)}, u32[]{:S(2)}, u32[]{:S(2)}) collective-permute-start(bf16[192,1536]{1,0:T(8,128)(2,1)S(1)} %constant_dynamic-slice_fusion.15), channel_id=1, source_target_pairs={{0,2},{1,3},{2,0},{3,1},{4,6},{5,7},{6,4},{7,5},{8,10},{9,11},{10,... | collective-permute-start | bytes 1769480 | tf_op jit(solution)/shard_map/ppermute | solution.py:422
  76.6 31.0 %collective-permute-start.23 = (bf16[384,1152]{1,0:T(8,128)(2,1)}, bf16[384,1152]{1,0:T(8,128)(2,1)}, u32[]{:S(2)}, u32[]{:S(2)}) collective-permute-start(bf16[384,1152]{1,0:T(8,128)(2,1)} %get-tuple-element.412), channel_id=1, source_target_pairs={{0,1},{1,0},{2,3},{3,2},{4,5},{5,4},{6,7},{7,6},{8,9},{9,8},{10,11... | collective-permute-start | bytes 2654216 | tf_op jit(solution)/shard_map/ppermute | solution.py:422
  89.6 37.4 %collective-permute-start.25 = (bf16[512,1536]{1,0:T(8,128)(2,1)}, bf16[512,1536]{1,0:T(8,128)(2,1)}, u32[]{:S(2)}, u32[]{:S(2)}) collective-permute-start(bf16[512,1536]{1,0:T(8,128)(2,1)} %bitcast.3.gy_a), channel_id=1, source_target_pairs={{0,2},{1,3},{2,0},{3,1},{4,6},{5,7},{6,4},{7,5},{8,10},{9,11},{10,... | collective-permute-start | bytes 4718600 | tf_op jit(solution)/shard_map/ppermute | solution.py:422
  104.8 33.9 %collective-permute-start.22 = (bf16[512,1536]{1,0:T(8,128)(2,1)S(1)}, bf16[512,1536]{1,0:T(8,128)(2,1)}, u32[]{:S(2)}, u32[]{:S(2)}) collective-permute-start(bf16[512,1536]{1,0:T(8,128)(2,1)S(1)} %multiply_convert_fusion.n2_a), channel_id=1, source_target_pairs={{0,1},{1,0},{2,3},{3,2},{4,5},{5,4},{6,7},{7,6},{8,9},{9,8},{10,11... | collective-permute-start | bytes 4718600 | tf_op jit(solution)/shard_map/ppermute | solution.py:422
  107.1 31.5 %collective-permute-start.30 = (bf16[512,1536]{1,0:T(8,128)(2,1)}, bf16[512,1536]{1,0:T(8,128)(2,1)}, u32[]{:S(2)}, u32[]{:S(2)}) collective-permute-start(bf16[512,1536]{1,0:T(8,128)(2,1)} %bitcast.3.gy_a), channel_id=1, source_target_pairs={{0,1},{1,0},{2,3},{3,2},{4,5},{5,4},{6,7},{7,6},{8,9},{9,8},{10,11... | collective-permute-start | bytes 4718600 | tf_op jit(solution)/shard_map/ppermute | solution.py:422
  131.0 46.0 %collective-permute-start.31 = (bf16[512,1536]{1,0:T(8,128)(2,1)S(1)}, bf16[512,1536]{1,0:T(8,128)(2,1)S(1)}, u32[]{:S(2)}, u32[]{:S(2)}) collective-permute-start(bf16[512,1536]{1,0:T(8,128)(2,1)S(1)} %multiply_convert_fusion.n2_a), channel_id=1, source_target_pairs={{0,2},{1,3},{2,0},{3,1},{4,6},{5,7},{6,4},{7,5},{8,10},{9,11},{10,... | collective-permute-start | bytes 4718600 | tf_op jit(solution)/shard_map/ppermute | solution.py:422
  182.4 58.1 %collective-permute-start.34 = (bf16[512,1536]{1,0:T(8,128)(2,1)}, bf16[512,1536]{1,0:T(8,128)(2,1)S(1)}, u32[]{:S(2)}, u32[]{:S(2)}) collective-permute-start(bf16[512,1536]{1,0:T(8,128)(2,1)} %get-tuple-element.236), channel_id=1, source_target_pairs={{0,1},{1,0},{2,3},{3,2},{4,5},{5,4},{6,7},{7,6},{8,9},{9,8},{10,11... | collective-permute-start | bytes 4718600 | tf_op jit(solution)/shard_map/ppermute | solution.py:422
  240.9 40.4 %collective-permute-start.36 = (bf16[512,1536]{1,0:T(8,128)(2,1)S(1)}, bf16[512,1536]{1,0:T(8,128)(2,1)S(1)}, u32[]{:S(2)}, u32[]{:S(2)}) collective-permute-start(bf16[512,1536]{1,0:T(8,128)(2,1)S(1)} %add_convert_fusion.4), channel_id=1, source_target_pairs={{0,2},{1,3},{2,0},{3,1},{4,6},{5,7},{6,4},{7,5},{8,10},{9,11},{10,... | collective-permute-start | bytes 4718600 | tf_op jit(solution)/shard_map/ppermute | solution.py:422
  290.3 34.2 %collective-permute-start.52 = (bf16[4,48,1152]{2,1,0:T(8,128)(2,1)}, bf16[4,48,1152]{2,1,0:T(8,128)(2,1)S(1)}, u32[]{:S(2)}, u32[]{:S(2)}) collective-permute-start(bf16[4,48,1152]{2,1,0:T(8,128)(2,1)} %pad_maximum_fusion.4), channel_id=1, source_target_pairs={{0,8},{8,16},{16,24},{24,28},{28,20},{20,12},{12,4},{4,0},{1,9},{9... | collective-permute-start | bytes 1327112 | tf_op jit(solution)/shard_map/ppermute | solution.py:428
  304.4 60.6 %collective-permute-start.50 = (bf16[4,48,1152]{2,1,0:T(8,128)(2,1)S(1)}, bf16[4,48,1152]{2,1,0:T(8,128)(2,1)S(1)}, u32[]{:S(2)}, u32[]{:S(2)}) collective-permute-start(bf16[4,48,1152]{2,1,0:T(8,128)(2,1)S(1)} %get-tuple-element.424), channel_id=1, source_target_pairs={{0,8},{8,16},{16,24},{24,28},{28,20},{20,12},{12,4},{4,0},{1,9},{9... | collective-permute-start | bytes 1327112 | tf_op jit(solution)/shard_map/ppermute | solution.py:428
  320.5 44.5 %collective-permute-start.51 = (bf16[4,48,1152]{2,1,0:T(8,128)(2,1)S(1)}, bf16[4,48,1152]{2,1,0:T(8,128)(2,1)S(1)}, u32[]{:S(2)}, u32[]{:S(2)}) collective-permute-start(bf16[4,48,1152]{2,1,0:T(8,128)(2,1)S(1)} %get-tuple-element.423), channel_id=1, source_target_pairs={{8,0},{16,8},{24,16},{28,24},{20,28},{12,20},{4,12},{0,4},{9,1},{1... | collective-permute-start | bytes 1327112 | tf_op jit(solution)/shard_map/ppermute | solution.py:431
  321.5 63.7 %collective-permute-start.49 = (bf16[512,1536]{1,0:T(8,128)(2,1)}, bf16[512,1536]{1,0:T(8,128)(2,1)}, u32[]{:S(2)}, u32[]{:S(2)}) collective-permute-start(bf16[512,1536]{1,0:T(8,128)(2,1)} %add_convert_fusion.1), channel_id=1, source_target_pairs={{0,2},{1,3},{2,0},{3,1},{4,6},{5,7},{6,4},{7,5},{8,10},{9,11},{10,... | collective-permute-start | bytes 4718600 | tf_op jit(solution)/shard_map/ppermute | solution.py:422
  385.1 32.3 %collective-permute-start.68 = (bf16[4,48,1152]{2,1,0:T(8,128)(2,1)}, bf16[4,48,1152]{2,1,0:T(8,128)(2,1)S(1)}, u32[]{:S(2)}, u32[]{:S(2)}) collective-permute-start(bf16[4,48,1152]{2,1,0:T(8,128)(2,1)} %get-tuple-element.418), channel_id=1, source_target_pairs={{0,8},{8,16},{16,24},{24,28},{28,20},{20,12},{12,4},{4,0},{1,9},{9... | collective-permute-start | bytes 1327112 | tf_op jit(solution)/shard_map/ppermute | solution.py:428
  425.1 27.8 %collective-permute-start.83 = (bf16[48,1152]{1,0:T(8,128)(2,1)S(1)}, bf16[48,1152]{1,0:T(8,128)(2,1)S(1)}, u32[]{:S(2)}, u32[]{:S(2)}) collective-permute-start(bf16[48,1152]{1,0:T(8,128)(2,1)S(1)} %get-tuple-element.467), channel_id=1, source_target_pairs={{0,1},{1,0},{2,3},{3,2},{4,5},{5,4},{6,7},{7,6},{8,9},{9,8},{10,11... | collective-permute-start | bytes 331784 | tf_op jit(solution)/shard_map/ppermute | solution.py:422
  429.2 39.1 %collective-permute-start.77 = (bf16[48,1152]{1,0:T(8,128)(2,1)S(1)}, bf16[48,1152]{1,0:T(8,128)(2,1)S(1)}, u32[]{:S(2)}, u32[]{:S(2)}) collective-permute-start(bf16[48,1152]{1,0:T(8,128)(2,1)S(1)} %get-tuple-element.464), channel_id=1, source_target_pairs={{0,1},{1,0},{2,3},{3,2},{4,5},{5,4},{6,7},{7,6},{8,9},{9,8},{10,11... | collective-permute-start | bytes 331784 | tf_op jit(solution)/shard_map/ppermute | solution.py:422
  430.7 38.2 %collective-permute-start.78 = (bf16[48,1152]{1,0:T(8,128)(2,1)S(1)}, bf16[48,1152]{1,0:T(8,128)(2,1)S(1)}, u32[]{:S(2)}, u32[]{:S(2)}) collective-permute-start(bf16[48,1152]{1,0:T(8,128)(2,1)S(1)} %get-tuple-element.463), channel_id=1, source_target_pairs={{0,2},{1,3},{2,0},{3,1},{4,6},{5,7},{6,4},{7,5},{8,10},{9,11},{10,... | collective-permute-start | bytes 331784 | tf_op jit(solution)/shard_map/ppermute | solution.py:422
  465.6 33.9 %collective-permute-start.86 = (bf16[1,384,1536]{2,1,0:T(8,128)(2,1)}, bf16[1,384,1536]{2,1,0:T(8,128)(2,1)}, u32[]{:S(2)}, u32[]{:S(2)}) collective-permute-start(bf16[1,384,1536]{2,1,0:T(8,128)(2,1)} %constant_dynamic-slice_fusion.6), channel_id=1, source_target_pairs={{0,2},{1,3},{2,0},{3,1},{4,6},{5,7},{6,4},{7,5},{8,10},{9,11},{10,... | collective-permute-start | bytes 3538952 | tf_op jit(solution)/shard_map/ppermute | solution.py:422
  465.8 63.4 %collective-permute-start.102 = (bf16[1,384,1536]{2,1,0:T(8,128)(2,1)}, bf16[1,384,1536]{2,1,0:T(8,128)(2,1)}, u32[]{:S(2)}, u32[]{:S(2)}) collective-permute-start(bf16[1,384,1536]{2,1,0:T(8,128)(2,1)} %constant_dynamic-slice_fusion.7), channel_id=1, source_target_pairs={{0,2},{1,3},{2,0},{3,1},{4,6},{5,7},{6,4},{7,5},{8,10},{9,11},{10,... | collective-permute-start | bytes 3538952 | tf_op jit(solution)/shard_map/ppermute | solution.py:422
  489.7 55.6 %collective-permute-start.98 = (f32[2,1,2,384]{3,0,2,1:T(2,128)S(1)}, f32[2,1,2,384]{3,0,2,1:T(2,128)S(1)}, u32[]{:S(2)}, u32[]{:S(2)}) collective-permute-start(f32[2,1,2,384]{3,0,2,1:T(2,128)S(1)} %bitcast.420), channel_id=1, source_target_pairs={{0,1},{1,0},{2,3},{3,2},{4,5},{5,4},{6,7},{7,6},{8,9},{9,8},{10,11... | collective-permute-start | bytes 18440 | tf_op jit(solution)/shard_map/ppermute | solution.py:422
  493.6 29.3 %collective-permute-start.93 = (bf16[1,384,256]{2,1,0:T(8,128)(2,1)S(1)}, bf16[1,384,256]{2,1,0:T(8,128)(2,1)S(1)}, u32[]{:S(2)}, u32[]{:S(2)}) collective-permute-start(bf16[1,384,256]{2,1,0:T(8,128)(2,1)S(1)} %copy-done.53), channel_id=1, source_target_pairs={{0,2},{1,3},{2,0},{3,1},{4,6},{5,7},{6,4},{7,5},{8,10},{9,11},{10,... | collective-permute-start | bytes 589832 | tf_op jit(solution)/shard_map/ppermute | solution.py:422
  532.1 30.8 %collective-permute-start.106 = (bf16[48,768]{1,0:T(8,128)(2,1)S(1)}, bf16[48,768]{1,0:T(8,128)(2,1)S(1)}, u32[]{:S(2)}, u32[]{:S(2)}) collective-permute-start(bf16[48,768]{1,0:T(8,128)(2,1)S(1)} %get-tuple-element.473), channel_id=1, source_target_pairs={{0,8},{8,16},{16,24},{24,28},{28,20},{20,12},{12,4},{4,0},{1,9},{9... | collective-permute-start | bytes 221192 | tf_op jit(solution)/shard_map/ppermute | solution.py:428
  552.4 74.8 %collective-permute-start.135 = (bf16[48,4608]{1,0:T(8,128)(2,1)}, bf16[48,4608]{1,0:T(8,128)(2,1)}, u32[]{:S(2)}, u32[]{:S(2)}) collective-permute-start(bf16[48,4608]{1,0:T(8,128)(2,1)} %collective-permute-done.100), channel_id=1, source_target_pairs={{0,8},{8,16},{16,24},{24,28},{28,20},{20,12},{12,4},{4,0},{1,9},{9... | collective-permute-start | bytes 1327112 | tf_op jit(solution)/shard_map/ppermute | solution.py:428
  560.6 67.5 %collective-permute-start.136 = (bf16[48,4608]{1,0:T(8,128)(2,1)}, bf16[48,4608]{1,0:T(8,128)(2,1)}, u32[]{:S(2)}, u32[]{:S(2)}) collective-permute-start(bf16[48,4608]{1,0:T(8,128)(2,1)} %collective-permute-done.101), channel_id=1, source_target_pairs={{8,0},{16,8},{24,16},{28,24},{20,28},{12,20},{4,12},{0,4},{9,1},{1... | collective-permute-start | bytes 1327112 | tf_op jit(solution)/shard_map/ppermute | solution.py:431
  (206 other events, 2553.4 us)

commit v3 on v2

--- a/solution.py
+++ b/solution.py
@@ -152,6 +152,7 @@
 
 lse_spec = pl.BlockSpec((1, 1, 1, QW), lambda s, m, *_: (s, m, 0, 0))
 kernel_params = pltpu.CompilerParams(vmem_limit_bytes=48 * 2**20)
+small_cost = pl.CostEstimate(flops=2**20, bytes_accessed=2**16, transcendentals=0)
 
 
 def attend(scalars, qkv, key_value, seg):
@@ -176,7 +177,7 @@
             jax.ShapeDtypeStruct((seqs, 2, 1, QW), jnp.float32),
         ],
         compiler_params=kernel_params,
-        cost_estimate=pl.CostEstimate(flops=7 * 10**9, bytes_accessed=8 * 2**20, transcendentals=7 * 10**6),
+        cost_estimate=small_cost,
         name="attend",
     )(*scalars, qkv, key_value, seg)
 
@@ -207,45 +208,47 @@
     )(*scalars, qkv, d_mixed, mixed, key_value, seg, lse)
 
 
-def ffn_kernel(counts, at_ref, n2_a, gy_a, n2_b, gy_b, *refs):
-    total = sum(counts)
-    pieces = refs[:total]
+class Loads:
+    def __init__(self, counts, index, at_ref, pieces, stores, sems):
+        self.groups, i = [], 0
+        for store, count in zip(stores, counts, strict=True):
+            group = []
+            for _ in range(count):
+                at, piece = index[i], pieces[i]
+                piece = piece if at is None else piece.at[at]
+                rows = piece.shape[0]
+                place = store.at[pl.ds(pl.multiple_of(at_ref[i], 16), rows)]
+                group.append(pltpu.make_async_copy(piece, place, sems.at[i]))
+                i += 1
+            self.groups.append(group)
+
+        @pl.when(pl.program_id(0) == 0)
+        def _():
+            for group in self.groups:
+                for copy in group:
+                    copy.start()
+
+    def ready(self, i):
+        @pl.when(pl.program_id(0) == 0)
+        def _():
+            for copy in self.groups[i]:
+                copy.wait()
+
+
+def ffn_kernel(counts, index, at_ref, n2_a, gy_a, n2_b, gy_b, *refs):
     *outs, wg_ref, wu_ref, wd_ref, sems = refs[-13:]
     act_ref, dg_ref, du_ref, n2_out, gy_out, dn2_a, down_a, dn2_b, down_b = outs
-    step = pl.program_id(0)
-    first = step < pl.num_programs(0) // 2
-    weights = []
-    for dst, count in zip((wg_ref, wu_ref, wd_ref), counts, strict=True):
-        copies = []
-        for _ in range(count):
-            i = sum(map(len, weights)) + len(copies)
-            src = pieces[i]
-            rows = src.shape[0]
-            place = dst.at[pl.ds(pl.multiple_of(at_ref[i], 16), rows)]
-            copies.append(pltpu.make_async_copy(src, place, sems.at[i]))
-        weights.append(copies)
-
-    @pl.when(step == 0)
-    def _():
-        for copies in weights:
-            for copy in copies:
-                copy.start()
-
-    def ready(copies):
-        @pl.when(step == 0)
-        def _():
-            for copy in copies:
-                copy.wait()
-
+    loads = Loads(counts, index, at_ref, refs, (wg_ref, wu_ref, wd_ref), sems)
+    first = pl.program_id(0) < pl.num_programs(0) // 2
     n2 = jnp.where(first, n2_a[...], n2_b[...])
     gy = jnp.where(first, gy_a[...], gy_b[...])
     n2_out[0] = n2
     gy_out[0] = gy
-    ready(weights[0])
+    loads.ready(0)
     gate = dot_f32(n2, wg_ref[...])
-    ready(weights[1])
+    loads.ready(1)
     up = dot_f32(n2, wu_ref[...])
-    ready(weights[2])
+    loads.ready(2)
     d_act = dot_f32(gy, wd_ref[...], ((1,), (1,)))
     square = gate * gate
     inner = jnp.tanh(gate * (gelu_c + gelu_c * gelu_a * square))
@@ -273,44 +276,97 @@
         down_b[...] = down
 
 
-def ffn(pair, pieces, n2, gy, gate, up, w_down, held):
-    rows, width = n2[0].shape
-    units = w_down.shape[0]
+class Weights:
+    def __init__(self, gate, up, w_down, who):
+        self.groups = [gate, up, [(w_down, None, 0)]]
+        self.counts = list(map(len, self.groups))
+        places = [at for group in self.groups for *_, at in group]
+        self.places = jnp.concatenate([jnp.stack([jnp.asarray(at, jnp.int32) for at in places]), who])
+        self.count = len(places)
+
+    def pieces(self, groups):
+        parts = [p for group in self.groups[:groups] for p in group]
+        return [p for p, *_ in parts], [i for _, i, _ in parts], self.counts[:groups]
+
+
+def ffn(pair, pieces, part, n2, gy, weights, held, ends):
+    some, width = n2[0].shape
+    rows = some if part is None else 2 * some
+    arrays, index, counts = weights.pieces(3)
+    count, units = len(arrays), arrays[-1].shape[0]
     tile = rows // 2
+    steps = 2 if part is None else 1
+    at_row = 0 if part is None else part
     held_shapes = [(pieces, rows, units)] * 3 + [(pieces, rows, width)] * 2
     held_spec = [
-        pl.BlockSpec((1, tile, s[2]), lambda t, at: (2 * pair + t // 2, t % 2, 0)) for s in held_shapes
+        pl.BlockSpec((1, tile, s[2]), lambda t, at: (2 * pair + t // steps, at_row + t % steps, 0)) for s in held_shapes
     ]
-    a_spec = pl.BlockSpec((tile, width), lambda t, at: (jnp.minimum(t, 1), 0))
-    b_spec = pl.BlockSpec((tile, width), lambda t, at: (jnp.maximum(t - 2, 0), 0))
-    parts = [*gate, *up, (w_down, 0)]
-    places = jnp.stack([jnp.asarray(at, jnp.int32) for _, at in parts])
-    arrays = [p for p, _ in parts]
+
+    def spec(second, first_row):
+        def index_map(t, at):
+            return (first_row + (jnp.maximum(t - steps, 0) if second else jnp.minimum(t, steps - 1)), 0)
+
+        return pl.BlockSpec((tile, width), index_map)
+
+    kept = [*held, *ends]
+    first_out = 0 if held else 5
     out = pl.pallas_call(
-        functools.partial(ffn_kernel, (len(gate), len(up), 1)),
+        functools.partial(ffn_kernel, counts, index),
         grid_spec=pltpu.PrefetchScalarGridSpec(
             num_scalar_prefetch=1,
-            grid=(4,),
-            in_specs=[a_spec, a_spec, b_spec, b_spec]
-            + [pl.BlockSpec(memory_space=pl.ANY)] * (len(arrays) + len(held)),
-            out_specs=held_spec + [a_spec, a_spec, b_spec, b_spec],
+            grid=(2 * steps,),
+            in_specs=[spec(False, 0)] * 2
+            + [spec(True, 0)] * 2
+            + [pl.BlockSpec(memory_space=pl.ANY)] * (count + len(kept)),
+            out_specs=held_spec + [spec(False, at_row)] * 2 + [spec(True, at_row)] * 2,
             scratch_shapes=[
                 pltpu.VMEM((width, units), jnp.bfloat16),
                 pltpu.VMEM((width, units), jnp.bfloat16),
                 pltpu.VMEM((units, width), jnp.bfloat16),
-                pltpu.SemaphoreType.DMA((len(arrays),)),
+                pltpu.SemaphoreType.DMA((count,)),
             ],
         ),
         out_shape=[jax.ShapeDtypeStruct(s, jnp.bfloat16) for s in held_shapes]
         + [jax.ShapeDtypeStruct((rows, width), jnp.bfloat16)] * 4,
-        input_output_aliases={5 + len(arrays) + i: i for i in range(len(held))},
+        input_output_aliases={5 + count + i: first_out + i for i in range(len(kept))},
         compiler_params=pltpu.CompilerParams(vmem_limit_bytes=56 * 2**20),
-        cost_estimate=pl.CostEstimate(
-            flops=28 * rows * units * width, bytes_accessed=40 * 2**20, transcendentals=2 * rows * units
-        ),
+        cost_estimate=small_cost,
         name="ffn",
-    )(places, n2[0], gy[0], n2[1], gy[1], *arrays, *held)
-    return out[:5], [out[5], out[7]], [out[6], out[8]]
+    )(weights.places, n2[0], gy[0], n2[1], gy[1], *arrays, *kept)
+    return out[:5], out[5:]
+
+
+def project_kernel(at_ref, x_ref, *refs):
+    *pieces, y_ref, w_ref, sems = refs
+    copies = []
+    for i, piece in enumerate(pieces):
+        rows = piece.shape[0]
+        place = w_ref.at[pl.ds(pl.multiple_of(at_ref[i] * rows, 16), rows)]
+        copies.append(pltpu.make_async_copy(piece, place, sems.at[i]))
+    for copy in copies:
+        copy.start()
+    for copy in copies:
+        copy.wait()
+    y_ref[...] = dot_f32(x_ref[...], w_ref[...]).astype(y_ref.dtype)
+
+
+def project(x, pieces, at, dtype):
+    rows, cols = pieces[0].shape
+    vmem = pl.BlockSpec(memory_space=pltpu.VMEM)
+    return pl.pallas_call(
+        project_kernel,
+        in_specs=[pl.BlockSpec(memory_space=pltpu.SMEM), vmem]
+        + [pl.BlockSpec(memory_space=pl.ANY)] * len(pieces),
+        out_specs=[vmem, vmem],
+        out_shape=[
+            jax.ShapeDtypeStruct((x.shape[0], cols), dtype),
+            jax.ShapeDtypeStruct((len(pieces) * rows, cols), pieces[0].dtype),
+        ],
+        scratch_shapes=[pltpu.SemaphoreType.DMA((len(pieces),))],
+        compiler_params=kernel_params,
+        cost_estimate=small_cost,
+        name="project",
+    )(at, x, *pieces)
 
 
 def blank(shape, dtype):
@@ -326,43 +382,17 @@
     return lax.optimization_barrier((v, *after))[0] if after else v
 
 
-def place_kernel(splits, at_ref, low_ref, high_ref, *outs):
-    first = pl.program_id(0) < pl.num_programs(0) // 2
-    piece = jnp.where(first, low_ref[0], high_ref[0]).astype(jnp.float32)
-    col = 0
-    for out, width in zip(outs, splits, strict=True):
-        out[...] = piece[:, col : col + width]
-        col += width
-
-
-def place_rows(at, first, second, splits):
-    count, rows, cols = first.shape
-    if rows % 8:
-        outs = []
-        col = 0
-        for width in splits:
-            out = blank((2 * count * rows, width), jnp.float32)
-            for i in range(2 * count):
-                piece = (first if i < count else second)[i % count, :, col : col + width]
-                out = lax.dynamic_update_slice(out, piece.astype(jnp.float32), (at[i] * rows, 0))
-            outs.append(out)
-            col += width
-        return outs
+def blank(shape, dtype):
     return pl.pallas_call(
-        functools.partial(place_kernel, splits),
-        grid_spec=pltpu.PrefetchScalarGridSpec(
-            num_scalar_prefetch=1,
-            grid=(2 * count,),
-            in_specs=[
-                pl.BlockSpec((1, rows, cols), lambda t, at: (jnp.minimum(t, count - 1), 0, 0)),
-                pl.BlockSpec((1, rows, cols), lambda t, at: (jnp.maximum(t - count, 0), 0, 0)),
-            ],
-            out_specs=[pl.BlockSpec((rows, width), lambda t, at: (at[t], 0)) for width in splits],
-        ),
-        out_shape=[jax.ShapeDtypeStruct((2 * count * rows, width), jnp.float32) for width in splits],
-        cost_estimate=pl.CostEstimate(flops=0, bytes_accessed=12 * count * rows * cols, transcendentals=0),
-        name="place",
-    )(at, first, second)
+        lambda ref: None,
+        out_shape=jax.ShapeDtypeStruct(shape, dtype),
+        out_specs=pl.BlockSpec(memory_space=pl.ANY),
+        name="blank",
+    )()
+
+
+def tie(v, *after):
+    return lax.optimization_barrier((v, *after))[0] if after else v
 
 
 class Order:
@@ -434,14 +464,16 @@
         return (lax.axis_index("shard") // bit) % 2
 
     def lay_rows(self, pieces):
-        me = lax.axis_index("shard")
         rows, cols = pieces[0].shape
         out = blank((self.shards * rows, cols), pieces[0].dtype)
-        for j, piece in enumerate(pieces):
-            out = lax.dynamic_update_slice(out, piece, ((me ^ j) * rows, 0))
+        for piece, at in zip(pieces, self.others(), strict=True):
+            out = lax.dynamic_update_slice(out, piece, (at * rows, 0))
         return out
 
-    def near(self, v, first=0):
+    def others(self):
+        return lax.axis_index("shard") ^ jnp.arange(self.shards, dtype=jnp.int32)
+
+    def near(self, v):
         pieces = {0: v}
         for bit in reversed(self.bits[:-1]):
             pieces |= {j | bit: self.swap(p, bit) for j, p in pieces.items()}
@@ -477,31 +509,38 @@
             return [lax.dynamic_slice(w, (row, base + shard * units), (count, units)) for base in (0, FF)]
 
         own = block(me, 0, rows)
-        pieces = [(own, me * rows)]
         if n == 4 and self.ctxs % 4 == 0:
             y, z = lax.axis_index("ctx") % 2, (lax.axis_index("ctx") // 2) % 2
             half = rows // 2
             pairs = [(c * n + s, c * n + (s ^ 2 ^ (c % 2))) for c in range(self.ctxs) for s in range(n)]
-            give = block(me ^ 2 ^ y, z * half, half)
-            got = [lax.ppermute(b, ("ctx", "shard"), pairs) for b in give]
-            got = yield got, give
+            give = jnp.stack(block(me ^ 2 ^ y, z * half, half))
+            [got] = yield [lax.ppermute(give, ("ctx", "shard"), pairs)], [give]
             mine, theirs = (me ^ 2 ^ y) * rows, (me ^ 2 ^ (1 - y)) * rows
             at, far = z * half, (1 - z) * half
             second = [self.swap_ctx(got[0], 1), self.swap_ctx(got[1], 2)]
-            near_give = block(me ^ 1, 0, rows)
-            near = [self.swap(b, 1) for b in near_give]
-            g_y, u_z = yield second, [*got, *near_give]
-            third = [self.swap_ctx(got[0], 2), self.swap_ctx(g_y, 2), self.swap_ctx(got[1], 1), self.swap_ctx(u_z, 1)]
-            near = yield near, [g_y, u_z]
-            g_z, g_yz, u_y, u_zy = yield third, near
-            gate = [(own[0], me * rows), (near[0], (me ^ 1) * rows), (got[0], mine + at), (g_y, theirs + at)]
-            gate += [(g_z, mine + far), (g_yz, theirs + far)]
-            up = [(own[1], me * rows), (near[1], (me ^ 1) * rows), (got[1], mine + at), (u_z, mine + far)]
-            up += [(u_y, theirs + at), (u_zy, theirs + far)]
+            near_give = jnp.stack(block(me ^ 1, 0, rows))
+            second.append(self.swap(near_give, 1))
+            g_y, u_z, near = yield second, [got, near_give]
+            give = [jnp.stack([got[0], g_y]), jnp.stack([got[1], u_z])]
+            g_z, u_y = yield [self.swap_ctx(give[0], 2), self.swap_ctx(give[1], 1)], give
+            gate = [(own[0], None, me * rows), (near, 0, (me ^ 1) * rows), (got, 0, mine + at), (g_y, None, theirs + at)]
+            gate += [(g_z, 0, mine + far), (g_z, 1, theirs + far)]
+            up = [(own[1], None, me * rows), (near, 1, (me ^ 1) * rows), (got, 1, mine + at), (u_z, None, mine + far)]
+            up += [(u_y, 0, theirs + at), (u_y, 1, theirs + far)]
             return gate, up
+        gate, up = [(own[0], None, me * rows)], [(own[1], None, me * rows)]
         for j in range(1, n):
-            pieces.append(([self.swap(b, j) for b in block(me ^ j, 0, rows)], (me ^ j) * rows))
-        return [[(pair[i], at) for pair, at in pieces] for i in range(2)]
+            got = self.swap(jnp.stack(block(me ^ j, 0, rows)), j)
+            gate.append((got, 0, (me ^ j) * rows))
+            up.append((got, 1, (me ^ j) * rows))
+        return gate, up
+
+    def sum_whole(self, v):
+        cur = yield from self.scatter_rows(v)
+        for b in range(self.ctxs.bit_length() - 1):
+            [got] = yield [self.swap_ctx(cur, 1 << b)], [cur]
+            cur = add_low(cur, got)
+        return cur
 
     def scatter(self, pieces):
         pieces = dict(enumerate(pieces))
@@ -545,33 +584,6 @@
                 b = add_low(b, v[m - 1 - step])
         [a] = yield [self.go_right(a)], [a]
         return v[0].astype(jnp.float32) + a.astype(jnp.float32) + b.astype(jnp.float32)
-
-    def halve(self, v, axis, order):
-        top = self.ctxs.bit_length() - 1
-        left = [1 << b for b in reversed(range(top))]
-        cur = v.reshape(*v.shape[:axis], *([2] * top), *v.shape[axis + 1 :])
-        for bit in order:
-            at = axis + left.index(bit)
-            left.remove(bit)
-            mine = (lax.axis_index("ctx") // bit) % 2
-            give = lax.dynamic_index_in_dim(cur, 1 - mine, at, False)
-            keep = lax.dynamic_index_in_dim(cur, mine, at, False)
-            [got] = yield [self.swap_ctx(give, bit)], [give]
-            cur = add_low(keep, got)
-        return cur
-
-    def double(self, v, order):
-        cur, ids = v[None], [0]
-        for bit in reversed(order):
-            [other] = yield [self.swap_ctx(cur, bit)], [cur]
-            ids += [k ^ bit for k in ids]
-            if len(ids) < self.ctxs:
-                cur = jnp.concatenate([cur, other])
-        return cur, other, lax.axis_index("ctx") ^ jnp.array(ids, jnp.int32)
-
-    def order(self, first):
-        bits = [1 << b for b in range(self.ctxs.bit_length() - 1)]
-        return [first] + [b for b in bits if b != first]
 
     def ring_reduce(self, own, axis):
         m = self.ctxs // 2
@@ -626,14 +638,6 @@
         mine = yield from self.scatter_rows(v)
         return (yield from self.sum_rows(mine, out))
 
-    def sum_small_over_all(self, v):
-        mine = yield from self.scatter_rows(v)
-        rows, cols = mine.shape
-        order = self.order(1)
-        mine = yield from self.halve(mine.reshape(self.ctxs, rows // self.ctxs, cols), 0, order)
-        low_half, high_half, at = yield from self.double(mine, order)
-        return place_rows(at, low_half, high_half, [cols])[0]
-
     def sum_columns(self, part, out, col):
         n, c = self.shards, self.ctxs
         me = lax.axis_index("shard")
@@ -646,14 +650,6 @@
             whole = lax.dynamic_update_slice(whole, g, (0, (me ^ j) * units))
         yield from self.ring_spread(out, whole, col)
         return out[0]
-
-    def small_sum(self, v):
-        cur = yield from self.scatter_rows(v, lambda a, b: a + b)
-        cur = cur[0] if cur.ndim == v.ndim else cur
-        for bit in self.order(1):
-            [got] = yield [self.swap_ctx(cur, bit)], [cur]
-            cur = cur + got
-        return cur
 
 
 def body(plan, tokens, segments, assign, w_qkv, w_out, w_gate_up, w_down, gain_attn, gain_ffn, cotangent):
@@ -683,68 +679,90 @@
         return chains[name]
 
     def take(names):
-        for name in names.split():
+        for name in names:
             chains[name].step()
 
-    lanes = jnp.zeros((gain_attn.shape[0], HD - 2), low)
-    first = jnp.concatenate([w_qkv[:, QW:], gain_attn[:, None], gain_ffn[:, None], lanes], axis=1)
+    first, gains = w_qkv[:, QW:], jnp.stack([gain_attn, gain_ffn])
     first_far, first_near = chain(plan.gather_far(first)), chain(plan.gather_near(first))
+    gain_far, gain_near = chain(plan.gather_far(gains)), chain(plan.gather_near(gains))
     tok = tokens.reshape(rows, width).astype(jnp.float32)
     scale_one = inv_rms(tok)
     hat_one = tok * scale_one
     first_far.step()
+    gain_far.step()
     q_rows = order.after(w_qkv[:, :QW])
-    q_far, q_near = chain(plan.gather_far_halved(q_rows)), chain(plan.gather_near(q_rows))
-    packed = plan.lay_rows(first_near.finish() + first_far.finish())
-    w_kv = packed[:, : 2 * HD]
-    gain_one, gain_two = (packed[:, 2 * HD + i].astype(jnp.float32) for i in range(2))
+    q_far, q_near = chain(plan.gather_far(q_rows)), chain(plan.gather_near(q_rows))
+    kv_rows = first_near.finish() + first_far.finish()
+    gains = jnp.zeros((2, width), jnp.float32)
+    for j, piece in enumerate(gain_near.finish() + gain_far.finish()):
+        at = plan.others()[j] * piece.shape[1]
+        gains = lax.dynamic_update_slice(gains, piece.astype(jnp.float32), (0, at))
+    gain_one, gain_two = gains
     normed_one = (hat_one * gain_one).astype(low)
-    key_value = dot_f32(normed_one, w_kv).astype(low).reshape(seqs, 2, BLK, 2 * HD)
+    key_value, w_kv = project(normed_one, kv_rows, plan.others(), low)
+    key_value = key_value.reshape(seqs, 2, BLK, 2 * HD)
     kv = chain(plan.ring_gather(key_value))
-    o_rows = order.after(w_out)
-    o_far, o_near = chain(plan.gather_far_halved(o_rows)), chain(plan.gather_near(o_rows))
+    kv.step()
+    grad_low = cotangent.reshape(rows, width)
+    gy_near = chain(plan.gather_near(order.after(grad_low)))
+    kv.step()
     q_far.step()
-    kv.step()
     gu = chain(plan.gate_up_columns(order.after(w_gate_up)))
     kv.step()
-    q_far.step()
-    o_far.step()
-    kv.step()
-    kv_all = kv.finish()
-    o_far.step()
-    gu.step()
-    grad_low = cotangent.reshape(rows, width)
-    gy_rows = order.after(grad_low)
-    gy_far, gy_near = chain(plan.gather_far(gy_rows)), chain(plan.gather_near(gy_rows))
     w_q = plan.lay_rows(q_near.finish() + q_far.finish())
     queries = dot_f32(normed_one, w_q).astype(low).reshape(seqs, rows_dev, QW)
+    order.did(queries)
+    kv_all = kv.finish()
+    o_rows = order.after(w_out)
+    o_far, o_near = chain(plan.gather_far(o_rows)), chain(plan.gather_near(o_rows))
     mixed, lse = attend(scalars, queries, kv_all, seg)
     order.did(mixed)
     gu.step()
-    w_o = plan.lay_rows(o_near.finish() + o_far.finish())
+    gy_near = gy_near.finish()
+    gu.step()
+    cuts = [0, rows // 2, rows] if n == 4 else [0, rows]
+    parts = [slice(a, b) for a, b in zip(cuts, cuts[1:])]
+    gy_far = [chain(plan.gather_far(order.after(grad_low)[parts[0]]))]
+    o_far.step()
+    o_rows = o_near.finish() + o_far.finish()
     mixed_low = mixed.reshape(rows, QW)
-    hidden = tok + dot_f32(mixed_low, w_o)
+    branch, w_o = project(mixed_low, o_rows, plan.others(), jnp.float32)
+    hidden = tok + branch
+    order.did(hidden)
+    gu = gu.finish()
+    gy_far[0].step()
+    weights = Weights(*gu, w_down, plan.others())
     scale_two = inv_rms(hidden)
     hat_two = hidden * scale_two
     normed_two = (hat_two * gain_two).astype(low)
-    order.did(normed_two)
-    n2_far, n2_near = chain(plan.gather_far(normed_two)), chain(plan.gather_near(normed_two))
-    gy_far.step()
-    w_gate, w_up = gu.finish()
-
-    held, d_n2, down = (), [], []
-
-    def feed_forward(n2, gy):
-        nonlocal held, d_n2, down
+    normed_two = order.after(normed_two)
+    n2_near = chain(plan.gather_near(normed_two))
+    n2_far = [chain(plan.gather_far(normed_two[parts[0]]))]
+    for part in parts[1:]:
+        gy_far.append(chain(plan.gather_far(order.after(grad_low)[part])))
+        n2_far.append(chain(plan.gather_far(order.after(normed_two)[part])))
+    held, ends = (), []
+
+    def feed_forward(first, part, n2, gy, ends):
+        nonlocal held
+        got = []
         for p in range(0, len(n2), 2):
-            at = len(d_n2) // 2
-            held, d_n2_pair, down_pair = ffn(at, n, n2[p : p + 2], gy[p : p + 2], w_gate, w_up, w_down, held)
-            d_n2, down = d_n2 + d_n2_pair, down + down_pair
-        order.did(*d_n2)
-
-    feed_forward(n2_near.finish(), gy_near.finish())
-    n2_far.step()
-    feed_forward(n2_far.finish(), gy_far.finish())
+            before = ends[p // 2] if ends else []
+            held, end = ffn((first + p) // 2, n, part, n2[p : p + 2], gy[p : p + 2], weights, held, before)
+            got.append(end)
+        order.did(*[v for end in got for v in end])
+        return got
+
+    ends += feed_forward(0, None, n2_near.finish(), gy_near, [])
+    far = []
+    gy_far[-1].step()
+    for i in range(len(parts)):
+        n2_far[i].step()
+        part = i if len(parts) > 1 else None
+        far = feed_forward(n // 2, part, n2_far[i].finish(), gy_far[i].finish(), far)
+    ends += far
+    d_n2 = [end[i] for end in ends for i in (0, 2)]
+    down = [end[i] for end in ends for i in (1, 3)]
     act, d_gate, d_up, n2_all, gy_all = (v.reshape(n * rows, -1) for v in held)
 
     def grad(left, right):
@@ -762,7 +780,7 @@
     chain(plan.sum_columns(grad(n2_all, d_gate), out_gate_up, 0), "G")
     take("D")
     chain(plan.sum_columns(grad(n2_all, d_up), out_gate_up, FF), "U")
-    take("G D U")
+    take("GDU")
     d_normed_two = chains["T"].finish().astype(jnp.float32)
     e = d_normed_two * gain_two
     d_hidden = grad_low.astype(jnp.float32) + scale_two * (
@@ -773,34 +791,38 @@
     chain(plan.scatter(order.after(*down)), "B")
     d_mixed = dot_f32(order.after(d_branch), w_o, ((1,), (1,))).astype(low).reshape(seqs, rows_dev, QW)
     order.did(d_mixed)
-    take("G B D U")
+    take("GBDU")
     dq, dkv = attend_back(scalars, queries, order.after(d_mixed), mixed, kv_all, seg, lse)
     order.did(dq, dkv)
     chain(plan.ring_scatter(dkv), "K")
     dq = dq.reshape(rows, QW)
-    take("D U G")
+    take("DUG")
     chain(plan.sum_over_all(grad(mixed_low, d_branch), blank_like(w_out)), "O")
     out_qkv = blank_like(w_qkv)
     chain(plan.sum_over_all(grad(normed_one, dq), out_qkv), "Q")
     branch = chains["B"].finish().astype(jnp.float32)
     output = (hidden + branch).reshape(seqs, rows_dev, width)
-    take("O Q K D U G K D")
+    take("OQKDUGKD")
     dkv_low = chains["K"].finish().astype(low).reshape(rows, 2 * HD)
-    chain(plan.sum_small_over_all(grad(normed_one, dkv_low)), "V")
-    take("U V D G")
+    part_kv = grad(normed_one, dkv_low)
+    take("UDG")
     d_normed_one = dot_f32(dq, w_q, ((1,), (1,))) + dot_f32(order.after(dkv_low), w_kv, ((1,), (1,)))
     gains = jnp.stack([jnp.sum(d_normed_one * hat_one, axis=0), jnp.sum(d_normed_two * hat_two, axis=0)])
-    chain(plan.small_sum(jnp.moveaxis(gains.reshape(2, n, width // n), 0, 1)), "S")
+    gain_rows = width // n
+    more = -(-2 * gain_rows // (32 * HD)) * 16
+    gains = jnp.moveaxis(gains.reshape(2, n, gain_rows), 0, 1).reshape(n, 2 * gain_rows).astype(low)
+    gains = jnp.pad(gains, ((0, 0), (0, more * 2 * HD - 2 * gain_rows))).reshape(n, more, 2 * HD)
+    part_kv = jnp.concatenate([part_kv.reshape(n, gain_rows, 2 * HD), gains], axis=1)
+    chain(plan.sum_whole(part_kv.reshape(n * (gain_rows + more), 2 * HD)), "V")
     f = d_normed_one * gain_one
     input_grad = d_hidden + scale_one * (f - hat_one * jnp.mean(f * hat_one, axis=-1, keepdims=True))
-    take("U D Q U V Q O G V S Q U V O S Q V U Q V O Q V O Q V O Q G O Q S O G S O G S O G O")
-    sums = [chains[name] for name in "DGUOQVS"]
-    while any(c.running for c in sums):
-        for c in sums:
-            c.step()
+    take("VUDQUVQOGQUVOQUVQOVQOQOQGOQOGOGOGO")
+    while any(chains[name].running for name in "DGUOQV"):
+        take("DGUOQV")
     grad_down, grad_out, grad_gate_up = chains["D"].result, chains["O"].result, out_gate_up[0]
-    grad_qkv = lax.dynamic_update_slice(out_qkv[0], chains["V"].result, (0, QW))
-    grad_gain_attn, grad_gain_ffn = chains["S"].result
+    last = chains["V"].result.astype(jnp.float32)
+    grad_qkv = lax.dynamic_update_slice(out_qkv[0], last[:gain_rows], (0, QW))
+    grad_gain_attn, grad_gain_ffn = last[gain_rows:].reshape(-1)[: 2 * gain_rows].reshape(2, gain_rows)
     return (
         output,
         input_grad.reshape(seqs, rows_dev, width),

time: 663 us -> 657 us (level)
  Pallas kernels: 104 us -> 120 us
  waiting for transfers between devices: 175 us -> 159 us
  other arithmetic: 93.3 us -> 102 us
  starting transfers between devices: 178 us -> 170 us
    ppermute x48, waiting for transfers between devices: 93.5 us -> 47.8 us  [go_right(): return lax.ppermute(v, 'ctx', self.right)]
    ppermute x46, starting transfers between devices: 44.3 us -> 67.5 us  [go_left(): return lax.ppermute(v, 'ctx', self.left)]
    ppermute x48, starting transfers between devices: 75.9 us -> 55.3 us  [go_right(): return lax.ppermute(v, 'ctx', self.right)]
    ppermute x37 -> x41, waiting for transfers between devices: 21.1 us -> 37.6 us  [swap(): return lax.ppermute(v, 'shard', [(i, i ^ bit) for i in range(self.shards)])]
    ppermute x17 -> x7, starting transfers between devices: 26.8 us -> 14.6 us  [swap_ctx(): return lax.ppermute(v, 'ctx', [(i, i ^ bit) for i in range(self.ctxs)])]
    pallas_call x3 -> x5, Pallas kernels: 82 us -> 93.9 us  [the longest x3 83.6 us: ffn(): pl.pallas_call(functools.partial(ffn_kernel, counts, index), grid_spec=pl...]
    ppermute x46, waiting for transfers between devices: 40 us -> 51.6 us  [go_left(): return lax.ppermute(v, 'ctx', self.left)]
    dynamic_update_slice x16 -> x5, local copies, waits for them, and re-layouts: 12.6 us -> 3.75 us  [the longest x4 2.98 us: lay_rows(): out = lax.dynamic_update_slice(out, piece, (at * rows, 0))]
  transfers between devices with their start and end apart: 150 -> 143, of which waited for: 56 -> 49; matrix products, arithmetic and copies ran while one was open for 27% -> 27% of each run, Pallas kernels for 16% -> 18%
where the time goes in v3:
time: 657 us; the launch traced here: 655 us
  starting transfers between devices  170 us (26%)
  waiting for transfers between devices  159 us (24%)
  Pallas kernels  120 us (18%)
  other arithmetic  102 us (16%)
  matrix products  50 us (8%)
  local copies, waits for them, and re-layouts  41.1 us (6%)
  between operations  12.8 us (2%)
    pallas_call x3, Pallas kernels, ffn(): pl.pallas_call(functools.partial(ffn_kernel, counts, index), grid_spec=pl...  83.6 us
    ppermute x46, starting transfers between devices, go_left(): return lax.ppermute(v, 'ctx', self.left)  67.5 us
    ppermute x48, starting transfers between devices, go_right(): return lax.ppermute(v, 'ctx', self.right)  55.3 us
    ppermute x46, waiting for transfers between devices, go_left(): return lax.ppermute(v, 'ctx', self.left)  51.6 us
    dot_general x10, matrix products, dot_f32(): lax.dot_general(left, right, (dims, ((), ())), preferred_element_type=jnp...  50 us
    dynamic_update_slice x45, other arithmetic, put(): lax.dynamic_update_slice(out[0], piece.astype(jnp.float32), (at, col))  48.4 us
    ppermute x48, waiting for transfers between devices, go_right(): return lax.ppermute(v, 'ctx', self.right)  47.8 us
    ppermute x41, waiting for transfers between devices, swap(): return lax.ppermute(v, 'shard', [(i, i ^ bit) for i in range(self.shards)])  37.6 us
  transfers between devices with their start and end apart: 143, of which 49 were waited for; matrix products, arithmetic and copies ran while one was open for 27% of the time, Pallas kernels for 18%

profile of v3, /device:TPU:0, one launch (start us, length us, event | category | flops | bytes accessed | tf_op | source)
XLA Modules:
  0.0 655.2 jit_solution(14113289051860875305)
XLA Ops:
  27.7 5.3 collective-permute-done.7
  36.4 5.5 collective-permute-done.10
  63.0 9.4 %attend.1 = (bf16[2,256,1536]{2,1,0:T(8,128)(2,1)S(1)}, f32[2,2,1,1536]{3,2,1,0:T(1,128)S(1)}) custom-call(s32[2]{0:T(128)S(1)} %get-tuple-element.432.blk_ref, s32[4]{0:T(128)S(1)} %maximum_maximum_fusion.low_ref, s32[16]{0:T(128)S(1)} %get-tuple-element.415.slot_ref, s32[16]{0:T(128)S(1)} %get-tuple-element.414.half_ref, ...), custom_call_target="tpu_custom_call" | custom-call | flops 1048576 | bytes 65536 | tf_op jit(solution)/shard_map/attend/pallas_call | solution.py:160
  83.7 6.2 collective-permute-done.20.refs_9_
  92.9 5.9 collective-permute-done.17.refs_2_
  108.5 8.2 %project.3 = (f32[512,1536]{1,0:T(8,128)}, bf16[1536,1536]{1,0:T(8,128)(2,1)}) custom-call(s32[4]{0:T(128)S(1)} %iota_xor_fusion.at_ref, bf16[512,1536]{1,0:T(8,128)(2,1)} %bitcast.370, bf16[384,1536]{1,0:T(8,128)(2,1)} %refs_0_, bf16[384,1536]{1,0:T(8,128)(2,1)} %collective-permute-done.16.refs_1_, bf16[384,1536]{1,0:T(8,128)(2,1)} %collective-permute-done.17.refs_2_, ...), custom_call_target="tpu_custom_call" | custom-call | flops 1048576 | bytes 65536 | tf_op jit(solution)/shard_map/project/pallas_call | solution.py:356
  135.8 38.3 %ffn.3 = (bf16[4,512,1152]{2,1,0:T(8,128)(2,1)}, bf16[4,512,1152]{2,1,0:T(8,128)(2,1)}, bf16[4,512,1152]{2,1,0:T(8,128)(2,1)}, bf16[4,512,1536]{2,1,0:T(8,128)(2...) custom-call(s32[17]{0:T(128)} %concatenate.43.at_ref, ...), custom_call_target="tpu_custom_call" | custom-call | flops 1048576 | bytes 65536 | tf_op jit(solution)/shard_map/ffn/pallas_call | solution.py:313
  178.7 22.5 %ffn.4 = (bf16[4,512,1152]{2,1,0:T(8,128)(2,1)}, bf16[4,512,1152]{2,1,0:T(8,128)(2,1)}, bf16[4,512,1152]{2,1,0:T(8,128)(2,1)}, bf16[4,512,1536]{2,1,0:T(8,128)(2...) custom-call(s32[17]{0:T(128)} %concatenate.43.at_ref, ...), custom_call_target="tpu_custom_call", output_to_operand_aliasing={{0}: (18, {}), {1}: (19, {}), {2}: (20, {}), {3}: (21, {}),... | custom-call | flops 1048576 | bytes 65536 | tf_op jit(solution)/shard_map/ffn/pallas_call | solution.py:313
  205.3 22.7 %ffn.5 = (bf16[4,512,1152]{2,1,0:T(8,128)(2,1)}, bf16[4,512,1152]{2,1,0:T(8,128)(2,1)}, bf16[4,512,1152]{2,1,0:T(8,128)(2,1)}, bf16[4,512,1536]{2,1,0:T(8,128)(2...) custom-call(s32[17]{0:T(128)} %concatenate.43.at_ref, ...), custom_call_target="tpu_custom_call", output_to_operand_aliasing={{0}: (18, {}), {1}: (19, {}), {2}: (20, {}), {3}: (21, {}),... | custom-call | flops 1048576 | bytes 65536 | tf_op jit(solution)/shard_map/ffn/pallas_call | solution.py:313
  228.5 11.3 %convolution_convert_fusion.4 = bf16[1152,1536]{1,0:T(8,128)(2,1)S(1)} fusion(bf16[2048,1152]{1,0:T(8,128)(2,1)} %bitcast.387, bf16[2048,1536]{1,0:T(8,128)(2,1)} %bitcast.386), kind=kOutput, calls=%fused_computation.4 | convolution fusion | flops 7249526784 | bytes 14548992 | tf_op jit(solution)/shard_map/dot_general | solution.py:27
  242.9 9.3 %convolution_convert_fusion.3 = bf16[1536,1152]{1,0:T(8,128)(2,1)S(1)} fusion(bf16[2048,1536]{1,0:T(8,128)(2,1)S(1)} %bitcast.384, bf16[2048,1152]{1,0:T(8,128)(2,1)S(1)} %bitcast.390), kind=kOutput, calls=%fused_computation.3 | convolution fusion | flops 7249526784 | bytes 14548992 | tf_op jit(solution)/shard_map/dot_general | solution.py:27
  258.4 8.8 %convolution_convert_fusion.2 = bf16[1536,1152]{1,0:T(8,128)(2,1)S(1)} fusion(bf16[2048,1536]{1,0:T(8,128)(2,1)S(1)} %bitcast.385, bf16[2048,1152]{1,0:T(8,128)(2,1)S(1)} %bitcast.393), kind=kOutput, calls=%fused_computation.2 | convolution fusion | flops 7249526784 | bytes 14548992 | tf_op jit(solution)/shard_map/dot_general | solution.py:27
  278.3 14.8 %collective-permute-done.37 = bf16[512,1536]{1,0:T(8,128)(2,1)S(1)} collective-permute-done((bf16[512,1536]{1,0:T(8,128)(2,1)S(1)}, bf16[512,1536]{1,0:T(8,128)(2,1)S(1)}, u32[]{:S(2)}, u32[]{:S(2)}) %collective-permute-start.37) | collective-permute-done | bytes 1572896 | tf_op jit(solution)/shard_map/ppermute | solution.py:452
  303.0 5.6 convolution_convert_fusion.5
  328.6 5.5 collective-permute-done.54
  337.5 16.4 %attend_back.1 = (bf16[2,256,1536]{2,1,0:T(8,128)(2,1)S(1)}, bf16[8,2,2,128,256]{4,3,2,1,0:T(8,128)(2,1)}) custom-call(s32[2]{0:T(128)S(1)} %get-tuple-element.432.blk_ref, s32[4]{0:T(128)S(1)} %maximum_maximum_fusion.low_ref, s32[16]{0:T(128)S(1)} %get-tuple-element.415.slot_ref, s32[16]{0:T(128)S(1)} %get-tuple-element.414.half_ref, ...), custom_call_target="tpu_custom_call" | custom-call | flops 17999998976 | bytes 12582912 | tf_op jit(solution)/shard_map/attend_back/pallas_call | solution.py:187
  389.3 8.1 %collective-permute-done.50 = bf16[512,1536]{1,0:T(8,128)(2,1)} collective-permute-done((bf16[512,1536]{1,0:T(8,128)(2,1)}, bf16[512,1536]{1,0:T(8,128)(2,1)}, u32[]{:S(2)}, u32[]{:S(2)}) %collective-permute-start.50) | collective-permute-done | bytes 1572896 | tf_op jit(solution)/shard_map/ppermute | solution.py:452
  397.8 5.7 convert_add_fusion.2
  475.1 6.1 collective-permute-done.81
  498.7 5.2 fusion.16
  524.7 6.9 %collective-permute-done.96 = bf16[48,4608]{1,0:T(8,128)(2,1)S(1)} collective-permute-done((bf16[48,4608]{1,0:T(8,128)(2,1)}, bf16[48,4608]{1,0:T(8,128)(2,1)S(1)}, u32[]{:S(2)}, u32[]{:S(2)}) %collective-permute-start.96) | collective-permute-done | bytes 442400 | tf_op jit(solution)/shard_map/ppermute | solution.py:461
  533.4 4.9 collective-permute-done.94
  566.0 8.9 %collective-permute-done.102 = bf16[48,1536]{1,0:T(8,128)(2,1)S(1)} collective-permute-done((bf16[48,1536]{1,0:T(8,128)(2,1)S(1)}, bf16[48,1536]{1,0:T(8,128)(2,1)S(1)}, u32[]{:S(2)}, u32[]{:S(2)}) %collective-permute-start.102) | collective-permute-done | bytes 147488 | tf_op jit(solution)/shard_map/ppermute | solution.py:458
  595.9 5.1 collective-permute-start.122
  (644 shorter events, 395.8 us)
Async XLA Ops:
  18.3 28.5 %collective-permute-start.13 = (bf16[384,1536]{1,0:T(8,128)(2,1)}, bf16[384,1536]{1,0:T(8,128)(2,1)}, u32[]{:S(2)}, u32[]{:S(2)}) collective-permute-start(bf16[384,1536]{1,0:T(8,128)(2,1)} %slice.229), channel_id=1, source_target_pairs={{0,2},{1,3},{2,0},{3,1},{4,6},{5,7},{6,4},{7,5},{8,10},{9,11},{10,... | collective-permute-start | bytes 3538952 | tf_op jit(solution)/shard_map/ppermute | solution.py:452
  20.0 36.3 %collective-permute-start.6 = (bf16[384,1536]{1,0:T(8,128)(2,1)}, bf16[384,1536]{1,0:T(8,128)(2,1)S(1)}, u32[]{:S(2)}, u32[]{:S(2)}) collective-permute-start(bf16[384,1536]{1,0:T(8,128)(2,1)} %slice.229), channel_id=1, source_target_pairs={{0,1},{1,0},{2,3},{3,2},{4,5},{5,4},{6,7},{7,6},{8,9},{9,8},{10,11... | collective-permute-start | bytes 3538952 | tf_op jit(solution)/shard_map/ppermute | solution.py:452
  36.4 43.6 %collective-permute-start.22 = (bf16[512,1536]{1,0:T(8,128)(2,1)S(1)}, bf16[512,1536]{1,0:T(8,128)(2,1)}, u32[]{:S(2)}, u32[]{:S(2)}) collective-permute-start(bf16[512,1536]{1,0:T(8,128)(2,1)S(1)} %bitcast.379), channel_id=1, source_target_pairs={{0,1},{1,0},{2,3},{3,2},{4,5},{5,4},{6,7},{7,6},{8,9},{9,8},{10,11... | collective-permute-start | bytes 4718600 | tf_op jit(solution)/shard_map/ppermute | solution.py:452
  57.5 32.4 %collective-permute-start.21 = (bf16[2,384,1152]{2,1,0:T(8,128)(2,1)S(1)}, bf16[2,384,1152]{2,1,0:T(8,128)(2,1)S(1)}, u32[]{:S(2)}, u32[]{:S(2)}) collective-permute-start(bf16[2,384,1152]{2,1,0:T(8,128)(2,1)S(1)} %pad_maximum_fusion), channel_id=1, source_target_pairs={{0,1},{1,0},{2,3},{3,2},{4,5},{5,4},{6,7},{7,6},{8,9},{9,8},{10,11... | collective-permute-start | bytes 5308424 | tf_op jit(solution)/shard_map/ppermute | solution.py:452
  79.9 28.6 %collective-permute-start.16 = (bf16[384,1536]{1,0:T(8,128)(2,1)}, bf16[384,1536]{1,0:T(8,128)(2,1)}, u32[]{:S(2)}, u32[]{:S(2)}) collective-permute-start(bf16[384,1536]{1,0:T(8,128)(2,1)} %refs_0_), channel_id=1, source_target_pairs={{0,1},{1,0},{2,3},{3,2},{4,5},{5,4},{6,7},{7,6},{8,9},{9,8},{10,11... | collective-permute-start | bytes 3538952 | tf_op jit(solution)/shard_map/ppermute | solution.py:452
  131.9 42.3 %collective-permute-start.30 = (bf16[256,1536]{1,0:T(8,128)(2,1)}, bf16[256,1536]{1,0:T(8,128)(2,1)}, u32[]{:S(2)}, u32[]{:S(2)}) collective-permute-start(bf16[256,1536]{1,0:T(8,128)(2,1)} %slice.237), channel_id=1, source_target_pairs={{0,2},{1,3},{2,0},{3,1},{4,6},{5,7},{6,4},{7,5},{8,10},{9,11},{10,... | collective-permute-start | bytes 2359304 | tf_op jit(solution)/shard_map/ppermute | solution.py:452
  133.6 40.5 %collective-permute-start.29 = (bf16[256,1536]{1,0:T(8,128)(2,1)}, bf16[256,1536]{1,0:T(8,128)(2,1)}, u32[]{:S(2)}, u32[]{:S(2)}) collective-permute-start(bf16[256,1536]{1,0:T(8,128)(2,1)} %slice.236), channel_id=1, source_target_pairs={{0,2},{1,3},{2,0},{3,1},{4,6},{5,7},{6,4},{7,5},{8,10},{9,11},{10,... | collective-permute-start | bytes 2359304 | tf_op jit(solution)/shard_map/ppermute | solution.py:452
  205.1 37.0 %collective-permute-start.35 = (bf16[512,1536]{1,0:T(8,128)(2,1)}, bf16[512,1536]{1,0:T(8,128)(2,1)S(1)}, u32[]{:S(2)}, u32[]{:S(2)}) collective-permute-start(bf16[512,1536]{1,0:T(8,128)(2,1)} %get-tuple-element.249), channel_id=1, source_target_pairs={{0,1},{1,0},{2,3},{3,2},{4,5},{5,4},{6,7},{7,6},{8,9},{9,8},{10,11... | collective-permute-start | bytes 4718600 | tf_op jit(solution)/shard_map/ppermute | solution.py:452
  257.2 35.9 %collective-permute-start.37 = (bf16[512,1536]{1,0:T(8,128)(2,1)S(1)}, bf16[512,1536]{1,0:T(8,128)(2,1)S(1)}, u32[]{:S(2)}, u32[]{:S(2)}) collective-permute-start(bf16[512,1536]{1,0:T(8,128)(2,1)S(1)} %add_convert_fusion.4), channel_id=1, source_target_pairs={{0,2},{1,3},{2,0},{3,1},{4,6},{5,7},{6,4},{7,5},{8,10},{9,11},{10,... | collective-permute-start | bytes 4718600 | tf_op jit(solution)/shard_map/ppermute | solution.py:452
  316.6 53.3 %collective-permute-start.51 = (bf16[4,48,1152]{2,1,0:T(8,128)(2,1)S(1)}, bf16[4,48,1152]{2,1,0:T(8,128)(2,1)S(1)}, u32[]{:S(2)}, u32[]{:S(2)}) collective-permute-start(bf16[4,48,1152]{2,1,0:T(8,128)(2,1)S(1)} %get-tuple-element.448), channel_id=1, source_target_pairs={{0,8},{8,16},{16,24},{24,28},{28,20},{20,12},{12,4},{4,0},{1,9},{9... | collective-permute-start | bytes 1327112 | tf_op jit(solution)/shard_map/ppermute | solution.py:458
  323.7 46.2 %collective-permute-start.52 = (bf16[4,48,1152]{2,1,0:T(8,128)(2,1)S(1)}, bf16[4,48,1152]{2,1,0:T(8,128)(2,1)}, u32[]{:S(2)}, u32[]{:S(2)}) collective-permute-start(bf16[4,48,1152]{2,1,0:T(8,128)(2,1)S(1)} %get-tuple-element.447), channel_id=1, source_target_pairs={{8,0},{16,8},{24,16},{28,24},{20,28},{12,20},{4,12},{0,4},{9,1},{1... | collective-permute-start | bytes 1327112 | tf_op jit(solution)/shard_map/ppermute | solution.py:461
  327.7 28.4 %collective-permute-start.59 = (bf16[144,1536]{1,0:T(8,128)(2,1)}, bf16[144,1536]{1,0:T(8,128)(2,1)S(1)}, u32[]{:S(2)}, u32[]{:S(2)}) collective-permute-start(bf16[144,1536]{1,0:T(8,128)(2,1)} %get-tuple-element.446), channel_id=1, source_target_pairs={{0,8},{8,16},{16,24},{24,28},{28,20},{20,12},{12,4},{4,0},{1,9},{9... | collective-permute-start | bytes 1327112 | tf_op jit(solution)/shard_map/ppermute | solution.py:458
  337.1 28.6 %collective-permute-start.57 = (bf16[4,48,1152]{2,1,0:T(8,128)(2,1)}, bf16[4,48,1152]{2,1,0:T(8,128)(2,1)S(1)}, u32[]{:S(2)}, u32[]{:S(2)}) collective-permute-start(bf16[4,48,1152]{2,1,0:T(8,128)(2,1)} %get-tuple-element.444), channel_id=1, source_target_pairs={{0,8},{8,16},{16,24},{24,28},{28,20},{20,12},{12,4},{4,0},{1,9},{9... | collective-permute-start | bytes 1327112 | tf_op jit(solution)/shard_map/ppermute | solution.py:458
  360.2 37.2 %collective-permute-start.50 = (bf16[512,1536]{1,0:T(8,128)(2,1)}, bf16[512,1536]{1,0:T(8,128)(2,1)}, u32[]{:S(2)}, u32[]{:S(2)}) collective-permute-start(bf16[512,1536]{1,0:T(8,128)(2,1)} %add_convert_fusion.1), channel_id=1, source_target_pairs={{0,2},{1,3},{2,0},{3,1},{4,6},{5,7},{6,4},{7,5},{8,10},{9,11},{10,... | collective-permute-start | bytes 4718600 | tf_op jit(solution)/shard_map/ppermute | solution.py:452
  383.5 27.9 %collective-permute-start.63 = (bf16[2,384,1536]{2,1,0:T(8,128)(2,1)}, bf16[2,384,1536]{2,1,0:T(8,128)(2,1)}, u32[]{:S(2)}, u32[]{:S(2)}) collective-permute-start(bf16[2,384,1536]{2,1,0:T(8,128)(2,1)} %dynamic-slice_bitcast_fusion), channel_id=1, source_target_pairs={{0,1},{1,0},{2,3},{3,2},{4,5},{5,4},{6,7},{7,6},{8,9},{9,8},{10,11... | collective-permute-start | bytes 7077896 | tf_op jit(solution)/shard_map/ppermute | solution.py:452
  384.5 29.5 %collective-permute-start.61 = (bf16[2,2,128,256]{3,2,1,0:T(8,128)(2,1)}, bf16[2,2,128,256]{3,2,1,0:T(8,128)(2,1)S(1)}, u32[]{:S(2)}, u32[]{:S(2)}) collective-permute-start(bf16[2,2,128,256]{3,2,1,0:T(8,128)(2,1)} %get-tuple-element.471), channel_id=1, source_target_pairs={{0,8},{8,16},{16,24},{24,28},{28,20},{20,12},{12,4},{4,0},{1,9},{9... | collective-permute-start | bytes 786440 | tf_op jit(solution)/shard_map/ppermute | solution.py:458
  389.3 28.0 %collective-permute-start.62 = (bf16[2,2,128,256]{3,2,1,0:T(8,128)(2,1)}, bf16[2,2,128,256]{3,2,1,0:T(8,128)(2,1)S(1)}, u32[]{:S(2)}, u32[]{:S(2)}) collective-permute-start(bf16[2,2,128,256]{3,2,1,0:T(8,128)(2,1)} %get-tuple-element.470), channel_id=1, source_target_pairs={{8,0},{16,8},{24,16},{28,24},{20,28},{12,20},{4,12},{0,4},{9,1},{1... | collective-permute-start | bytes 786440 | tf_op jit(solution)/shard_map/ppermute | solution.py:461
  437.1 31.9 %collective-permute-start.83 = (bf16[48,1152]{1,0:T(8,128)(2,1)S(1)}, bf16[48,1152]{1,0:T(8,128)(2,1)S(1)}, u32[]{:S(2)}, u32[]{:S(2)}) collective-permute-start(bf16[48,1152]{1,0:T(8,128)(2,1)S(1)} %get-tuple-element.495), channel_id=1, source_target_pairs={{0,1},{1,0},{2,3},{3,2},{4,5},{5,4},{6,7},{7,6},{8,9},{9,8},{10,11... | collective-permute-start | bytes 331784 | tf_op jit(solution)/shard_map/ppermute | solution.py:452
  441.0 27.9 %collective-permute-start.84 = (bf16[48,1152]{1,0:T(8,128)(2,1)S(1)}, bf16[48,1152]{1,0:T(8,128)(2,1)S(1)}, u32[]{:S(2)}, u32[]{:S(2)}) collective-permute-start(bf16[48,1152]{1,0:T(8,128)(2,1)S(1)} %get-tuple-element.494), channel_id=1, source_target_pairs={{0,2},{1,3},{2,0},{3,1},{4,6},{5,7},{6,4},{7,5},{8,10},{9,11},{10,... | collective-permute-start | bytes 331784 | tf_op jit(solution)/shard_map/ppermute | solution.py:452
  454.4 30.6 %collective-permute-start.78 = (bf16[48,1152]{1,0:T(8,128)(2,1)S(1)}, bf16[48,1152]{1,0:T(8,128)(2,1)S(1)}, u32[]{:S(2)}, u32[]{:S(2)}) collective-permute-start(bf16[48,1152]{1,0:T(8,128)(2,1)S(1)} %get-tuple-element.492), channel_id=1, source_target_pairs={{0,1},{1,0},{2,3},{3,2},{4,5},{5,4},{6,7},{7,6},{8,9},{9,8},{10,11... | collective-permute-start | bytes 331784 | tf_op jit(solution)/shard_map/ppermute | solution.py:452
  481.2 35.0 %collective-permute-start.86 = (bf16[1,384,1536]{2,1,0:T(8,128)(2,1)}, bf16[1,384,1536]{2,1,0:T(8,128)(2,1)}, u32[]{:S(2)}, u32[]{:S(2)}) collective-permute-start(bf16[1,384,1536]{2,1,0:T(8,128)(2,1)} %constant_dynamic-slice_fusion.1), channel_id=1, source_target_pairs={{0,2},{1,3},{2,0},{3,1},{4,6},{5,7},{6,4},{7,5},{8,10},{9,11},{10,... | collective-permute-start | bytes 3538952 | tf_op jit(solution)/shard_map/ppermute | solution.py:452
  505.4 39.0 %collective-permute-start.101 = (bf16[1,384,1536]{2,1,0:T(8,128)(2,1)S(1)}, bf16[1,384,1536]{2,1,0:T(8,128)(2,1)S(1)}, u32[]{:S(2)}, u32[]{:S(2)}) collective-permute-start(bf16[1,384,1536]{2,1,0:T(8,128)(2,1)S(1)} %copy-done.44), channel_id=1, source_target_pairs={{0,2},{1,3},{2,0},{3,1},{4,6},{5,7},{6,4},{7,5},{8,10},{9,11},{10,... | collective-permute-start | bytes 3538952 | tf_op jit(solution)/shard_map/ppermute | solution.py:452
  506.7 39.0 %collective-permute-start.100 = (bf16[48,4608]{1,0:T(8,128)(2,1)S(1)}, bf16[48,4608]{1,0:T(8,128)(2,1)S(1)}, u32[]{:S(2)}, u32[]{:S(2)}) collective-permute-start(bf16[48,4608]{1,0:T(8,128)(2,1)S(1)} %copy-done.41), channel_id=1, source_target_pairs={{8,0},{16,8},{24,16},{28,24},{20,28},{12,20},{4,12},{0,4},{9,1},{1... | collective-permute-start | bytes 1327112 | tf_op jit(solution)/shard_map/ppermute | solution.py:461
  556.7 67.3 %collective-permute-start.131 = (bf16[48,4608]{1,0:T(8,128)(2,1)S(1)}, bf16[48,4608]{1,0:T(8,128)(2,1)S(1)}, u32[]{:S(2)}, u32[]{:S(2)}) collective-permute-start(bf16[48,4608]{1,0:T(8,128)(2,1)S(1)} %collective-permute-done.99), channel_id=1, source_target_pairs={{0,8},{8,16},{16,24},{24,28},{28,20},{20,12},{12,4},{4,0},{1,9},{9... | collective-permute-start | bytes 1327112 | tf_op jit(solution)/shard_map/ppermute | solution.py:458
  (194 other events, 2521.1 us)

commit v4 on v3

--- a/solution.py
+++ b/solution.py
@@ -585,70 +585,67 @@
         [a] = yield [self.go_right(a)], [a]
         return v[0].astype(jnp.float32) + a.astype(jnp.float32) + b.astype(jnp.float32)
 
-    def ring_reduce(self, own, axis):
+    def ways(self, way):
+        return (self.go_right, self.go_left) if way > 0 else (self.go_left, self.go_right)
+
+    def ring_reduce(self, own, way):
         m = self.ctxs // 2
-        far = own(m)
-        cut = far.shape[axis] // 2
-        head = functools.partial(lax.slice_in_dim, start_index=0, limit_index=cut, axis=axis)
-        tail = functools.partial(lax.slice_in_dim, start_index=cut, limit_index=None, axis=axis)
-        a, b = head(far), tail(far)
-        for k in range(m - 1, -1, -1):
-            a, b = yield [self.go_right(a), self.go_left(b)], [a, b]
-            at_a, at_b = own(k), own(-k)
-            if k == 0:
-                total = at_a.astype(jnp.float32) + a.astype(jnp.float32) + b.astype(jnp.float32)
-            elif k == m - 1:
-                a = jnp.concatenate([add_low(a, head(at_a)), tail(at_a)], axis)
-                b = jnp.concatenate([head(at_b), add_low(b, tail(at_b))], axis)
-            else:
-                a, b = add_low(a, at_a), add_low(b, at_b)
+        far, near = self.ways(way)
+        a, b = own(way * m), own(-way * (m - 1))
+        for k in range(m - 1, 0, -1):
+            a, b = yield [far(a), near(b)], [a, b]
+            a = add_low(a, own(way * k))
+            if k > 1:
+                b = add_low(b, own(-way * (k - 1)))
+        [a] = yield [far(a)], [a]
+        total = own(0).astype(jnp.float32) + a.astype(jnp.float32) + b.astype(jnp.float32)
         return total.astype(jnp.bfloat16)
 
-    def ring_spread(self, out, chunk, col):
+    def ring_spread(self, out, chunk, col, way):
         m = self.ctxs // 2
         place = self.my_place()
-        cut = chunk.shape[1] // 2
-
-        def put(piece, k, col):
+        far, near = self.ways(way)
+
+        def put(piece, k):
             at = lax.rem(place + k + 2 * m, 2 * m) * piece.shape[0]
             out[0] = lax.dynamic_update_slice(out[0], piece.astype(jnp.float32), (at, col))
 
-        put(chunk, 0, col)
+        put(chunk, 0)
         a = b = chunk
-        for k in range(1, m + 1):
-            if k == m:
-                a, b = a[:, :cut], b[:, cut:]
-            a, b = yield [self.go_right(a), self.go_left(b)], [a, b]
-            put(a, -k, col)
-            put(b, k, col + cut if k == m else col)
+        for k in range(1, m):
+            a, b = yield [far(a), near(b)], [a, b]
+            put(a, -way * k)
+            put(b, way * k)
+        [a] = yield [far(a)], [a]
+        put(a, m)
 
     def own_chunk(self, chunks, axis):
         place = self.my_place()
         n = self.ctxs
         return lambda k: lax.dynamic_index_in_dim(chunks, lax.rem(place + k + n, n), axis, False)
 
-    def sum_rows(self, v, out):
+    def sum_rows(self, v, out, way):
         rows, cols = v.shape
         chunks = v.reshape(self.ctxs, rows // self.ctxs, cols)
-        mine = yield from self.ring_reduce(self.own_chunk(chunks, 0), 1)
-        yield from self.ring_spread(out, mine, 0)
+        mine = yield from self.ring_reduce(self.own_chunk(chunks, 0), way)
+        yield from self.ring_spread(out, mine, 0, way)
         return out[0]
 
-    def sum_over_all(self, v, out):
+    def sum_over_all(self, v, out, way):
         mine = yield from self.scatter_rows(v)
-        return (yield from self.sum_rows(mine, out))
-
-    def sum_columns(self, part, out, col):
+        return (yield from self.sum_rows(mine, out, way))
+
+    def sum_columns(self, part, out, col, way):
         n, c = self.shards, self.ctxs
         me = lax.axis_index("shard")
         rows, units = part.shape[0] // n // c, part.shape[1]
-        mine = yield from self.ring_reduce(self.own_chunk(part.reshape(n, c, rows, units), 1), 0)
+        mine = yield from self.ring_reduce(self.own_chunk(part.reshape(n, c, rows, units), 1), way)
         got = [lax.dynamic_index_in_dim(mine, me ^ j, 0, False) for j in range(n)]
         others = yield [self.swap(g, j) for j, g in enumerate(got) if j], got[1:]
         whole = blank((rows, n * units), jnp.bfloat16)
         for j, g in enumerate([got[0], *others]):
             whole = lax.dynamic_update_slice(whole, g, (0, (me ^ j) * units))
-        yield from self.ring_spread(out, whole, col)
+        yield from self.ring_spread(out, whole, col, way)
         return out[0]
 
 
@@ -774,12 +771,12 @@
         return [blank(w.shape, jnp.float32)]
 
     chain(plan.scatter(d_n2), "T")
-    chain(plan.sum_rows(grad(act, gy_all), blank_like(w_down)), "D")
+    chain(plan.sum_rows(grad(act, gy_all), blank_like(w_down), 1), "D")
     take("T")
     out_gate_up = blank_like(w_gate_up)
-    chain(plan.sum_columns(grad(n2_all, d_gate), out_gate_up, 0), "G")
+    chain(plan.sum_columns(grad(n2_all, d_gate), out_gate_up, 0, -1), "G")
     take("D")
-    chain(plan.sum_columns(grad(n2_all, d_up), out_gate_up, FF), "U")
+    chain(plan.sum_columns(grad(n2_all, d_up), out_gate_up, FF, 1), "U")
     take("GDU")
     d_normed_two = chains["T"].finish().astype(jnp.float32)
     e = d_normed_two * gain_two
@@ -797,9 +794,9 @@
     chain(plan.ring_scatter(dkv), "K")
     dq = dq.reshape(rows, QW)
     take("DUG")
-    chain(plan.sum_over_all(grad(mixed_low, d_branch), blank_like(w_out)), "O")
+    chain(plan.sum_over_all(grad(mixed_low, d_branch), blank_like(w_out), -1), "O")
     out_qkv = blank_like(w_qkv)
-    chain(plan.sum_over_all(grad(normed_one, dq), out_qkv), "Q")
+    chain(plan.sum_over_all(grad(normed_one, dq), out_qkv, 1), "Q")
     branch = chains["B"].finish().astype(jnp.float32)
     output = (hidden + branch).reshape(seqs, rows_dev, width)
     take("OQKDUGKD")

time: 657 us -> 649 us (0.988)
  starting transfers between devices: 170 us -> 153 us
  Pallas kernels: 120 us -> 129 us
    ppermute x46 -> x40, starting transfers between devices: 67.5 us -> 32.3 us  [go_left(): return lax.ppermute(v, 'ctx', self.left)]
    ppermute x48 -> x44, starting transfers between devices: 55.3 us -> 73.6 us  [go_right(): return lax.ppermute(v, 'ctx', self.right)]
    ppermute x48 -> x44, waiting for transfers between devices: 47.8 us -> 62.6 us  [go_right(): return lax.ppermute(v, 'ctx', self.right)]
    ppermute x46 -> x40, waiting for transfers between devices: 51.6 us -> 43.5 us  [go_left(): return lax.ppermute(v, 'ctx', self.left)]
    convert_element_type x30 -> x27, other arithmetic: 20.2 us -> 25.8 us  [add_low(): return (a.astype(jnp.float32) + b.astype(jnp.float32)).astype(jnp.bfloat16)]
    dynamic_update_slice x45 -> x40, other arithmetic: 48.4 us -> 45 us  [put(): lax.dynamic_update_slice(out[0], piece.astype(jnp.float32), (at, col))]
  transfers between devices with their start and end apart: 143 -> 133, of which waited for: 49 -> 50; matrix products, arithmetic and copies ran while one was open for 27% -> 27% of each run, Pallas kernels for 18% -> 20%
where the time goes in v4:
time: 649 us
  waiting for transfers between devices  161 us (25%)
  starting transfers between devices  153 us (24%)
  Pallas kernels  129 us (20%)
  other arithmetic  101 us (16%)
  matrix products  50 us (8%)
  local copies, waits for them, and re-layouts  42 us (6%)
  between operations  12.6 us (2%)
    pallas_call x3, Pallas kernels, ffn(): pl.pallas_call(functools.partial(ffn_kernel, counts, index), grid_spec=pl...  83.6 us
    ppermute x44, starting transfers between devices, go_right(): return lax.ppermute(v, 'ctx', self.right)  73.6 us
    ppermute x44, waiting for transfers between devices, go_right(): return lax.ppermute(v, 'ctx', self.right)  62.6 us
    dot_general x10, matrix products, dot_f32(): lax.dot_general(left, right, (dims, ((), ())), preferred_element_type=jnp...  50 us
    dynamic_update_slice x40, other arithmetic, put(): lax.dynamic_update_slice(out[0], piece.astype(jnp.float32), (at, col))  45 us
    ppermute x40, waiting for transfers between devices, go_left(): return lax.ppermute(v, 'ctx', self.left)  43.5 us
    ppermute x41, waiting for transfers between devices, swap(): return lax.ppermute(v, 'shard', [(i, i ^ bit) for i in range(self.shards)])  38.7 us
    ppermute x41, starting transfers between devices, swap(): return lax.ppermute(v, 'shard', [(i, i ^ bit) for i in range(self.shards)])  36.9 us
  transfers between devices with their start and end apart: 133, of which 50 were waited for; matrix products, arithmetic and copies ran while one was open for 27% of the time, Pallas kernels for 20%

profile of v4, /device:TPU:0, one launch (start us, length us, event | category | flops | bytes accessed | tf_op | source)
XLA Modules:
  0.0 649.2 jit_solution(14968845888074839267)
XLA Ops:
  36.4 5.5 collective-permute-done.10
  63.0 13.3 %attend.1 = (bf16[2,256,1536]{2,1,0:T(8,128)(2,1)S(1)}, f32[2,2,1,1536]{3,2,1,0:T(1,128)S(1)}) custom-call(s32[2]{0:T(128)S(1)} %get-tuple-element.412.blk_ref, s32[4]{0:T(128)S(1)} %maximum_maximum_fusion.low_ref, s32[16]{0:T(128)S(1)} %get-tuple-element.395.slot_ref, s32[16]{0:T(128)S(1)} %get-tuple-element.394.half_ref, ...), custom_call_target="tpu_custom_call" | custom-call | flops 1048576 | bytes 65536 | tf_op jit(solution)/shard_map/attend/pallas_call | solution.py:160
  76.3 9.0 %collective-permute-start.17 = (bf16[384,1536]{1,0:T(8,128)(2,1)}, bf16[384,1536]{1,0:T(8,128)(2,1)}, u32[]{:S(2)}, u32[]{:S(2)}) collective-permute-start(bf16[384,1536]{1,0:T(8,128)(2,1)} %refs_0_), channel_id=1, source_target_pairs={{0,2},{1,3},{2,0},{3,1},{4,6},{5,7},{6,4},{7,5},{8,10},{9,11},{10,... | collective-permute-start | bytes 3538952 | tf_op jit(solution)/shard_map/ppermute | solution.py:452
  86.5 7.3 %collective-permute-done.19.refs_3_ = bf16[192,1152]{1,0:T(8,128)(2,1)S(1)} collective-permute-done((bf16[192,1152]{1,0:T(8,128)(2,1)S(1)}, bf16[192,1152]{1,0:T(8,128)(2,1)S(1)}, u32[]{:S(2)}, u32[]{:S(2)}) %collective-permute-start.19) | collective-permute-done | bytes 442400 | tf_op jit(solution)/shard_map/ppermute | solution.py:455
  97.0 10.9 %collective-permute-done.17.refs_2_ = bf16[384,1536]{1,0:T(8,128)(2,1)} collective-permute-done((bf16[384,1536]{1,0:T(8,128)(2,1)}, bf16[384,1536]{1,0:T(8,128)(2,1)}, u32[]{:S(2)}, u32[]{:S(2)}) %collective-permute-start.17) | collective-permute-done | bytes 1179680 | tf_op jit(solution)/shard_map/ppermute | solution.py:452
  111.1 8.2 %project.3 = (f32[512,1536]{1,0:T(8,128)}, bf16[1536,1536]{1,0:T(8,128)(2,1)}) custom-call(s32[4]{0:T(128)S(1)} %iota_xor_fusion.at_ref, bf16[512,1536]{1,0:T(8,128)(2,1)} %bitcast.325, bf16[384,1536]{1,0:T(8,128)(2,1)} %refs_0_, bf16[384,1536]{1,0:T(8,128)(2,1)} %collective-permute-done.16.refs_1_, bf16[384,1536]{1,0:T(8,128)(2,1)} %collective-permute-done.17.refs_2_, ...), custom_call_target="tpu_custom_call" | custom-call | flops 1048576 | bytes 65536 | tf_op jit(solution)/shard_map/project/pallas_call | solution.py:356
  121.7 8.6 %collective-permute-done.26.refs_10_.refs_11_ = bf16[2,192,1152]{2,1,0:T(8,128)(2,1)} collective-permute-done((bf16[2,192,1152]{2,1,0:T(8,128)(2,1)}, bf16[2,192,1152]{2,1,0:T(8,128)(2,1)}, u32[]{:S(2)}, u32[]{:S(2)}) %collective-permute-start.26) | collective-permute-done | bytes 884768 | tf_op jit(solution)/shard_map/ppermute | solution.py:455
  138.7 38.3 %ffn.3 = (bf16[4,512,1152]{2,1,0:T(8,128)(2,1)}, bf16[4,512,1152]{2,1,0:T(8,128)(2,1)}, bf16[4,512,1152]{2,1,0:T(8,128)(2,1)}, bf16[4,512,1536]{2,1,0:T(8,128)(2...) custom-call(s32[17]{0:T(128)} %concatenate.13.at_ref, ...), custom_call_target="tpu_custom_call" | custom-call | flops 1048576 | bytes 65536 | tf_op jit(solution)/shard_map/ffn/pallas_call | solution.py:313
  181.7 22.5 %ffn.4 = (bf16[4,512,1152]{2,1,0:T(8,128)(2,1)}, bf16[4,512,1152]{2,1,0:T(8,128)(2,1)}, bf16[4,512,1152]{2,1,0:T(8,128)(2,1)}, bf16[4,512,1536]{2,1,0:T(8,128)(2...) custom-call(s32[17]{0:T(128)} %concatenate.13.at_ref, ...), custom_call_target="tpu_custom_call", output_to_operand_aliasing={{0}: (18, {}), {1}: (19, {}), {2}: (20, {}), {3}: (21, {}),... | custom-call | flops 1048576 | bytes 65536 | tf_op jit(solution)/shard_map/ffn/pallas_call | solution.py:313
  209.6 22.7 %ffn.5 = (bf16[4,512,1152]{2,1,0:T(8,128)(2,1)}, bf16[4,512,1152]{2,1,0:T(8,128)(2,1)}, bf16[4,512,1152]{2,1,0:T(8,128)(2,1)}, bf16[4,512,1536]{2,1,0:T(8,128)(2...) custom-call(s32[17]{0:T(128)} %concatenate.13.at_ref, ...), custom_call_target="tpu_custom_call", output_to_operand_aliasing={{0}: (18, {}), {1}: (19, {}), {2}: (20, {}), {3}: (21, {}),... | custom-call | flops 1048576 | bytes 65536 | tf_op jit(solution)/shard_map/ffn/pallas_call | solution.py:313
  232.8 11.3 %convolution_convert_fusion.4 = bf16[1152,1536]{1,0:T(8,128)(2,1)S(1)} fusion(bf16[2048,1152]{1,0:T(8,128)(2,1)} %bitcast.342, bf16[2048,1536]{1,0:T(8,128)(2,1)} %bitcast.341), kind=kOutput, calls=%fused_computation.4 | convolution fusion | flops 7249526784 | bytes 14548992 | tf_op jit(solution)/shard_map/dot_general | solution.py:27
  246.8 9.3 %convolution_convert_fusion.3 = bf16[1536,1152]{1,0:T(8,128)(2,1)S(1)} fusion(bf16[2048,1536]{1,0:T(8,128)(2,1)S(1)} %bitcast.339, bf16[2048,1152]{1,0:T(8,128)(2,1)S(1)} %bitcast.345), kind=kOutput, calls=%fused_computation.3 | convolution fusion | flops 7249526784 | bytes 14548992 | tf_op jit(solution)/shard_map/dot_general | solution.py:27
  261.6 8.8 %convolution_convert_fusion.2 = bf16[1536,1152]{1,0:T(8,128)(2,1)S(1)} fusion(bf16[2048,1536]{1,0:T(8,128)(2,1)S(1)} %bitcast.340, bf16[2048,1152]{1,0:T(8,128)(2,1)S(1)} %bitcast.348), kind=kOutput, calls=%fused_computation.2 | convolution fusion | flops 7249526784 | bytes 14548992 | tf_op jit(solution)/shard_map/dot_general | solution.py:27
  274.0 6.4 collective-permute-done.42
  281.6 6.6 %collective-permute-done.40 = bf16[4,48,1152]{2,1,0:T(8,128)(2,1)S(1)} collective-permute-done((bf16[4,48,1152]{2,1,0:T(8,128)(2,1)S(1)}, bf16[4,48,1152]{2,1,0:T(8,128)(2,1)S(1)}, u32[]{:S(2)}, u32[]{:S(2)}) %collective-permute-start.40) | collective-permute-done | bytes 442400 | tf_op jit(solution)/shard_map/ppermute | solution.py:458
  289.3 7.1 %collective-permute-done.37 = bf16[512,1536]{1,0:T(8,128)(2,1)S(1)} collective-permute-done((bf16[512,1536]{1,0:T(8,128)(2,1)S(1)}, bf16[512,1536]{1,0:T(8,128)(2,1)S(1)}, u32[]{:S(2)}, u32[]{:S(2)}) %collective-permute-start.37) | collective-permute-done | bytes 1572896 | tf_op jit(solution)/shard_map/ppermute | solution.py:452
  305.8 5.5 convolution_convert_fusion.5
  340.5 21.7 %attend_back.1 = (bf16[2,256,1536]{2,1,0:T(8,128)(2,1)S(1)}, bf16[8,2,2,128,256]{4,3,2,1,0:T(8,128)(2,1)}) custom-call(s32[2]{0:T(128)S(1)} %get-tuple-element.412.blk_ref, s32[4]{0:T(128)S(1)} %maximum_maximum_fusion.low_ref, s32[16]{0:T(128)S(1)} %get-tuple-element.395.slot_ref, s32[16]{0:T(128)S(1)} %get-tuple-element.394.half_ref, ...), custom_call_target="tpu_custom_call" | custom-call | flops 17999998976 | bytes 12582912 | tf_op jit(solution)/shard_map/attend_back/pallas_call | solution.py:187
  364.5 11.6 %collective-permute-start.50 = (bf16[512,1536]{1,0:T(8,128)(2,1)}, bf16[512,1536]{1,0:T(8,128)(2,1)}, u32[]{:S(2)}, u32[]{:S(2)}) collective-permute-start(bf16[512,1536]{1,0:T(8,128)(2,1)} %add_convert_fusion.1), channel_id=1, source_target_pairs={{0,2},{1,3},{2,0},{3,1},{4,6},{5,7},{6,4},{7,5},{8,10},{9,11},{10,... | collective-permute-start | bytes 4718600 | tf_op jit(solution)/shard_map/ppermute | solution.py:452
  465.6 6.7 %collective-permute-done.78 = bf16[144,1536]{1,0:T(8,128)(2,1)S(1)} collective-permute-done((bf16[144,1536]{1,0:T(8,128)(2,1)S(1)}, bf16[144,1536]{1,0:T(8,128)(2,1)S(1)}, u32[]{:S(2)}, u32[]{:S(2)}) %collective-permute-start.78) | collective-permute-done | bytes 442400 | tf_op jit(solution)/shard_map/ppermute | solution.py:458
  521.3 9.0 %collective-permute-done.90 = bf16[1,400,256]{2,1,0:T(8,128)(2,1)S(1)} collective-permute-done((bf16[1,400,256]{2,1,0:T(8,128)(2,1)S(1)}, bf16[1,400,256]{2,1,0:T(8,128)(2,1)S(1)}, u32[]{:S(2)}, u32[]{:S(2)}) %collective-permute-start.90) | collective-permute-done | bytes 204832 | tf_op jit(solution)/shard_map/ppermute | solution.py:452
  563.9 7.8 %collective-permute-done.99 = bf16[48,1536]{1,0:T(8,128)(2,1)S(1)} collective-permute-done((bf16[48,1536]{1,0:T(8,128)(2,1)S(1)}, bf16[48,1536]{1,0:T(8,128)(2,1)S(1)}, u32[]{:S(2)}, u32[]{:S(2)}) %collective-permute-start.99) | collective-permute-done | bytes 147488 | tf_op jit(solution)/shard_map/ppermute | solution.py:461
  581.3 6.6 %collective-permute-start.108 = (bf16[48,1536]{1,0:T(8,128)(2,1)S(1)}, bf16[48,1536]{1,0:T(8,128)(2,1)}, u32[]{:S(2)}, u32[]{:S(2)}) collective-permute-start(bf16[48,1536]{1,0:T(8,128)(2,1)S(1)} %get-tuple-element.401), channel_id=1, source_target_pairs={{0,8},{8,16},{16,24},{24,28},{28,20},{20,12},{12,4},{4,0},{1,9},{9... | collective-permute-start | bytes 442376 | tf_op jit(solution)/shard_map/ppermute | solution.py:458
  628.4 5.5 collective-permute-done.126
  (594 shorter events, 366.1 us)
Async XLA Ops:
  18.3 28.5 %collective-permute-start.13 = (bf16[384,1536]{1,0:T(8,128)(2,1)}, bf16[384,1536]{1,0:T(8,128)(2,1)}, u32[]{:S(2)}, u32[]{:S(2)}) collective-permute-start(bf16[384,1536]{1,0:T(8,128)(2,1)} %slice.81), channel_id=1, source_target_pairs={{0,2},{1,3},{2,0},{3,1},{4,6},{5,7},{6,4},{7,5},{8,10},{9,11},{10,... | collective-permute-start | bytes 3538952 | tf_op jit(solution)/shard_map/ppermute | solution.py:452
  20.0 36.3 %collective-permute-start.6 = (bf16[384,1536]{1,0:T(8,128)(2,1)}, bf16[384,1536]{1,0:T(8,128)(2,1)S(1)}, u32[]{:S(2)}, u32[]{:S(2)}) collective-permute-start(bf16[384,1536]{1,0:T(8,128)(2,1)} %slice.81), channel_id=1, source_target_pairs={{0,1},{1,0},{2,3},{3,2},{4,5},{5,4},{6,7},{7,6},{8,9},{9,8},{10,11... | collective-permute-start | bytes 3538952 | tf_op jit(solution)/shard_map/ppermute | solution.py:452
  36.4 50.1 %collective-permute-start.22 = (bf16[512,1536]{1,0:T(8,128)(2,1)S(1)}, bf16[512,1536]{1,0:T(8,128)(2,1)}, u32[]{:S(2)}, u32[]{:S(2)}) collective-permute-start(bf16[512,1536]{1,0:T(8,128)(2,1)S(1)} %bitcast.334), channel_id=1, source_target_pairs={{0,1},{1,0},{2,3},{3,2},{4,5},{5,4},{6,7},{7,6},{8,9},{9,8},{10,11... | collective-permute-start | bytes 4718600 | tf_op jit(solution)/shard_map/ppermute | solution.py:452
  49.0 27.3 %collective-permute-start.18 = (bf16[2,192,1152]{2,1,0:T(8,128)(2,1)}, bf16[2,192,1152]{2,1,0:T(8,128)(2,1)S(1)}, u32[]{:S(2)}, u32[]{:S(2)}) collective-permute-start(bf16[2,192,1152]{2,1,0:T(8,128)(2,1)} %pad_maximum_fusion.1), channel_id=1, source_target_pairs={{0,2},{1,3},{2,0},{3,1},{4,7},{5,6},{6,5},{7,4},{8,10},{9,11},{10,... | collective-permute-start | bytes 2654216 | tf_op jit(solution)/shard_map/ppermute | solution.py:517
  57.5 36.4 %collective-permute-start.21 = (bf16[2,384,1152]{2,1,0:T(8,128)(2,1)S(1)}, bf16[2,384,1152]{2,1,0:T(8,128)(2,1)S(1)}, u32[]{:S(2)}, u32[]{:S(2)}) collective-permute-start(bf16[2,384,1152]{2,1,0:T(8,128)(2,1)S(1)} %pad_maximum_fusion), channel_id=1, source_target_pairs={{0,1},{1,0},{2,3},{3,2},{4,5},{5,4},{6,7},{7,6},{8,9},{9,8},{10,11... | collective-permute-start | bytes 5308424 | tf_op jit(solution)/shard_map/ppermute | solution.py:452
  76.3 31.5 %collective-permute-start.17 = (bf16[384,1536]{1,0:T(8,128)(2,1)}, bf16[384,1536]{1,0:T(8,128)(2,1)}, u32[]{:S(2)}, u32[]{:S(2)}) collective-permute-start(bf16[384,1536]{1,0:T(8,128)(2,1)} %refs_0_), channel_id=1, source_target_pairs={{0,2},{1,3},{2,0},{3,1},{4,6},{5,7},{6,4},{7,5},{8,10},{9,11},{10,... | collective-permute-start | bytes 3538952 | tf_op jit(solution)/shard_map/ppermute | solution.py:452
  134.9 42.2 %collective-permute-start.30 = (bf16[256,1536]{1,0:T(8,128)(2,1)}, bf16[256,1536]{1,0:T(8,128)(2,1)}, u32[]{:S(2)}, u32[]{:S(2)}) collective-permute-start(bf16[256,1536]{1,0:T(8,128)(2,1)} %slice.89), channel_id=1, source_target_pairs={{0,2},{1,3},{2,0},{3,1},{4,6},{5,7},{6,4},{7,5},{8,10},{9,11},{10,... | collective-permute-start | bytes 2359304 | tf_op jit(solution)/shard_map/ppermute | solution.py:452
  135.2 41.9 %collective-permute-start.29 = (bf16[256,1536]{1,0:T(8,128)(2,1)}, bf16[256,1536]{1,0:T(8,128)(2,1)}, u32[]{:S(2)}, u32[]{:S(2)}) collective-permute-start(bf16[256,1536]{1,0:T(8,128)(2,1)} %slice.88), channel_id=1, source_target_pairs={{0,2},{1,3},{2,0},{3,1},{4,6},{5,7},{6,4},{7,5},{8,10},{9,11},{10,... | collective-permute-start | bytes 2359304 | tf_op jit(solution)/shard_map/ppermute | solution.py:452
  177.7 26.5 %collective-permute-start.28 = (bf16[256,1536]{1,0:T(8,128)(2,1)S(1)}, bf16[256,1536]{1,0:T(8,128)(2,1)}, u32[]{:S(2)}, u32[]{:S(2)}) collective-permute-start(bf16[256,1536]{1,0:T(8,128)(2,1)S(1)} %slice.90), channel_id=1, source_target_pairs={{0,2},{1,3},{2,0},{3,1},{4,6},{5,7},{6,4},{7,5},{8,10},{9,11},{10,... | collective-permute-start | bytes 2359304 | tf_op jit(solution)/shard_map/ppermute | solution.py:452
  209.4 36.9 %collective-permute-start.35 = (bf16[512,1536]{1,0:T(8,128)(2,1)}, bf16[512,1536]{1,0:T(8,128)(2,1)S(1)}, u32[]{:S(2)}, u32[]{:S(2)}) collective-permute-start(bf16[512,1536]{1,0:T(8,128)(2,1)} %get-tuple-element.239), channel_id=1, source_target_pairs={{0,1},{1,0},{2,3},{3,2},{4,5},{5,4},{6,7},{7,6},{8,9},{9,8},{10,11... | collective-permute-start | bytes 4718600 | tf_op jit(solution)/shard_map/ppermute | solution.py:452
  261.3 35.1 %collective-permute-start.37 = (bf16[512,1536]{1,0:T(8,128)(2,1)S(1)}, bf16[512,1536]{1,0:T(8,128)(2,1)S(1)}, u32[]{:S(2)}, u32[]{:S(2)}) collective-permute-start(bf16[512,1536]{1,0:T(8,128)(2,1)S(1)} %add_convert_fusion.4), channel_id=1, source_target_pairs={{0,2},{1,3},{2,0},{3,1},{4,6},{5,7},{6,4},{7,5},{8,10},{9,11},{10,... | collective-permute-start | bytes 4718600 | tf_op jit(solution)/shard_map/ppermute | solution.py:452
  319.2 61.3 %collective-permute-start.51 = (bf16[4,48,1152]{2,1,0:T(8,128)(2,1)S(1)}, bf16[4,48,1152]{2,1,0:T(8,128)(2,1)S(1)}, u32[]{:S(2)}, u32[]{:S(2)}) collective-permute-start(bf16[4,48,1152]{2,1,0:T(8,128)(2,1)S(1)} %get-tuple-element.422), channel_id=1, source_target_pairs={{8,0},{16,8},{24,16},{28,24},{20,28},{12,20},{4,12},{0,4},{9,1},{1... | collective-permute-start | bytes 1327112 | tf_op jit(solution)/shard_map/ppermute | solution.py:461
  325.2 55.3 %collective-permute-start.52 = (bf16[4,48,1152]{2,1,0:T(8,128)(2,1)S(1)}, bf16[4,48,1152]{2,1,0:T(8,128)(2,1)S(1)}, u32[]{:S(2)}, u32[]{:S(2)}) collective-permute-start(bf16[4,48,1152]{2,1,0:T(8,128)(2,1)S(1)} %get-tuple-element.421), channel_id=1, source_target_pairs={{0,8},{8,16},{16,24},{24,28},{28,20},{20,12},{12,4},{4,0},{1,9},{9... | collective-permute-start | bytes 1327112 | tf_op jit(solution)/shard_map/ppermute | solution.py:458
  328.5 36.0 %collective-permute-start.59 = (bf16[144,1536]{1,0:T(8,128)(2,1)S(1)}, bf16[144,1536]{1,0:T(8,128)(2,1)S(1)}, u32[]{:S(2)}, u32[]{:S(2)}) collective-permute-start(bf16[144,1536]{1,0:T(8,128)(2,1)S(1)} %fusion.29), channel_id=1, source_target_pairs={{0,8},{8,16},{16,24},{24,28},{28,20},{20,12},{12,4},{4,0},{1,9},{9... | collective-permute-start | bytes 1327112 | tf_op jit(solution)/shard_map/ppermute | solution.py:458
  338.2 40.2 %collective-permute-start.57 = (bf16[4,48,1152]{2,1,0:T(8,128)(2,1)S(1)}, bf16[4,48,1152]{2,1,0:T(8,128)(2,1)S(1)}, u32[]{:S(2)}, u32[]{:S(2)}) collective-permute-start(bf16[4,48,1152]{2,1,0:T(8,128)(2,1)S(1)} %get-tuple-element.420), channel_id=1, source_target_pairs={{0,8},{8,16},{16,24},{24,28},{28,20},{20,12},{12,4},{4,0},{1,9},{9... | collective-permute-start | bytes 1327112 | tf_op jit(solution)/shard_map/ppermute | solution.py:458
  340.0 38.4 %collective-permute-start.58 = (bf16[4,48,1152]{2,1,0:T(8,128)(2,1)S(1)}, bf16[4,48,1152]{2,1,0:T(8,128)(2,1)S(1)}, u32[]{:S(2)}, u32[]{:S(2)}) collective-permute-start(bf16[4,48,1152]{2,1,0:T(8,128)(2,1)S(1)} %get-tuple-element.419), channel_id=1, source_target_pairs={{8,0},{16,8},{24,16},{28,24},{20,28},{12,20},{4,12},{0,4},{9,1},{1... | collective-permute-start | bytes 1327112 | tf_op jit(solution)/shard_map/ppermute | solution.py:461
  364.5 37.0 %collective-permute-start.50 = (bf16[512,1536]{1,0:T(8,128)(2,1)}, bf16[512,1536]{1,0:T(8,128)(2,1)}, u32[]{:S(2)}, u32[]{:S(2)}) collective-permute-start(bf16[512,1536]{1,0:T(8,128)(2,1)} %add_convert_fusion.1), channel_id=1, source_target_pairs={{0,2},{1,3},{2,0},{3,1},{4,6},{5,7},{6,4},{7,5},{8,10},{9,11},{10,... | collective-permute-start | bytes 4718600 | tf_op jit(solution)/shard_map/ppermute | solution.py:452
  430.9 28.4 %collective-permute-start.80 = (bf16[48,1152]{1,0:T(8,128)(2,1)S(1)}, bf16[48,1152]{1,0:T(8,128)(2,1)S(1)}, u32[]{:S(2)}, u32[]{:S(2)}) collective-permute-start(bf16[48,1152]{1,0:T(8,128)(2,1)S(1)} %get-tuple-element.464), channel_id=1, source_target_pairs={{0,1},{1,0},{2,3},{3,2},{4,5},{5,4},{6,7},{7,6},{8,9},{9,8},{10,11... | collective-permute-start | bytes 331784 | tf_op jit(solution)/shard_map/ppermute | solution.py:452
  446.9 27.6 %collective-permute-start.75 = (bf16[48,1152]{1,0:T(8,128)(2,1)S(1)}, bf16[48,1152]{1,0:T(8,128)(2,1)S(1)}, u32[]{:S(2)}, u32[]{:S(2)}) collective-permute-start(bf16[48,1152]{1,0:T(8,128)(2,1)S(1)} %get-tuple-element.461), channel_id=1, source_target_pairs={{0,1},{1,0},{2,3},{3,2},{4,5},{5,4},{6,7},{7,6},{8,9},{9,8},{10,11... | collective-permute-start | bytes 331784 | tf_op jit(solution)/shard_map/ppermute | solution.py:452
  472.3 37.1 %collective-permute-start.83 = (bf16[1,384,1536]{2,1,0:T(8,128)(2,1)}, bf16[1,384,1536]{2,1,0:T(8,128)(2,1)}, u32[]{:S(2)}, u32[]{:S(2)}) collective-permute-start(bf16[1,384,1536]{2,1,0:T(8,128)(2,1)} %constant_dynamic-slice_fusion.1), channel_id=1, source_target_pairs={{0,2},{1,3},{2,0},{3,1},{4,6},{5,7},{6,4},{7,5},{8,10},{9,11},{10,... | collective-permute-start | bytes 3538952 | tf_op jit(solution)/shard_map/ppermute | solution.py:452
  473.5 64.2 %collective-permute-start.97 = (bf16[1,384,1536]{2,1,0:T(8,128)(2,1)}, bf16[1,384,1536]{2,1,0:T(8,128)(2,1)}, u32[]{:S(2)}, u32[]{:S(2)}) collective-permute-start(bf16[1,384,1536]{2,1,0:T(8,128)(2,1)} %constant_dynamic-slice_fusion.2), channel_id=1, source_target_pairs={{0,2},{1,3},{2,0},{3,1},{4,6},{5,7},{6,4},{7,5},{8,10},{9,11},{10,... | collective-permute-start | bytes 3538952 | tf_op jit(solution)/shard_map/ppermute | solution.py:452
  496.8 42.8 %collective-permute-start.95 = (bf16[48,4608]{1,0:T(8,128)(2,1)S(1)}, bf16[48,4608]{1,0:T(8,128)(2,1)}, u32[]{:S(2)}, u32[]{:S(2)}) collective-permute-start(bf16[48,4608]{1,0:T(8,128)(2,1)S(1)} %copy-done.40), channel_id=1, source_target_pairs={{8,0},{16,8},{24,16},{28,24},{20,28},{12,20},{4,12},{0,4},{9,1},{1... | collective-permute-start | bytes 1327112 | tf_op jit(solution)/shard_map/ppermute | solution.py:461
  550.1 67.4 %collective-permute-start.123 = (bf16[48,4608]{1,0:T(8,128)(2,1)}, bf16[48,4608]{1,0:T(8,128)(2,1)}, u32[]{:S(2)}, u32[]{:S(2)}) collective-permute-start(bf16[48,4608]{1,0:T(8,128)(2,1)} %collective-permute-done.95), channel_id=1, source_target_pairs={{8,0},{16,8},{24,16},{28,24},{20,28},{12,20},{4,12},{0,4},{9,1},{1... | collective-permute-start | bytes 1327112 | tf_op jit(solution)/shard_map/ppermute | solution.py:461
  560.6 27.4 %collective-permute-start.111 = (bf16[48,1536]{1,0:T(8,128)(2,1)S(1)}, bf16[48,1536]{1,0:T(8,128)(2,1)S(1)}, u32[]{:S(2)}, u32[]{:S(2)}) collective-permute-start(bf16[48,1536]{1,0:T(8,128)(2,1)S(1)} %get-tuple-element.446), channel_id=1, source_target_pairs={{8,0},{16,8},{24,16},{28,24},{20,28},{12,20},{4,12},{0,4},{9,1},{1... | collective-permute-start | bytes 442376 | tf_op jit(solution)/shard_map/ppermute | solution.py:461
  (188 other events, 2463.4 us)

commit v5 on v4

--- a/solution.py
+++ b/solution.py
@@ -788,12 +788,12 @@
     chain(plan.scatter(order.after(*down)), "B")
     d_mixed = dot_f32(order.after(d_branch), w_o, ((1,), (1,))).astype(low).reshape(seqs, rows_dev, QW)
     order.did(d_mixed)
-    take("GBDU")
+    take("GB")
     dq, dkv = attend_back(scalars, queries, order.after(d_mixed), mixed, kv_all, seg, lse)
     order.did(dq, dkv)
     chain(plan.ring_scatter(dkv), "K")
     dq = dq.reshape(rows, QW)
-    take("DUG")
+    take("DUGDU")
     chain(plan.sum_over_all(grad(mixed_low, d_branch), blank_like(w_out), -1), "O")
     out_qkv = blank_like(w_qkv)
     chain(plan.sum_over_all(grad(normed_one, dq), out_qkv, 1), "Q")

time: 649 us -> 647 us (level); the launches traced: 649 us -> 640 us
  starting transfers between devices: 153 us -> 132 us
  waiting for transfers between devices: 161 us -> 174 us
    ppermute x44, starting transfers between devices: 73.6 us -> 30 us  [go_right(): return lax.ppermute(v, 'ctx', self.right)]
    ppermute x40, starting transfers between devices: 32.3 us -> 60.7 us  [go_left(): return lax.ppermute(v, 'ctx', self.left)]
    ppermute x44, waiting for transfers between devices: 62.6 us -> 86.3 us  [go_right(): return lax.ppermute(v, 'ctx', self.right)]
    ppermute x40, waiting for transfers between devices: 43.5 us -> 34.4 us  [go_left(): return lax.ppermute(v, 'ctx', self.left)]
    ppermute x41, waiting for transfers between devices: 38.7 us -> 31.2 us  [swap(): return lax.ppermute(v, 'shard', [(i, i ^ bit) for i in range(self.shards)])]
  transfers between devices with their start and end apart: 133 -> 133, of which waited for: 50 -> 45; matrix products, arithmetic and copies ran while one was open for 27% -> 28% of each run, Pallas kernels for 20% -> 20%
where the time goes in v5:
time: 647 us; the launch traced here: 640 us
  waiting for transfers between devices  174 us (27%)
  starting transfers between devices  132 us (20%)
  Pallas kernels  129 us (20%)
  other arithmetic  101 us (16%)
  matrix products  50 us (8%)
  local copies, waits for them, and re-layouts  41 us (6%)
  between operations  12.4 us (2%)
    ppermute x44, waiting for transfers between devices, go_right(): return lax.ppermute(v, 'ctx', self.right)  86.3 us
    pallas_call x3, Pallas kernels, ffn(): pl.pallas_call(functools.partial(ffn_kernel, counts, index), grid_spec=pl...  83.6 us
    ppermute x40, starting transfers between devices, go_left(): return lax.ppermute(v, 'ctx', self.left)  60.7 us
    dot_general x10, matrix products, dot_f32(): lax.dot_general(left, right, (dims, ((), ())), preferred_element_type=jnp...  50 us
    dynamic_update_slice x40, other arithmetic, put(): lax.dynamic_update_slice(out[0], piece.astype(jnp.float32), (at, col))  45 us
    ppermute x40, waiting for transfers between devices, go_left(): return lax.ppermute(v, 'ctx', self.left)  34.4 us
    ppermute x41, starting transfers between devices, swap(): return lax.ppermute(v, 'shard', [(i, i ^ bit) for i in range(self.shards)])  33.5 us
    ppermute x41, waiting for transfers between devices, swap(): return lax.ppermute(v, 'shard', [(i, i ^ bit) for i in range(self.shards)])  31.2 us
  transfers between devices with their start and end apart: 133, of which 45 were waited for; matrix products, arithmetic and copies ran while one was open for 28% of the time, Pallas kernels for 20%

profile of v5, /device:TPU:0, one launch (start us, length us, event | category | flops | bytes accessed | tf_op | source)
XLA Modules:
  0.0 639.9 jit_solution(15063416620236775168)
XLA Ops:
  36.4 5.5 collective-permute-done.10
  62.9 13.3 %attend.1 = (bf16[2,256,1536]{2,1,0:T(8,128)(2,1)S(1)}, f32[2,2,1,1536]{3,2,1,0:T(1,128)S(1)}) custom-call(s32[2]{0:T(128)S(1)} %get-tuple-element.412.blk_ref, s32[4]{0:T(128)S(1)} %maximum_maximum_fusion.low_ref, s32[16]{0:T(128)S(1)} %get-tuple-element.395.slot_ref, s32[16]{0:T(128)S(1)} %get-tuple-element.394.half_ref, ...), custom_call_target="tpu_custom_call" | custom-call | flops 1048576 | bytes 65536 | tf_op jit(solution)/shard_map/attend/pallas_call | solution.py:160
  80.3 10.1 %collective-permute-done.19.refs_3_ = bf16[192,1152]{1,0:T(8,128)(2,1)S(1)} collective-permute-done((bf16[192,1152]{1,0:T(8,128)(2,1)S(1)}, bf16[192,1152]{1,0:T(8,128)(2,1)S(1)}, u32[]{:S(2)}, u32[]{:S(2)}) %collective-permute-start.19) | collective-permute-done | bytes 442400 | tf_op jit(solution)/shard_map/ppermute | solution.py:455
  93.5 10.0 %collective-permute-done.17.refs_2_ = bf16[384,1536]{1,0:T(8,128)(2,1)} collective-permute-done((bf16[384,1536]{1,0:T(8,128)(2,1)}, bf16[384,1536]{1,0:T(8,128)(2,1)}, u32[]{:S(2)}, u32[]{:S(2)}) %collective-permute-start.17) | collective-permute-done | bytes 1179680 | tf_op jit(solution)/shard_map/ppermute | solution.py:452
  108.2 8.2 %project.3 = (f32[512,1536]{1,0:T(8,128)}, bf16[1536,1536]{1,0:T(8,128)(2,1)}) custom-call(s32[4]{0:T(128)S(1)} %iota_xor_fusion.at_ref, bf16[512,1536]{1,0:T(8,128)(2,1)} %bitcast.325, bf16[384,1536]{1,0:T(8,128)(2,1)} %refs_0_, bf16[384,1536]{1,0:T(8,128)(2,1)} %collective-permute-done.16.refs_1_, bf16[384,1536]{1,0:T(8,128)(2,1)} %collective-permute-done.17.refs_2_, ...), custom_call_target="tpu_custom_call" | custom-call | flops 1048576 | bytes 65536 | tf_op jit(solution)/shard_map/project/pallas_call | solution.py:356
  118.7 8.5 %collective-permute-done.26.refs_10_.refs_11_ = bf16[2,192,1152]{2,1,0:T(8,128)(2,1)} collective-permute-done((bf16[2,192,1152]{2,1,0:T(8,128)(2,1)}, bf16[2,192,1152]{2,1,0:T(8,128)(2,1)}, u32[]{:S(2)}, u32[]{:S(2)}) %collective-permute-start.26) | collective-permute-done | bytes 884768 | tf_op jit(solution)/shard_map/ppermute | solution.py:455
  135.7 38.3 %ffn.3 = (bf16[4,512,1152]{2,1,0:T(8,128)(2,1)}, bf16[4,512,1152]{2,1,0:T(8,128)(2,1)}, bf16[4,512,1152]{2,1,0:T(8,128)(2,1)}, bf16[4,512,1536]{2,1,0:T(8,128)(2...) custom-call(s32[17]{0:T(128)} %concatenate.13.at_ref, ...), custom_call_target="tpu_custom_call" | custom-call | flops 1048576 | bytes 65536 | tf_op jit(solution)/shard_map/ffn/pallas_call | solution.py:313
  178.7 22.5 %ffn.4 = (bf16[4,512,1152]{2,1,0:T(8,128)(2,1)}, bf16[4,512,1152]{2,1,0:T(8,128)(2,1)}, bf16[4,512,1152]{2,1,0:T(8,128)(2,1)}, bf16[4,512,1536]{2,1,0:T(8,128)(2...) custom-call(s32[17]{0:T(128)} %concatenate.13.at_ref, ...), custom_call_target="tpu_custom_call", output_to_operand_aliasing={{0}: (18, {}), {1}: (19, {}), {2}: (20, {}), {3}: (21, {}),... | custom-call | flops 1048576 | bytes 65536 | tf_op jit(solution)/shard_map/ffn/pallas_call | solution.py:313
  206.6 22.7 %ffn.5 = (bf16[4,512,1152]{2,1,0:T(8,128)(2,1)}, bf16[4,512,1152]{2,1,0:T(8,128)(2,1)}, bf16[4,512,1152]{2,1,0:T(8,128)(2,1)}, bf16[4,512,1536]{2,1,0:T(8,128)(2...) custom-call(s32[17]{0:T(128)} %concatenate.13.at_ref, ...), custom_call_target="tpu_custom_call", output_to_operand_aliasing={{0}: (18, {}), {1}: (19, {}), {2}: (20, {}), {3}: (21, {}),... | custom-call | flops 1048576 | bytes 65536 | tf_op jit(solution)/shard_map/ffn/pallas_call | solution.py:313
  229.8 11.3 %convolution_convert_fusion.4 = bf16[1152,1536]{1,0:T(8,128)(2,1)S(1)} fusion(bf16[2048,1152]{1,0:T(8,128)(2,1)} %bitcast.342, bf16[2048,1536]{1,0:T(8,128)(2,1)} %bitcast.341), kind=kOutput, calls=%fused_computation.4 | convolution fusion | flops 7249526784 | bytes 14548992 | tf_op jit(solution)/shard_map/dot_general | solution.py:27
  243.8 9.3 %convolution_convert_fusion.3 = bf16[1536,1152]{1,0:T(8,128)(2,1)S(1)} fusion(bf16[2048,1536]{1,0:T(8,128)(2,1)S(1)} %bitcast.339, bf16[2048,1152]{1,0:T(8,128)(2,1)S(1)} %bitcast.345), kind=kOutput, calls=%fused_computation.3 | convolution fusion | flops 7249526784 | bytes 14548992 | tf_op jit(solution)/shard_map/dot_general | solution.py:27
  259.2 8.8 %convolution_convert_fusion.2 = bf16[1536,1152]{1,0:T(8,128)(2,1)S(1)} fusion(bf16[2048,1536]{1,0:T(8,128)(2,1)S(1)} %bitcast.340, bf16[2048,1152]{1,0:T(8,128)(2,1)S(1)} %bitcast.348), kind=kOutput, calls=%fused_computation.2 | convolution fusion | flops 7249526784 | bytes 14548992 | tf_op jit(solution)/shard_map/dot_general | solution.py:27
  271.6 5.9 collective-permute-done.42
  278.6 6.6 %collective-permute-done.40 = bf16[4,48,1152]{2,1,0:T(8,128)(2,1)S(1)} collective-permute-done((bf16[4,48,1152]{2,1,0:T(8,128)(2,1)S(1)}, bf16[4,48,1152]{2,1,0:T(8,128)(2,1)S(1)}, u32[]{:S(2)}, u32[]{:S(2)}) %collective-permute-start.40) | collective-permute-done | bytes 442400 | tf_op jit(solution)/shard_map/ppermute | solution.py:458
  286.3 6.0 collective-permute-done.37
  319.8 21.7 %attend_back.1 = (bf16[2,256,1536]{2,1,0:T(8,128)(2,1)S(1)}, bf16[8,2,2,128,256]{4,3,2,1,0:T(8,128)(2,1)}) custom-call(s32[2]{0:T(128)S(1)} %get-tuple-element.412.blk_ref, s32[4]{0:T(128)S(1)} %maximum_maximum_fusion.low_ref, s32[16]{0:T(128)S(1)} %get-tuple-element.395.slot_ref, s32[16]{0:T(128)S(1)} %get-tuple-element.394.half_ref, ...), custom_call_target="tpu_custom_call" | custom-call | flops 17999998976 | bytes 12582912 | tf_op jit(solution)/shard_map/attend_back/pallas_call | solution.py:187
  358.1 7.4 %collective-permute-done.57 = bf16[144,1536]{1,0:T(8,128)(2,1)S(1)} collective-permute-done((bf16[144,1536]{1,0:T(8,128)(2,1)S(1)}, bf16[144,1536]{1,0:T(8,128)(2,1)S(1)}, u32[]{:S(2)}, u32[]{:S(2)}) %collective-permute-start.57) | collective-permute-done | bytes 442400 | tf_op jit(solution)/shard_map/ppermute | solution.py:458
  367.8 7.2 %collective-permute-done.55 = bf16[4,48,1152]{2,1,0:T(8,128)(2,1)S(1)} collective-permute-done((bf16[4,48,1152]{2,1,0:T(8,128)(2,1)S(1)}, bf16[4,48,1152]{2,1,0:T(8,128)(2,1)S(1)}, u32[]{:S(2)}, u32[]{:S(2)}) %collective-permute-start.55) | collective-permute-done | bytes 442400 | tf_op jit(solution)/shard_map/ppermute | solution.py:458
  413.3 6.0 collective-permute-done.67
  443.2 7.0 %collective-permute-done.74 = bf16[2,2,128,256]{3,2,1,0:T(8,128)(2,1)S(1)} collective-permute-done((bf16[2,2,128,256]{3,2,1,0:T(8,128)(2,1)S(1)}, bf16[2,2,128,256]{3,2,1,0:T(8,128)(2,1)S(1)}, u32[]{:S(2)}, u32[]{:S(2)}) %collective-permute-start.74) | collective-permute-done | bytes 262176 | tf_op jit(solution)/shard_map/ppermute | solution.py:458
  460.4 6.0 collective-permute-done.78
  495.2 6.4 %collective-permute-done.84 = bf16[144,1536]{1,0:T(8,128)(2,1)S(1)} collective-permute-done((bf16[144,1536]{1,0:T(8,128)(2,1)S(1)}, bf16[144,1536]{1,0:T(8,128)(2,1)S(1)}, u32[]{:S(2)}, u32[]{:S(2)}) %collective-permute-start.84) | collective-permute-done | bytes 442400 | tf_op jit(solution)/shard_map/ppermute | solution.py:458
  513.6 10.3 %collective-permute-done.90 = bf16[1,400,256]{2,1,0:T(8,128)(2,1)S(1)} collective-permute-done((bf16[1,400,256]{2,1,0:T(8,128)(2,1)S(1)}, bf16[1,400,256]{2,1,0:T(8,128)(2,1)S(1)}, u32[]{:S(2)}, u32[]{:S(2)}) %collective-permute-start.90) | collective-permute-done | bytes 204832 | tf_op jit(solution)/shard_map/ppermute | solution.py:452
  557.2 6.4 collective-permute-done.99
  (594 shorter events, 362.1 us)
Async XLA Ops:
  18.3 28.5 %collective-permute-start.13 = (bf16[384,1536]{1,0:T(8,128)(2,1)}, bf16[384,1536]{1,0:T(8,128)(2,1)}, u32[]{:S(2)}, u32[]{:S(2)}) collective-permute-start(bf16[384,1536]{1,0:T(8,128)(2,1)} %slice.81), channel_id=1, source_target_pairs={{0,2},{1,3},{2,0},{3,1},{4,6},{5,7},{6,4},{7,5},{8,10},{9,11},{10,... | collective-permute-start | bytes 3538952 | tf_op jit(solution)/shard_map/ppermute | solution.py:452
  20.0 36.2 %collective-permute-start.6 = (bf16[384,1536]{1,0:T(8,128)(2,1)}, bf16[384,1536]{1,0:T(8,128)(2,1)S(1)}, u32[]{:S(2)}, u32[]{:S(2)}) collective-permute-start(bf16[384,1536]{1,0:T(8,128)(2,1)} %slice.81), channel_id=1, source_target_pairs={{0,1},{1,0},{2,3},{3,2},{4,5},{5,4},{6,7},{7,6},{8,9},{9,8},{10,11... | collective-permute-start | bytes 3538952 | tf_op jit(solution)/shard_map/ppermute | solution.py:452
  36.4 41.9 %collective-permute-start.22 = (bf16[512,1536]{1,0:T(8,128)(2,1)S(1)}, bf16[512,1536]{1,0:T(8,128)(2,1)}, u32[]{:S(2)}, u32[]{:S(2)}) collective-permute-start(bf16[512,1536]{1,0:T(8,128)(2,1)S(1)} %bitcast.334), channel_id=1, source_target_pairs={{0,1},{1,0},{2,3},{3,2},{4,5},{5,4},{6,7},{7,6},{8,9},{9,8},{10,11... | collective-permute-start | bytes 4718600 | tf_op jit(solution)/shard_map/ppermute | solution.py:452
  49.0 27.3 %collective-permute-start.18 = (bf16[2,192,1152]{2,1,0:T(8,128)(2,1)}, bf16[2,192,1152]{2,1,0:T(8,128)(2,1)S(1)}, u32[]{:S(2)}, u32[]{:S(2)}) collective-permute-start(bf16[2,192,1152]{2,1,0:T(8,128)(2,1)} %pad_maximum_fusion.1), channel_id=1, source_target_pairs={{0,2},{1,3},{2,0},{3,1},{4,7},{5,6},{6,5},{7,4},{8,10},{9,11},{10,... | collective-permute-start | bytes 2654216 | tf_op jit(solution)/shard_map/ppermute | solution.py:517
  57.4 33.0 %collective-permute-start.21 = (bf16[2,384,1152]{2,1,0:T(8,128)(2,1)S(1)}, bf16[2,384,1152]{2,1,0:T(8,128)(2,1)S(1)}, u32[]{:S(2)}, u32[]{:S(2)}) collective-permute-start(bf16[2,384,1152]{2,1,0:T(8,128)(2,1)S(1)} %pad_maximum_fusion), channel_id=1, source_target_pairs={{0,1},{1,0},{2,3},{3,2},{4,5},{5,4},{6,7},{7,6},{8,9},{9,8},{10,11... | collective-permute-start | bytes 5308424 | tf_op jit(solution)/shard_map/ppermute | solution.py:452
  76.3 27.2 %collective-permute-start.17 = (bf16[384,1536]{1,0:T(8,128)(2,1)}, bf16[384,1536]{1,0:T(8,128)(2,1)}, u32[]{:S(2)}, u32[]{:S(2)}) collective-permute-start(bf16[384,1536]{1,0:T(8,128)(2,1)} %refs_0_), channel_id=1, source_target_pairs={{0,2},{1,3},{2,0},{3,1},{4,6},{5,7},{6,4},{7,5},{8,10},{9,11},{10,... | collective-permute-start | bytes 3538952 | tf_op jit(solution)/shard_map/ppermute | solution.py:452
  78.3 28.8 %collective-permute-start.16 = (bf16[384,1536]{1,0:T(8,128)(2,1)}, bf16[384,1536]{1,0:T(8,128)(2,1)}, u32[]{:S(2)}, u32[]{:S(2)}) collective-permute-start(bf16[384,1536]{1,0:T(8,128)(2,1)} %refs_0_), channel_id=1, source_target_pairs={{0,1},{1,0},{2,3},{3,2},{4,5},{5,4},{6,7},{7,6},{8,9},{9,8},{10,11... | collective-permute-start | bytes 3538952 | tf_op jit(solution)/shard_map/ppermute | solution.py:452
  131.9 42.2 %collective-permute-start.30 = (bf16[256,1536]{1,0:T(8,128)(2,1)}, bf16[256,1536]{1,0:T(8,128)(2,1)}, u32[]{:S(2)}, u32[]{:S(2)}) collective-permute-start(bf16[256,1536]{1,0:T(8,128)(2,1)} %slice.89), channel_id=1, source_target_pairs={{0,2},{1,3},{2,0},{3,1},{4,6},{5,7},{6,4},{7,5},{8,10},{9,11},{10,... | collective-permute-start | bytes 2359304 | tf_op jit(solution)/shard_map/ppermute | solution.py:452
  133.6 40.5 %collective-permute-start.29 = (bf16[256,1536]{1,0:T(8,128)(2,1)}, bf16[256,1536]{1,0:T(8,128)(2,1)}, u32[]{:S(2)}, u32[]{:S(2)}) collective-permute-start(bf16[256,1536]{1,0:T(8,128)(2,1)} %slice.88), channel_id=1, source_target_pairs={{0,2},{1,3},{2,0},{3,1},{4,6},{5,7},{6,4},{7,5},{8,10},{9,11},{10,... | collective-permute-start | bytes 2359304 | tf_op jit(solution)/shard_map/ppermute | solution.py:452
  206.4 36.9 %collective-permute-start.35 = (bf16[512,1536]{1,0:T(8,128)(2,1)}, bf16[512,1536]{1,0:T(8,128)(2,1)S(1)}, u32[]{:S(2)}, u32[]{:S(2)}) collective-permute-start(bf16[512,1536]{1,0:T(8,128)(2,1)} %get-tuple-element.239), channel_id=1, source_target_pairs={{0,1},{1,0},{2,3},{3,2},{4,5},{5,4},{6,7},{7,6},{8,9},{9,8},{10,11... | collective-permute-start | bytes 4718600 | tf_op jit(solution)/shard_map/ppermute | solution.py:452
  257.5 34.8 %collective-permute-start.37 = (bf16[512,1536]{1,0:T(8,128)(2,1)S(1)}, bf16[512,1536]{1,0:T(8,128)(2,1)S(1)}, u32[]{:S(2)}, u32[]{:S(2)}) collective-permute-start(bf16[512,1536]{1,0:T(8,128)(2,1)S(1)} %add_convert_fusion.4), channel_id=1, source_target_pairs={{0,2},{1,3},{2,0},{3,1},{4,6},{5,7},{6,4},{7,5},{8,10},{9,11},{10,... | collective-permute-start | bytes 4718600 | tf_op jit(solution)/shard_map/ppermute | solution.py:452
  299.9 43.8 %collective-permute-start.53 = (bf16[144,1536]{1,0:T(8,128)(2,1)}, bf16[144,1536]{1,0:T(8,128)(2,1)S(1)}, u32[]{:S(2)}, u32[]{:S(2)}) collective-permute-start(bf16[144,1536]{1,0:T(8,128)(2,1)} %get-tuple-element.426), channel_id=1, source_target_pairs={{0,8},{8,16},{16,24},{24,28},{28,20},{20,12},{12,4},{4,0},{1,9},{9... | collective-permute-start | bytes 1327112 | tf_op jit(solution)/shard_map/ppermute | solution.py:458
  310.1 33.5 %collective-permute-start.54 = (bf16[144,1536]{1,0:T(8,128)(2,1)S(1)}, bf16[144,1536]{1,0:T(8,128)(2,1)S(1)}, u32[]{:S(2)}, u32[]{:S(2)}) collective-permute-start(bf16[144,1536]{1,0:T(8,128)(2,1)S(1)} %copy-done.53), channel_id=1, source_target_pairs={{8,0},{16,8},{24,16},{28,24},{20,28},{12,20},{4,12},{0,4},{9,1},{1... | collective-permute-start | bytes 1327112 | tf_op jit(solution)/shard_map/ppermute | solution.py:461
  312.8 35.2 %collective-permute-start.51 = (bf16[4,48,1152]{2,1,0:T(8,128)(2,1)S(1)}, bf16[4,48,1152]{2,1,0:T(8,128)(2,1)S(1)}, u32[]{:S(2)}, u32[]{:S(2)}) collective-permute-start(bf16[4,48,1152]{2,1,0:T(8,128)(2,1)S(1)} %copy-done.54), channel_id=1, source_target_pairs={{0,8},{8,16},{16,24},{24,28},{28,20},{20,12},{12,4},{4,0},{1,9},{9... | collective-permute-start | bytes 1327112 | tf_op jit(solution)/shard_map/ppermute | solution.py:458
  314.5 34.0 %collective-permute-start.52 = (bf16[4,48,1152]{2,1,0:T(8,128)(2,1)S(1)}, bf16[4,48,1152]{2,1,0:T(8,128)(2,1)S(1)}, u32[]{:S(2)}, u32[]{:S(2)}) collective-permute-start(bf16[4,48,1152]{2,1,0:T(8,128)(2,1)S(1)} %copy-done.52), channel_id=1, source_target_pairs={{8,0},{16,8},{24,16},{28,24},{20,28},{12,20},{4,12},{0,4},{9,1},{1... | collective-permute-start | bytes 1327112 | tf_op jit(solution)/shard_map/ppermute | solution.py:461
  316.2 33.8 %collective-permute-start.58 = (bf16[4,48,1152]{2,1,0:T(8,128)(2,1)S(1)}, bf16[4,48,1152]{2,1,0:T(8,128)(2,1)S(1)}, u32[]{:S(2)}, u32[]{:S(2)}) collective-permute-start(bf16[4,48,1152]{2,1,0:T(8,128)(2,1)S(1)} %get-tuple-element.422), channel_id=1, source_target_pairs={{8,0},{16,8},{24,16},{28,24},{20,28},{12,20},{4,12},{0,4},{9,1},{1... | collective-permute-start | bytes 1327112 | tf_op jit(solution)/shard_map/ppermute | solution.py:461
  343.6 49.4 %collective-permute-start.50 = (bf16[512,1536]{1,0:T(8,128)(2,1)}, bf16[512,1536]{1,0:T(8,128)(2,1)}, u32[]{:S(2)}, u32[]{:S(2)}) collective-permute-start(bf16[512,1536]{1,0:T(8,128)(2,1)} %add_convert_fusion.1), channel_id=1, source_target_pairs={{0,2},{1,3},{2,0},{3,1},{4,6},{5,7},{6,4},{7,5},{8,10},{9,11},{10,... | collective-permute-start | bytes 4718600 | tf_op jit(solution)/shard_map/ppermute | solution.py:452
  422.1 32.1 %collective-permute-start.80 = (bf16[48,1152]{1,0:T(8,128)(2,1)S(1)}, bf16[48,1152]{1,0:T(8,128)(2,1)S(1)}, u32[]{:S(2)}, u32[]{:S(2)}) collective-permute-start(bf16[48,1152]{1,0:T(8,128)(2,1)S(1)} %get-tuple-element.464), channel_id=1, source_target_pairs={{0,1},{1,0},{2,3},{3,2},{4,5},{5,4},{6,7},{7,6},{8,9},{9,8},{10,11... | collective-permute-start | bytes 331784 | tf_op jit(solution)/shard_map/ppermute | solution.py:452
  426.0 28.2 %collective-permute-start.81 = (bf16[48,1152]{1,0:T(8,128)(2,1)S(1)}, bf16[48,1152]{1,0:T(8,128)(2,1)S(1)}, u32[]{:S(2)}, u32[]{:S(2)}) collective-permute-start(bf16[48,1152]{1,0:T(8,128)(2,1)S(1)} %get-tuple-element.463), channel_id=1, source_target_pairs={{0,2},{1,3},{2,0},{3,1},{4,6},{5,7},{6,4},{7,5},{8,10},{9,11},{10,... | collective-permute-start | bytes 331784 | tf_op jit(solution)/shard_map/ppermute | solution.py:452
  441.3 27.2 %collective-permute-start.75 = (bf16[48,1152]{1,0:T(8,128)(2,1)S(1)}, bf16[48,1152]{1,0:T(8,128)(2,1)S(1)}, u32[]{:S(2)}, u32[]{:S(2)}) collective-permute-start(bf16[48,1152]{1,0:T(8,128)(2,1)S(1)} %get-tuple-element.461), channel_id=1, source_target_pairs={{0,1},{1,0},{2,3},{3,2},{4,5},{5,4},{6,7},{7,6},{8,9},{9,8},{10,11... | collective-permute-start | bytes 331784 | tf_op jit(solution)/shard_map/ppermute | solution.py:452
  466.4 37.7 %collective-permute-start.83 = (bf16[1,384,1536]{2,1,0:T(8,128)(2,1)}, bf16[1,384,1536]{2,1,0:T(8,128)(2,1)}, u32[]{:S(2)}, u32[]{:S(2)}) collective-permute-start(bf16[1,384,1536]{2,1,0:T(8,128)(2,1)} %constant_dynamic-slice_fusion.1), channel_id=1, source_target_pairs={{0,2},{1,3},{2,0},{3,1},{4,6},{5,7},{6,4},{7,5},{8,10},{9,11},{10,... | collective-permute-start | bytes 3538952 | tf_op jit(solution)/shard_map/ppermute | solution.py:452
  467.7 61.5 %collective-permute-start.97 = (bf16[1,384,1536]{2,1,0:T(8,128)(2,1)}, bf16[1,384,1536]{2,1,0:T(8,128)(2,1)}, u32[]{:S(2)}, u32[]{:S(2)}) collective-permute-start(bf16[1,384,1536]{2,1,0:T(8,128)(2,1)} %constant_dynamic-slice_fusion.2), channel_id=1, source_target_pairs={{0,2},{1,3},{2,0},{3,1},{4,6},{5,7},{6,4},{7,5},{8,10},{9,11},{10,... | collective-permute-start | bytes 3538952 | tf_op jit(solution)/shard_map/ppermute | solution.py:452
  489.1 43.7 %collective-permute-start.95 = (bf16[48,4608]{1,0:T(8,128)(2,1)S(1)}, bf16[48,4608]{1,0:T(8,128)(2,1)}, u32[]{:S(2)}, u32[]{:S(2)}) collective-permute-start(bf16[48,4608]{1,0:T(8,128)(2,1)S(1)} %copy-done.40), channel_id=1, source_target_pairs={{8,0},{16,8},{24,16},{28,24},{20,28},{12,20},{4,12},{0,4},{9,1},{1... | collective-permute-start | bytes 1327112 | tf_op jit(solution)/shard_map/ppermute | solution.py:461
  544.1 62.4 %collective-permute-start.123 = (bf16[48,4608]{1,0:T(8,128)(2,1)}, bf16[48,4608]{1,0:T(8,128)(2,1)}, u32[]{:S(2)}, u32[]{:S(2)}) collective-permute-start(bf16[48,4608]{1,0:T(8,128)(2,1)} %collective-permute-done.95), channel_id=1, source_target_pairs={{8,0},{16,8},{24,16},{28,24},{20,28},{12,20},{4,12},{0,4},{9,1},{1... | collective-permute-start | bytes 1327112 | tf_op jit(solution)/shard_map/ppermute | solution.py:461
  (188 other events, 2486.6 us)
